TPU v7x, 32 devices: a whole 2x2x4 slice. The times are simulated.
32 devices in a mesh: dp: 4 (over y, x), vocab: 8 (over z, core).
Axes of the slice: x: 2, y: 2, z: 4, core: 2. Of those that a mesh axis runs over, the one named last changes fastest.
Arguments:
- hidden: bfloat16 [1024, 4096], P(('dp', 'vocab')), may hold values from -48 to 48
- weight: bfloat16 [8192, 4096], P('vocab'), may hold values from -3 to 3
- teacher: bfloat16 [1024, 8192], P('dp', 'vocab'), may hold values from 0 to 0.002, as said below
- block_ids: int32 [8, 64], P('dp'), may hold values from 0 to 63, as said below
Outputs:
- grad_hidden: bfloat16 [1024, 4096], P(('dp', 'vocab'))
- grad_weight: bfloat16 [8192, 4096], P('vocab', 'dp')
Inputs may be any that keep to these rules, and one draw needn't show every extreme that they name: `block_ids`: row b lists 64 different vocabulary blocks in no fixed order; frequent blocks recur over many rows. `teacher`: all entries are positive.
All inputs are finite; a program needn't handle non-finite values.
Results may differ from a plain program's by a relative error of at most 0.0051.
Values may be sent and summed in bfloat16 or wider, within the bound.
No kernel may reach another device: no remote copies, remote signals or barrier semaphores. Data moves between devices by JAX's collectives and lax.ppermute only.
A program may use at most 128 MiB of HBM per device.

v0:
```python
import jax
import jax.numpy as jnp
from jax import lax
from jax.sharding import PartitionSpec as P

BLK = 128


loss_scale = 1024.0


def shards(hidden, weight, teacher, block_ids):
    vocab_rows = weight.shape[0]
    owned_blocks = vocab_rows // BLK
    vocab_pos = lax.axis_index("vocab")
    full_hidden = lax.all_gather(hidden, "vocab", axis=0, tiled=True)
    token_count = full_hidden.shape[0]
    width = full_hidden.shape[1]
    logits = lax.dot_general(
        full_hidden, weight, (((1,), (1,)), ((), ())), preferred_element_type=jnp.float32
    )
    row_top = lax.pmax(jnp.max(logits, axis=1), "vocab")
    exp_terms = jnp.exp(logits - row_top[:, None])
    row_total = lax.psum(jnp.sum(exp_terms, axis=1), "vocab")
    block_count = token_count // BLK
    first_block = vocab_pos * owned_blocks
    block_range = jnp.arange(owned_blocks, dtype=jnp.int32)
    tile_cols = lax.all_gather(teacher, "vocab", axis=1, tiled=True)
    slot_count = tile_cols.shape[1] // BLK
    owned = block_ids - first_block
    onehot = (owned[:, :, None] == block_range[None, None, :]).astype(jnp.bfloat16)
    shaped = tile_cols.reshape(block_count, BLK, slot_count, BLK)
    placed = jnp.einsum("bkv,btkc->btvc", onehot, shaped, preferred_element_type=jnp.float32)
    target = placed
    row_mass = jnp.sum(tile_cols, axis=1, dtype=jnp.float32)
    target = target.reshape(token_count, vocab_rows)
    grad_logits = (
        loss_scale * (row_mass[:, None] * (exp_terms / row_total[:, None]) - target)
    ).astype(jnp.bfloat16)
    grad_hidden = lax.psum_scatter(
        jnp.dot(grad_logits, weight, preferred_element_type=jnp.float32),
        "vocab",
        scatter_dimension=0,
        tiled=True,
    ).astype(jnp.bfloat16)
    data_count = lax.axis_size("dp")
    quarter = width // data_count
    split_hidden = full_hidden.reshape(token_count, data_count, quarter)
    quarter_rows = lax.all_to_all(
        split_hidden, "dp", split_axis=1, concat_axis=0, tiled=True
    ).reshape(token_count * data_count, quarter)
    grad_weight = lax.dot_general(
        lax.all_gather(grad_logits, "dp", axis=0, tiled=True),
        quarter_rows,
        (((0,), (0,)), ((), ())),
        preferred_element_type=jnp.float32,
    ).astype(jnp.bfloat16)
    return (grad_hidden, grad_weight)


def solution(mesh):
    placed = (P(("dp", "vocab"), None), P("vocab", None), P("dp", "vocab"), P("dp", None))
    return jax.shard_map(
        shards,
        mesh=mesh,
        in_specs=placed,
        out_specs=(P(("dp", "vocab"), None), P("vocab", "dp")),
        check_vma=False,
    )
```

profile of v0, /device:TPU:0, one launch (start us, length us, event | category | flops | bytes accessed | tf_op | source)
XLA Modules:
  0.0 207.6 jit_solution(5680426274167567665)
XLA Ops:
  7.2 0.0 all-gather.6.cloned.1.call-start
  7.2 0.7 all-gather.6.cloned.1.call-update
  7.9 0.0 all-gather.4.cloned.1.call-start
  7.9 0.7 all-gather.4.cloned.1.call-update
  8.6 0.0 all-gather.8.cloned.1.call-start
  8.7 0.7 broadcast_subtract_fusion
  9.4 32.1 %all-gather.6.cloned.1.call-done = bf16[256,4096]{1,0:T(8,128)(2,1)} async-done(((bf16[32,4096]{1,0:T(8,128)(2,1)}), bf16[256,4096]{1,0:T(8,128)(2,1)}) %all-gather.6.cloned.1.call-update) | async-done | bytes 2097168 | tf_op jit(solution)/shard_map/all_gather | solution.py:16
  41.4 6.5 %fusion.8 = (f32[256]{0:T(256)S(1)}, f32[256,1024]{1,0:T(8,128)S(1)}) fusion(bf16[256,4096]{1,0:T(8,128)(2,1)} %all-gather.6.cloned.1.call-done, bf16[1024,4096]{1,0:T(8,128)(2,1)} %param.5), kind=kOutput, calls=%fused_computation.13 | convolution fusion | flops 2147745536 | bytes 11535360 | tf_op jit(solution)/shard_map/dot_general | solution.py:19
  47.9 16.0 %pmax.7 = f32[256]{0:T(256)S(1)} all-reduce(f32[256]{0:T(256)S(1)} %get-tuple-element.2), channel_id=1, replica_groups=mesh['dp'=4,'vocab'=8] {'vocab'}, use_global_device_ids=true, to_apply=%region_2.0 | all-reduce | flops 256 | bytes 2048 | tf_op jit(solution)/shard_map/pmax | solution.py:22
  63.9 0.3 fusion.4
  64.2 14.1 %psum.7 = f32[256]{0:T(256)S(1)} all-reduce(f32[256]{0:T(256)S(1)} %fusion.4), channel_id=1, replica_groups=mesh['dp'=4,'vocab'=8] {'vocab'}, use_global_device_ids=true, to_apply=%region_4.0 | all-reduce | flops 256 | bytes 2048 | tf_op jit(solution)/shard_map/psum | solution.py:24
  78.3 11.9 %all-gather.4.cloned.1.call-done = bf16[256,8192]{1,0:T(8,128)(2,1)} async-done(((bf16[256,1024]{1,0:T(8,128)(2,1)}), bf16[256,8192]{1,0:T(8,128)(2,1)}) %all-gather.4.cloned.1.call-update) | async-done | bytes 4194320 | tf_op jit(solution)/shard_map/all_gather | solution.py:28
  90.2 3.4 %copy.11 = bf16[32,8,64,128]{3,2,1,0:T(8,128)(2,1)S(1)} copy(bf16[32,8,64,128]{3,1,2,0:T(8,128)(2,1)} %bitcast.32) | data formatting | bytes 8388608
  93.6 0.0 copy-start
  93.6 0.7 fusion
  94.3 1.4 copy-done
  95.8 0.7 convert_reduce_fusion
  96.4 1.3 fusion.3
  97.7 0.0 all-gather.8.cloned.1.call-update
  97.7 0.0 reduce-scatter.2.cloned.1.call-start
  97.8 7.8 %fusion.9 = f32[256,4096]{1,0:T(8,128)} fusion(bf16[256,1024]{1,0:T(8,128)(2,1)} %fusion.3, bf16[1024,4096]{1,0:T(8,128)(2,1)} %param.5), kind=kOutput, calls=%fused_computation.14 | convolution fusion | flops 2147483648 | bytes 13107200 | tf_op jit(solution)/shard_map/dot_general | solution.py:41
  105.6 0.0 reduce-scatter.2.cloned.1.call-update
  105.6 3.3 %copy.8 = bf16[256,4096]{0,1:T(8,128)(2,1)S(1)} copy(bf16[256,4096]{1,0:T(8,128)(2,1)} %all-gather.6.cloned.1.call-done) | data formatting | bytes 4194304 | tf_op jit(solution)/shard_map/all_gather | solution.py:16
  108.9 40.5 %all_to_all.15 = bf16[256,4,1024]{0,2,1:T(8,128)(2,1)} all-to-all(bf16[256,4,1024]{0,2,1:T(8,128)(2,1)S(1)} %bitcast.34), channel_id=1, replica_groups=mesh['dp'=4,'vocab'=8] {'dp'}, dimensions={1} | all-to-all | bytes 4194304 | tf_op jit(solution)/shard_map/all_to_all | solution.py:49
  149.5 3.0 %copy.9 = bf16[4,256,1,1024]{3,1,0,2:T(8,128)(2,1)S(1)} copy(bf16[4,256,1,1024]{1,3,0,2:T(8,128)(2,1)} %bitcast.35) | data formatting | bytes 4194304 | tf_op jit(solution)/shard_map/all_to_all | solution.py:49
  152.5 0.0 all-gather.8.cloned.1.call-done
  152.5 5.3 %convolution_convert_fusion = bf16[1024,1024]{1,0:T(8,128)(2,1)} fusion(bf16[1024,1024]{1,0:T(8,128)(2,1)} %all-gather.8.cloned.1.call-done, bf16[1024,1024]{1,0:T(8,128)(2,1)S(1)} %bitcast.37), kind=kOutput, calls=%fused_computation.3 | convolution fusion | flops 2148532224 | bytes 6291456 | tf_op jit(solution)/shard_map/dot_general | solution.py:52
  157.8 41.5 %reduce-scatter.2.cloned.1.call-done = f32[32,4096]{1,0:T(8,128)} async-done(((f32[256,4096]{1,0:T(8,128)}), f32[32,4096]{1,0:T(8,128)}) %reduce-scatter.2.cloned.1.call-update) | async-done | bytes 524304 | tf_op jit(solution)/shard_map/reduce_scatter | solution.py:40
  199.3 1.8 convert_element_type.15
Async XLA Ops:
  7.2 34.3 %all-gather.6.cloned.1.call-start = ((), (), s32[]{:S(2)}) async-start(), calls=%async_computation.3 | async-start | bytes 2359296 | tf_op jit(solution)/shard_map/all_gather | solution.py:16
  7.9 82.3 %all-gather.4.cloned.1.call-start = ((), (), s32[]{:S(2)}) async-start(), calls=%async_computation.2 | async-start | bytes 4718592 | tf_op jit(solution)/shard_map/all_gather | solution.py:28
  8.6 143.8 %all-gather.8.cloned.1.call-start = ((), (), s32[]{:S(2)}) async-start(), calls=%async_computation.5 | async-start | bytes 2621440 | tf_op jit(solution)/shard_map/all_gather | solution.py:53
  93.6 2.2 %copy-start = (bf16[256,8192]{1,0:T(8,128)(2,1)S(1)}, bf16[256,8192]{1,0:T(8,128)(2,1)}, u32[]{:S(2)}) copy-start(bf16[256,8192]{1,0:T(8,128)(2,1)} %all-gather.4.cloned.1.call-done) | copy-start | bytes 12582916
  97.7 101.6 %reduce-scatter.2.cloned.1.call-start = ((), (), s32[]{:S(2)}) async-start(), calls=%async_computation.4 | async-start | bytes 4718592 | tf_op jit(solution)/shard_map/reduce_scatter | solution.py:40
Sparse Core Ops, SparseCore 0:
  9.6 31.7 all-gather.5
  43.0 47.1 all-gather.3
  97.9 50.7 all-gather.7
  150.8 48.4 reduce-scatter.1
where the time goes:
time: 208 us
  waiting for transfers between devices  86.9 us (42%)
  blocking collectives  70.6 us (34%)
  matrix products  20.3 us (10%)
  between operations  13.8 us (7%)
  local copies, waits for them, and re-layouts  11.1 us (5%)
  other arithmetic  4.69 us (2%)
    reduce_scatter x1, waiting for transfers between devices, shards(): lax.psum_scatter(jnp.dot(grad_logits, weight, preferred_element_type=jnp....  41.5 us
    all_to_all x1, blocking collectives, shards(): lax.all_to_all(split_hidden, 'dp', split_axis=1, concat_axis=0, tiled=True)  40.5 us
    all_gather x1, waiting for transfers between devices, shards(): full_hidden = lax.all_gather(hidden, 'vocab', axis=0, tiled=True)  32.1 us
    pmax x1, blocking collectives, shards(): row_top = lax.pmax(jnp.max(logits, axis=1), 'vocab')  16 us
    psum x1, blocking collectives, shards(): row_total = lax.psum(jnp.sum(exp_terms, axis=1), 'vocab')  14.1 us
    all_gather x1, waiting for transfers between devices, shards(): tile_cols = lax.all_gather(teacher, 'vocab', axis=1, tiled=True)  11.9 us
    dot_general x1, matrix products, shards(): jnp.dot(grad_logits, weight, preferred_element_type=jnp.float32)  7.83 us
    dot_general x1, matrix products, shards(): lax.dot_general(full_hidden, weight, (((1,), (1,)), ((), ())), preferred_...  6.46 us
  transfers between devices with their start and end apart: 4, of which 3 were waited for; matrix products, arithmetic and copies ran while one was open for 13% of the time, Pallas kernels for 0%

commit v1 on v0

--- a/solution.py
+++ b/solution.py
@@ -1,15 +1,18 @@
 import jax
 import jax.numpy as jnp
 from jax import lax
+from jax.experimental import pallas as pl
+from jax.experimental.pallas import tpu as pltpu
 from jax.sharding import PartitionSpec as P
 
 BLK = 128
+TILE_ROWS = 16
 
 
 loss_scale = 1024.0
 
 
-def shards(hidden, weight, teacher, block_ids):
+def plain_shards(hidden, weight, teacher, block_ids):
     vocab_rows = weight.shape[0]
     owned_blocks = vocab_rows // BLK
     vocab_pos = lax.axis_index("vocab")
@@ -30,8 +33,7 @@
     owned = block_ids - first_block
     onehot = (owned[:, :, None] == block_range[None, None, :]).astype(jnp.bfloat16)
     shaped = tile_cols.reshape(block_count, BLK, slot_count, BLK)
-    placed = jnp.einsum("bkv,btkc->btvc", onehot, shaped, preferred_element_type=jnp.float32)
-    target = placed
+    target = jnp.einsum("bkv,btkc->btvc", onehot, shaped, preferred_element_type=jnp.float32)
     row_mass = jnp.sum(tile_cols, axis=1, dtype=jnp.float32)
     target = target.reshape(token_count, vocab_rows)
     grad_logits = (
@@ -58,12 +60,163 @@
     return (grad_hidden, grad_weight)
 
 
+def swap(x, axis, bits):
+    return lax.ppermute(x, axis, [(i, i ^ bits) for i in range(lax.axis_size(axis))])
+
+
+def take_tiles(slots, teacher, rows, chips):
+    blocks, owned = slots.shape
+
+    def body(slots_ref, teacher_ref, out_ref, sem):
+        me = lax.axis_index("vocab")
+        core = lax.rem(me, 2)
+        chip = me // 2
+        copies = []
+        for h in range(2):
+            for j in range(chips):
+                source = ((chip ^ j) * 2 + (core ^ h)) * rows
+                block = source // BLK
+                for v in range(owned):
+                    copies.append(
+                        pltpu.make_async_copy(
+                            teacher_ref.at[
+                                pl.ds(pl.multiple_of(source, rows), rows),
+                                pl.ds(pl.multiple_of(slots_ref[block, v] * BLK, BLK), BLK),
+                            ],
+                            out_ref.at[pl.ds((h * chips + j) * rows, rows), pl.ds(v * BLK, BLK)],
+                            sem.at[len(copies)],
+                        )
+                    )
+        for copy in copies:
+            copy.start()
+        for copy in copies:
+            copy.wait()
+
+    return pl.pallas_call(
+        body,
+        out_shape=jax.ShapeDtypeStruct((teacher.shape[0], owned * BLK), teacher.dtype),
+        in_specs=[
+            pl.BlockSpec(memory_space=pltpu.SMEM),
+            pl.BlockSpec(memory_space=pl.ANY),
+        ],
+        out_specs=pl.BlockSpec(memory_space=pltpu.VMEM),
+        scratch_shapes=[pltpu.SemaphoreType.DMA((2 * chips * owned,))],
+        cost_estimate=pl.CostEstimate(flops=0, bytes_accessed=2**20, transcendentals=0),
+    )(slots, teacher)
+
+
+def shards(hidden, weight, teacher, block_ids):
+    vocab_size = lax.axis_size("vocab")
+    data_size = lax.axis_size("dp")
+    rows, width = hidden.shape
+    vocab_rows = weight.shape[0]
+    owned_blocks = vocab_rows // BLK
+    chips = vocab_size // 2
+    tokens = vocab_size * rows
+    half_tokens = chips * rows
+    me = lax.axis_index("vocab")
+    core = lax.rem(me, 2)
+    chip = me // 2
+    data_pos = lax.axis_index("dp")
+
+    gathered = lax.all_gather(teacher, "vocab", axis=1, tiled=True)
+    own = jnp.concatenate([hidden] + [swap(hidden, "vocab", 2 * j) for j in range(1, chips)])
+    other = swap(own, "vocab", 1)
+
+    def logits_of(part):
+        return lax.dot_general(
+            part, weight, (((1,), (1,)), ((), ())), preferred_element_type=jnp.float32
+        )
+
+    logits = [logits_of(own), logits_of(other)]
+
+    quarter = width // data_size
+    cols = [
+        lax.dynamic_slice_in_dim(own, (data_pos ^ r) * quarter, quarter, axis=1)
+        for r in range(data_size)
+    ]
+    cols = jnp.stack([cols[0]] + [swap(cols[r], "dp", r) for r in range(1, data_size)])
+    cols = jnp.stack([cols, swap(cols, "vocab", 1)], axis=1).reshape(data_size * tokens, quarter)
+
+    top = jnp.concatenate([jnp.max(x, axis=1) for x in logits])
+    total = jnp.concatenate([
+        jnp.sum(jnp.exp(x - jnp.max(x, axis=1)[:, None]), axis=1) for x in logits
+    ])
+    mass = jnp.sum(teacher, axis=1, dtype=jnp.float32)
+    bits = 1
+    while bits < vocab_size:
+        got = swap(jnp.stack([top, total, mass]), "vocab", bits)
+        grid = got[:2].reshape(2, 2, chips, rows)
+        if bits == 1:
+            grid = grid[:, ::-1]
+        else:
+            grid = jnp.stack([grid[:, :, j ^ (bits // 2)] for j in range(chips)], axis=2)
+        got_top, got_total = grid.reshape(2, tokens)
+        new_top = jnp.maximum(top, got_top)
+        total = total * jnp.exp(top - new_top) + got_total * jnp.exp(got_top - new_top)
+        top = new_top
+        mass = mass + got[2]
+        bits *= 2
+    groups = [(chip ^ j) * 2 + (core ^ h) for h in range(2) for j in range(chips)]
+    mass = jnp.concatenate([lax.dynamic_slice_in_dim(mass, g * rows, rows) for g in groups])
+
+    first_block = me * owned_blocks
+    wanted = first_block + jnp.arange(owned_blocks, dtype=jnp.int32)
+    match = block_ids[:, None, :] == wanted[None, :, None]
+    slots = jnp.argmax(match, axis=2).astype(jnp.int32)
+    listed = jnp.any(match, axis=2).astype(jnp.float32) * loss_scale
+    tiles = take_tiles(slots, gathered, rows, chips)
+    group_block = jnp.stack(groups) * rows // BLK
+    tile_scale = jnp.take(listed, group_block, axis=0)
+    tile_scale = jnp.broadcast_to(
+        tile_scale[:, None, :, None], (vocab_size, rows, owned_blocks, BLK)
+    ).reshape(tokens, vocab_rows)
+
+    factor = loss_scale * mass / total
+    grads = []
+    for h in range(2):
+        part = slice(h * half_tokens, (h + 1) * half_tokens)
+        grads.append(
+            (
+                factor[part, None] * jnp.exp(logits[h] - top[part, None])
+                - tile_scale[part] * tiles[part].astype(jnp.float32)
+            ).astype(jnp.bfloat16)
+        )
+    grad_logits = jnp.concatenate(grads)
+
+    all_grads = jnp.concatenate(
+        [grad_logits] + [swap(grad_logits, "dp", r) for r in range(1, data_size)]
+    )
+    grad_weight = lax.dot_general(
+        all_grads, cols, (((0,), (0,)), ((), ())), preferred_element_type=jnp.float32
+    ).astype(jnp.bfloat16)
+
+    sent = swap(
+        jnp.dot(grads[1], weight, preferred_element_type=jnp.float32).astype(jnp.bfloat16),
+        "vocab",
+        1,
+    )
+    share = jnp.dot(grads[0], weight, preferred_element_type=jnp.float32) + sent.astype(jnp.float32)
+    result = share[:rows]
+    for j in range(1, chips):
+        piece = share[j * rows : (j + 1) * rows].astype(jnp.bfloat16)
+        result = result + swap(piece, "vocab", 2 * j).astype(jnp.float32)
+    return (result.astype(jnp.bfloat16), grad_weight)
+
+
 def solution(mesh):
     placed = (P(("dp", "vocab"), None), P("vocab", None), P("dp", "vocab"), P("dp", None))
-    return jax.shard_map(
-        shards,
-        mesh=mesh,
-        in_specs=placed,
-        out_specs=(P(("dp", "vocab"), None), P("vocab", "dp")),
-        check_vma=False,
-    )
+
+    def run(hidden, weight, teacher, block_ids):
+        rows = hidden.shape[0] // (mesh.shape["dp"] * mesh.shape["vocab"])
+        paired = all(size & (size - 1) == 0 for size in mesh.shape.values())
+        form = shards if paired and rows % TILE_ROWS == 0 else plain_shards
+        return jax.shard_map(
+            form,
+            mesh=mesh,
+            in_specs=placed,
+            out_specs=(P(("dp", "vocab"), None), P("vocab", "dp")),
+            check_vma=False,
+        )(hidden, weight, teacher, block_ids)
+
+    return run

time: 208 us -> 159 us (0.76)
  blocking collectives: 70.6 us -> 0 us
  starting transfers between devices: 0.16 us -> 40.5 us
  waiting for transfers between devices: 86.9 us -> 67.9 us
  local copies, waits for them, and re-layouts: 11.1 us -> 4.36 us
  other arithmetic: 4.69 us -> 8.45 us
  Pallas kernels: 0 us -> 3.16 us
    ppermute x0 -> x18, waiting for transfers between devices: none -> 67.9 us  [swap(): lax.ppermute(x, axis, [(i, i ^ bits) for i in range(lax.axis_size(axis))])]
    all_gather x3 -> x1, waiting for transfers between devices: 44 us -> 0.02 us  [shards(): gathered = lax.all_gather(teacher, 'vocab', axis=1, tiled=True)]
    reduce_scatter x1 -> x0, waiting for transfers between devices: 41.5 us -> none  [shards(): lax.psum_scatter(jnp.dot(grad_logits, weight, preferred_element_type=jnp....]
    all_to_all x1 -> x0, blocking collectives: 40.5 us -> none  [shards(): lax.all_to_all(split_hidden, 'dp', split_axis=1, concat_axis=0, tiled=True)]
    ppermute x0 -> x18, starting transfers between devices: none -> 40.5 us  [swap(): lax.ppermute(x, axis, [(i, i ^ bits) for i in range(lax.axis_size(axis))])]
    pmax x1 -> x0, blocking collectives: 16 us -> none  [shards(): row_top = lax.pmax(jnp.max(logits, axis=1), 'vocab')]
    psum x1 -> x0, blocking collectives: 14.1 us -> none  [shards(): row_total = lax.psum(jnp.sum(exp_terms, axis=1), 'vocab')]
    another operation x0 -> x8, other arithmetic: none -> 3.55 us  [the longest x2 2.7 us: shards(): jnp.stack([cols, swap(cols, 'vocab', 1)], axis=1)]
  transfers between devices with their start and end apart: 4 -> 19, of which waited for: 3 -> 10; matrix products, arithmetic and copies ran while one was open for 13% -> 18% of each run, Pallas kernels for 0% -> 2%
where the time goes in v1:
time: 159 us; the launch traced here: 158 us
  waiting for transfers between devices  67.9 us (43%)
  starting transfers between devices  40.5 us (25%)
  matrix products  19.4 us (12%)
  between operations  14.4 us (9%)
  other arithmetic  8.45 us (5%)
  local copies, waits for them, and re-layouts  4.36 us (3%)
  Pallas kernels  3.16 us (2%)
    ppermute x18, waiting for transfers between devices, swap(): lax.ppermute(x, axis, [(i, i ^ bits) for i in range(lax.axis_size(axis))])  67.9 us
    ppermute x18, starting transfers between devices, swap(): lax.ppermute(x, axis, [(i, i ^ bits) for i in range(lax.axis_size(axis))])  40.5 us
    dot_general x2, matrix products, logits_of(): lax.dot_general(part, weight, (((1,), (1,)), ((), ())), preferred_element...  9.46 us
    dot_general x1, matrix products, shards(): jnp.dot(grads[1], weight, preferred_element_type=jnp.float32)  4.81 us
    dot_general x1, matrix products, shards(): lax.dot_general(all_grads, cols, (((0,), (0,)), ((), ())), preferred_elem...  3.76 us
  transfers between devices with their start and end apart: 19, of which 10 were waited for; matrix products, arithmetic and copies ran while one was open for 18% of the time, Pallas kernels for 2%

profile of v1, /device:TPU:0, one launch (start us, length us, event | category | flops | bytes accessed | tf_op | source)
XLA Modules:
  0.0 158.3 jit_solution(11029446233894636277)
XLA Ops:
  7.2 3.1 %collective-permute-start = (bf16[32,4096]{1,0:T(8,128)(2,1)}, bf16[32,4096]{1,0:T(8,128)(2,1)S(1)}, u32[]{:S(2)}, u32[]{:S(2)}) collective-permute-start(bf16[32,4096]{1,0:T(8,128)(2,1)} %param.4), channel_id=1, source_target_pairs={{0,2},{1,3},{2,0},{3,1},{4,6},{5,7},{6,4},{7,5},{8,10},{9,11},{10,... | collective-permute-start | bytes 786440 | tf_op jit(solution)/shard_map/ppermute | solution.py:64
  10.3 2.6 %collective-permute-start.1 = (bf16[32,4096]{1,0:T(8,128)(2,1)}, bf16[32,4096]{1,0:T(8,128)(2,1)S(1)}, u32[]{:S(2)}, u32[]{:S(2)}) collective-permute-start(bf16[32,4096]{1,0:T(8,128)(2,1)} %param.4), channel_id=1, source_target_pairs={{0,4},{1,5},{2,6},{3,7},{4,0},{5,1},{6,2},{7,3},{8,12},{9,13},{10,... | collective-permute-start | bytes 786440 | tf_op jit(solution)/shard_map/ppermute | solution.py:64
  13.0 1.0 constant_dynamic-update-slice_fusion.3
  13.9 1.2 convert_reduce_fusion
  15.1 0.1 stack.125
  15.3 0.1 stack.116
  15.4 0.9 compare_reduce_fusion.1
  16.2 5.4 %collective-permute-done = bf16[32,4096]{1,0:T(8,128)(2,1)S(1)} collective-permute-done((bf16[32,4096]{1,0:T(8,128)(2,1)}, bf16[32,4096]{1,0:T(8,128)(2,1)S(1)}, u32[]{:S(2)}, u32[]{:S(2)}) %collective-permute-start) | collective-permute-done | bytes 262176 | tf_op jit(solution)/shard_map/ppermute | solution.py:64
  21.7 15.9 %collective-permute-done.1 = bf16[32,4096]{1,0:T(8,128)(2,1)S(1)} collective-permute-done((bf16[32,4096]{1,0:T(8,128)(2,1)}, bf16[32,4096]{1,0:T(8,128)(2,1)S(1)}, u32[]{:S(2)}, u32[]{:S(2)}) %collective-permute-start.1) | collective-permute-done | bytes 262176 | tf_op jit(solution)/shard_map/ppermute | solution.py:64
  37.8 0.6 gather_fusion
  38.4 0.8 compare_reduce_fusion
  39.2 6.5 %fusion.29 = (f32[128]{0:T(128)S(1)}, f32[128,1024]{1,0:T(8,128)S(1)}) fusion(bf16[128,4096]{1,0:T(8,128)(2,1)S(1)} %constant_dynamic-update-slice_fusion, bf16[1024,4096]{1,0:T(8,128)(2,1)} %param.5), kind=kOutput, calls=%fused_computation.89 | convolution fusion | flops 1073872768 | bytes 9961984 | tf_op jit(solution)/shard_map/dot_general | solution.py:127
  45.7 3.0 %fusion.28 = (f32[128]{0:T(128)S(1)}, f32[128,1024]{1,0:T(8,128)S(1)}) fusion(bf16[128,4096]{1,0:T(8,128)(2,1)S(1)} %collective-permute-done.3, bf16[1024,4096]{1,0:T(8,128)(2,1)S(1)} %copy-done), kind=kOutput, calls=%fused_computation.88 | convolution fusion | flops 1073872768 | bytes 9961984 | tf_op jit(solution)/shard_map/dot_general | solution.py:127
  48.7 0.3 exponential_reduce_fusion
  49.0 0.6 collective-permute-start.4
  49.6 0.8 collective-permute-done.4
  50.4 0.1 unstack.57
  50.5 0.1 unstack.59
  50.6 0.1 unstack.53
  50.7 0.1 unstack.55
  50.8 17.6 %collective-permute-start.5 = (f32[3,256]{1,0:T(4,128)S(1)}, f32[3,256]{1,0:T(4,128)S(1)}, u32[]{:S(2)}, u32[]{:S(2)}) collective-permute-start(f32[3,256]{1,0:T(4,128)S(1)} %pad_maximum_fusion.6), channel_id=1, source_target_pairs={{0,2},{1,3},{2,0},{3,1},{4,6},{5,7},{6,4},{7,5},{8,10},{9,11},{10,... | collective-permute-start | bytes 9224 | tf_op jit(solution)/shard_map/ppermute | solution.py:64
  68.4 0.1 dynamic-slice_bitcast_fusion
  68.5 2.5 %collective-permute-start.16 = (bf16[128,1024]{1,0:T(8,128)(2,1)S(1)}, bf16[128,1024]{1,0:T(8,128)(2,1)S(1)}, u32[]{:S(2)}, u32[]{:S(2)}) collective-permute-start(bf16[128,1024]{1,0:T(8,128)(2,1)S(1)} %get-tuple-element.19), channel_id=1, source_target_pairs={{0,24},{8,16},{16,8},{24,0},{1,25},{9,17},{17,9},{25,1},{2,26},{10... | collective-permute-start | bytes 786440 | tf_op jit(solution)/shard_map/ppermute | solution.py:64
  71.0 0.5 collective-permute-start.15
  71.5 0.5 collective-permute-start.14
  72.1 0.1 reshape.506
  72.2 0.1 unstack.63
  72.3 0.1 unstack.61
  72.4 3.4 %collective-permute-start.6 = (f32[3,256]{1,0:T(4,128)S(1)}, f32[3,256]{1,0:T(4,128)S(1)}, u32[]{:S(2)}, u32[]{:S(2)}) collective-permute-start(f32[3,256]{1,0:T(4,128)S(1)} %pad_maximum_fusion.7), channel_id=1, source_target_pairs={{0,4},{1,5},{2,6},{3,7},{4,0},{5,1},{6,2},{7,3},{8,12},{9,13},{10,... | collective-permute-start | bytes 9224 | tf_op jit(solution)/shard_map/ppermute | solution.py:64
  75.8 2.9 %collective-permute-done.16 = bf16[128,1024]{1,0:T(8,128)(2,1)S(1)} collective-permute-done((bf16[128,1024]{1,0:T(8,128)(2,1)S(1)}, bf16[128,1024]{1,0:T(8,128)(2,1)S(1)}, u32[]{:S(2)}, u32[]{:S(2)}) %collective-permute-start.16) | collective-permute-done | bytes 262176 | tf_op jit(solution)/shard_map/ppermute | solution.py:64
  78.7 4.7 %collective-permute-done.15 = bf16[128,1024]{1,0:T(8,128)(2,1)S(1)} collective-permute-done((bf16[128,1024]{1,0:T(8,128)(2,1)S(1)}, bf16[128,1024]{1,0:T(8,128)(2,1)S(1)}, u32[]{:S(2)}, u32[]{:S(2)}) %collective-permute-start.15) | collective-permute-done | bytes 262176 | tf_op jit(solution)/shard_map/ppermute | solution.py:64
  83.4 0.1 collective-permute-done.14
  83.5 0.6 copy-done.3
  84.1 0.1 copy-done.4
  84.2 1.3 fusion.14
  85.5 0.1 unstack.65
  85.6 0.1 unstack.64
  85.7 0.1 unstack.67
  85.8 0.1 unstack.66
  85.9 0.1 reshape.507
  86.0 0.1 unstack.71
  86.1 0.1 unstack.69
  86.2 0.1 fusion.27
  86.3 0.1 concatenate.88
  86.4 3.2 %shard_map.59 = bf16[256,1024]{1,0:T(8,128)(2,1)} custom-call(s32[2,8]{1,0:T(2,128)} %get-tuple-element.3.slots_ref, bf16[256,8192]{1,0:T(8,128)(2,1)} %all-gather.2.cloned.1.call-done.teacher_ref), custom_call_target="tpu_custom_call" | custom-call | bytes 1048576 | tf_op jit(solution)/shard_map/pallas_call | solution.py:95
  89.6 0.1 broadcast_in_dim.16
  89.7 1.2 constant_dynamic-update-slice_fusion.8
  90.9 0.1 broadcast_in_dim.17
  91.1 0.2 constant_dynamic-update-slice_fusion.7
  91.3 4.8 %convolution_convert_fusion = bf16[128,4096]{1,0:T(8,128)(2,1)S(1)} fusion(bf16[128,1024]{1,0:T(8,128)(2,1)S(1)} %get-tuple-element.7, bf16[1024,4096]{1,0:T(8,128)(2,1)} %param.5), kind=kOutput, calls=%fused_computation.1 | convolution fusion | flops 1074266112 | bytes 9699328 | tf_op jit(solution)/shard_map/dot_general | solution.py:195
  96.2 0.6 collective-permute-start.7
  96.7 1.6 collective-permute-start.11
  98.3 0.8 collective-permute-start.12
  99.1 1.2 collective-permute-start.13
  100.3 1.4 pad_maximum_fusion
  101.7 9.9 %collective-permute-done.11 = bf16[256,1024]{1,0:T(8,128)(2,1)S(1)} collective-permute-done((bf16[256,1024]{1,0:T(8,128)(2,1)S(1)}, bf16[256,1024]{1,0:T(8,128)(2,1)S(1)}, u32[]{:S(2)}, u32[]{:S(2)}) %collective-permute-start.11) | collective-permute-done | bytes 524320 | tf_op jit(solution)/shard_map/ppermute | solution.py:64
  111.6 11.5 %collective-permute-done.12 = bf16[256,1024]{1,0:T(8,128)(2,1)S(1)} collective-permute-done((bf16[256,1024]{1,0:T(8,128)(2,1)S(1)}, bf16[256,1024]{1,0:T(8,128)(2,1)S(1)}, u32[]{:S(2)}, u32[]{:S(2)}) %collective-permute-start.12) | collective-permute-done | bytes 524320 | tf_op jit(solution)/shard_map/ppermute | solution.py:64
  123.2 1.4 fusion.17
  124.7 4.8 %collective-permute-start.10 = (bf16[32,4096]{1,0:T(8,128)(2,1)S(1)}, bf16[32,4096]{1,0:T(8,128)(2,1)S(1)}, u32[]{:S(2)}, u32[]{:S(2)}) collective-permute-start(bf16[32,4096]{1,0:T(8,128)(2,1)S(1)} %get-tuple-element.23), channel_id=1, source_target_pairs={{0,6},{1,7},{2,4},{3,5},{4,2},{5,3},{6,0},{7,1},{8,14},{9,15},{10,... | collective-permute-start | bytes 786440 | tf_op jit(solution)/shard_map/ppermute | solution.py:64
  129.5 0.6 collective-permute-start.8
  130.1 3.8 %convolution_convert_fusion.1 = bf16[1024,1024]{1,0:T(8,128)(2,1)} fusion(bf16[1024,1024]{1,0:T(8,128)(2,1)S(1)} %constant_dynamic-update-slice_fusion.4, bf16[1024,1024]{1,0:T(8,128)(2,1)S(1)} %bitcast.77), kind=kOutput, calls=%fused_computation.4 | convolution fusion | flops 2148532224 | bytes 6291456 | tf_op jit(solution)/shard_map/dot_general | solution.py:190
  133.9 2.9 %collective-permute-done.10 = bf16[32,4096]{1,0:T(8,128)(2,1)S(1)} collective-permute-done((bf16[32,4096]{1,0:T(8,128)(2,1)S(1)}, bf16[32,4096]{1,0:T(8,128)(2,1)S(1)}, u32[]{:S(2)}, u32[]{:S(2)}) %collective-permute-start.10) | collective-permute-done | bytes 262176 | tf_op jit(solution)/shard_map/ppermute | solution.py:64
  136.8 13.8 %collective-permute-done.9 = bf16[32,4096]{1,0:T(8,128)(2,1)S(1)} collective-permute-done((bf16[32,4096]{1,0:T(8,128)(2,1)S(1)}, bf16[32,4096]{1,0:T(8,128)(2,1)S(1)}, u32[]{:S(2)}, u32[]{:S(2)}) %collective-permute-start.9) | collective-permute-done | bytes 262176 | tf_op jit(solution)/shard_map/ppermute | solution.py:64
  150.6 0.8 fusion.6
  (68 shorter events, 0.9 us)
Async XLA Ops:
  7.2 31.3 %copy-start.5 = (s32[2,64]{1,0:T(2,128)S(1)}, s32[2,64]{1,0:T(2,128)}, u32[]{:S(2)}) copy-start(s32[2,64]{1,0:T(2,128)} %param.7) | copy-start | bytes 1540
  7.2 79.2 %all-gather.2.cloned.1.call-start = ((), (), s32[]{:S(2)}) async-start(), calls=%async_computation | async-start | bytes 4718592 | tf_op jit(solution)/shard_map/all_gather | solution.py:122
  7.2 14.5 %collective-permute-start = (bf16[32,4096]{1,0:T(8,128)(2,1)}, bf16[32,4096]{1,0:T(8,128)(2,1)S(1)}, u32[]{:S(2)}, u32[]{:S(2)}) collective-permute-start(bf16[32,4096]{1,0:T(8,128)(2,1)} %param.4), channel_id=1, source_target_pairs={{0,2},{1,3},{2,0},{3,1},{4,6},{5,7},{6,4},{7,5},{8,10},{9,11},{10,... | collective-permute-start | bytes 786440 | tf_op jit(solution)/shard_map/ppermute | solution.py:64
  10.3 27.3 %collective-permute-start.1 = (bf16[32,4096]{1,0:T(8,128)(2,1)}, bf16[32,4096]{1,0:T(8,128)(2,1)S(1)}, u32[]{:S(2)}, u32[]{:S(2)}) collective-permute-start(bf16[32,4096]{1,0:T(8,128)(2,1)} %param.4), channel_id=1, source_target_pairs={{0,4},{1,5},{2,6},{3,7},{4,0},{5,1},{6,2},{7,3},{8,12},{9,13},{10,... | collective-permute-start | bytes 786440 | tf_op jit(solution)/shard_map/ppermute | solution.py:64
  12.9 24.8 %collective-permute-start.2 = (bf16[32,4096]{1,0:T(8,128)(2,1)}, bf16[32,4096]{1,0:T(8,128)(2,1)S(1)}, u32[]{:S(2)}, u32[]{:S(2)}) collective-permute-start(bf16[32,4096]{1,0:T(8,128)(2,1)} %param.4), channel_id=1, source_target_pairs={{0,6},{1,7},{2,4},{3,5},{4,2},{5,3},{6,0},{7,1},{8,14},{9,15},{10,... | collective-permute-start | bytes 786440 | tf_op jit(solution)/shard_map/ppermute | solution.py:64
  37.7 8.0 %collective-permute-start.3 = (bf16[128,4096]{1,0:T(8,128)(2,1)S(1)}, bf16[128,4096]{1,0:T(8,128)(2,1)S(1)}, u32[]{:S(2)}, u32[]{:S(2)}) collective-permute-start(bf16[128,4096]{1,0:T(8,128)(2,1)S(1)} %constant_dynamic-update-slice_fusion), channel_id=1, source_target_pairs={{0,1},{1,0},{2,3},{3,2},{4,5},{5,4},{6,7},{7,6},{8,9},{9,8},{10,11... | collective-permute-start | bytes 3145736 | tf_op jit(solution)/shard_map/ppermute | solution.py:64
  39.2 6.5 %copy-start = (bf16[1024,4096]{1,0:T(8,128)(2,1)S(1)}, bf16[1024,4096]{1,0:T(8,128)(2,1)}, u32[]{:S(2)}) copy-start(bf16[1024,4096]{1,0:T(8,128)(2,1)} %param.5) | copy-start | bytes 25165828
  49.0 1.4 collective-permute-start.4
  50.8 21.2 %collective-permute-start.5 = (f32[3,256]{1,0:T(4,128)S(1)}, f32[3,256]{1,0:T(4,128)S(1)}, u32[]{:S(2)}, u32[]{:S(2)}) collective-permute-start(f32[3,256]{1,0:T(4,128)S(1)} %pad_maximum_fusion.6), channel_id=1, source_target_pairs={{0,2},{1,3},{2,0},{3,1},{4,6},{5,7},{6,4},{7,5},{8,10},{9,11},{10,... | collective-permute-start | bytes 9224 | tf_op jit(solution)/shard_map/ppermute | solution.py:64
  68.5 10.2 %collective-permute-start.16 = (bf16[128,1024]{1,0:T(8,128)(2,1)S(1)}, bf16[128,1024]{1,0:T(8,128)(2,1)S(1)}, u32[]{:S(2)}, u32[]{:S(2)}) collective-permute-start(bf16[128,1024]{1,0:T(8,128)(2,1)S(1)} %get-tuple-element.19), channel_id=1, source_target_pairs={{0,24},{8,16},{16,8},{24,0},{1,25},{9,17},{17,9},{25,1},{2,26},{10... | collective-permute-start | bytes 786440 | tf_op jit(solution)/shard_map/ppermute | solution.py:64
  71.0 12.3 %collective-permute-start.15 = (bf16[128,1024]{1,0:T(8,128)(2,1)S(1)}, bf16[128,1024]{1,0:T(8,128)(2,1)S(1)}, u32[]{:S(2)}, u32[]{:S(2)}) collective-permute-start(bf16[128,1024]{1,0:T(8,128)(2,1)S(1)} %get-tuple-element.20), channel_id=1, source_target_pairs={{0,16},{8,24},{16,0},{24,8},{1,17},{9,25},{17,1},{25,9},{2,18},{10... | collective-permute-start | bytes 786440 | tf_op jit(solution)/shard_map/ppermute | solution.py:64
  71.5 11.9 %collective-permute-start.14 = (bf16[128,1024]{1,0:T(8,128)(2,1)S(1)}, bf16[128,1024]{1,0:T(8,128)(2,1)S(1)}, u32[]{:S(2)}, u32[]{:S(2)}) collective-permute-start(bf16[128,1024]{1,0:T(8,128)(2,1)S(1)} %get-tuple-element.21), channel_id=1, source_target_pairs={{0,8},{8,0},{16,24},{24,16},{1,9},{9,1},{17,25},{25,17},{2,10},{10... | collective-permute-start | bytes 786440 | tf_op jit(solution)/shard_map/ppermute | solution.py:64
  72.4 13.5 %collective-permute-start.6 = (f32[3,256]{1,0:T(4,128)S(1)}, f32[3,256]{1,0:T(4,128)S(1)}, u32[]{:S(2)}, u32[]{:S(2)}) collective-permute-start(f32[3,256]{1,0:T(4,128)S(1)} %pad_maximum_fusion.7), channel_id=1, source_target_pairs={{0,4},{1,5},{2,6},{3,7},{4,0},{5,1},{6,2},{7,3},{8,12},{9,13},{10,... | collective-permute-start | bytes 9224 | tf_op jit(solution)/shard_map/ppermute | solution.py:64
  78.7 4.8 %copy-start.2 = (bf16[128,1024]{1,0:T(8,128)(2,1)}, bf16[128,1024]{1,0:T(8,128)(2,1)S(1)}, u32[]{:S(2)}) copy-start(bf16[128,1024]{1,0:T(8,128)(2,1)S(1)} %collective-permute-done.16) | copy-start | bytes 786436
  83.4 0.7 copy-start.3
  83.5 0.7 copy-start.4
  85.5 14.8 %collective-permute-start.17 = (bf16[4,128,1024]{2,1,0:T(8,128)(2,1)S(1)}, bf16[4,128,1024]{2,1,0:T(8,128)(2,1)}, u32[]{:S(2)}, u32[]{:S(2)}) collective-permute-start(bf16[4,128,1024]{2,1,0:T(8,128)(2,1)S(1)} %get-tuple-element.17), channel_id=1, source_target_pairs={{0,1},{1,0},{2,3},{3,2},{4,5},{5,4},{6,7},{7,6},{8,9},{9,8},{10,11... | collective-permute-start | bytes 3145736 | tf_op jit(solution)/shard_map/ppermute | solution.py:64
  89.6 1.5 copy-start.1
  91.1 32.1 %slice-start = ((s8[8388608]{0:T(1024)(128)(4,1)}), s8[4194304]{0:T(1024)(128)(4,1)S(1)}, s32[]{:S(2)}) async-start(s8[8388608]{0:T(1024)(128)(4,1)} %bitcast.73), calls=%async_computation.1 | async-start | bytes 8388608
  91.3 31.9 %slice-start.1 = ((s8[8388608]{0:T(1024)(128)(4,1)}), s8[4194304]{0:T(1024)(128)(4,1)S(1)}, s32[]{:S(2)}) async-start(s8[8388608]{0:T(1024)(128)(4,1)} %bitcast.73), calls=%async_computation.2 | async-start | bytes 8388608
  96.2 27.1 %collective-permute-start.7 = (bf16[128,4096]{1,0:T(8,128)(2,1)S(1)}, bf16[128,4096]{1,0:T(8,128)(2,1)S(1)}, u32[]{:S(2)}, u32[]{:S(2)}) collective-permute-start(bf16[128,4096]{1,0:T(8,128)(2,1)S(1)} %convolution_convert_fusion), channel_id=1, source_target_pairs={{0,1},{1,0},{2,3},{3,2},{4,5},{5,4},{6,7},{7,6},{8,9},{9,8},{10,11... | collective-permute-start | bytes 3145736 | tf_op jit(solution)/shard_map/ppermute | solution.py:64
  96.7 14.9 %collective-permute-start.11 = (bf16[256,1024]{1,0:T(8,128)(2,1)S(1)}, bf16[256,1024]{1,0:T(8,128)(2,1)S(1)}, u32[]{:S(2)}, u32[]{:S(2)}) collective-permute-start(bf16[256,1024]{1,0:T(8,128)(2,1)S(1)} %pad_maximum_fusion.2), channel_id=1, source_target_pairs={{0,8},{8,0},{16,24},{24,16},{1,9},{9,1},{17,25},{25,17},{2,10},{10... | collective-permute-start | bytes 1572872 | tf_op jit(solution)/shard_map/ppermute | solution.py:64
  98.3 24.8 %collective-permute-start.12 = (bf16[256,1024]{1,0:T(8,128)(2,1)S(1)}, bf16[256,1024]{1,0:T(8,128)(2,1)S(1)}, u32[]{:S(2)}, u32[]{:S(2)}) collective-permute-start(bf16[256,1024]{1,0:T(8,128)(2,1)S(1)} %pad_maximum_fusion.2), channel_id=1, source_target_pairs={{0,16},{8,24},{16,0},{24,8},{1,17},{9,25},{17,1},{25,9},{2,18},{10... | collective-permute-start | bytes 1572872 | tf_op jit(solution)/shard_map/ppermute | solution.py:64
  99.1 24.0 %collective-permute-start.13 = (bf16[256,1024]{1,0:T(8,128)(2,1)S(1)}, bf16[256,1024]{1,0:T(8,128)(2,1)S(1)}, u32[]{:S(2)}, u32[]{:S(2)}) collective-permute-start(bf16[256,1024]{1,0:T(8,128)(2,1)S(1)} %pad_maximum_fusion.2), channel_id=1, source_target_pairs={{0,24},{8,16},{16,8},{24,0},{1,25},{9,17},{17,9},{25,1},{2,26},{10... | collective-permute-start | bytes 1572872 | tf_op jit(solution)/shard_map/ppermute | solution.py:64
  124.7 12.1 %collective-permute-start.10 = (bf16[32,4096]{1,0:T(8,128)(2,1)S(1)}, bf16[32,4096]{1,0:T(8,128)(2,1)S(1)}, u32[]{:S(2)}, u32[]{:S(2)}) collective-permute-start(bf16[32,4096]{1,0:T(8,128)(2,1)S(1)} %get-tuple-element.23), channel_id=1, source_target_pairs={{0,6},{1,7},{2,4},{3,5},{4,2},{5,3},{6,0},{7,1},{8,14},{9,15},{10,... | collective-permute-start | bytes 786440 | tf_op jit(solution)/shard_map/ppermute | solution.py:64
  129.5 21.1 %collective-permute-start.9 = (bf16[32,4096]{1,0:T(8,128)(2,1)S(1)}, bf16[32,4096]{1,0:T(8,128)(2,1)S(1)}, u32[]{:S(2)}, u32[]{:S(2)}) collective-permute-start(bf16[32,4096]{1,0:T(8,128)(2,1)S(1)} %get-tuple-element.24), channel_id=1, source_target_pairs={{0,4},{1,5},{2,6},{3,7},{4,0},{5,1},{6,2},{7,3},{8,12},{9,13},{10,... | collective-permute-start | bytes 786440 | tf_op jit(solution)/shard_map/ppermute | solution.py:64
  129.5 21.1 %collective-permute-start.8 = (bf16[32,4096]{1,0:T(8,128)(2,1)S(1)}, bf16[32,4096]{1,0:T(8,128)(2,1)S(1)}, u32[]{:S(2)}, u32[]{:S(2)}) collective-permute-start(bf16[32,4096]{1,0:T(8,128)(2,1)S(1)} %get-tuple-element.22), channel_id=1, source_target_pairs={{0,2},{1,3},{2,0},{3,1},{4,6},{5,7},{6,4},{7,5},{8,10},{9,11},{10,... | collective-permute-start | bytes 786440 | tf_op jit(solution)/shard_map/ppermute | solution.py:64
Sparse Core Ops, SparseCore 0:
  13.0 58.3 all-gather.1

commit v2 on v0

--- a/solution.py
+++ b/solution.py
@@ -1,15 +1,18 @@
 import jax
 import jax.numpy as jnp
 from jax import lax
+from jax.experimental import pallas as pl
+from jax.experimental.pallas import tpu as pltpu
 from jax.sharding import PartitionSpec as P
 
 BLK = 128
+TILE_ROWS = 16
 
 
 loss_scale = 1024.0
 
 
-def shards(hidden, weight, teacher, block_ids):
+def plain_shards(hidden, weight, teacher, block_ids):
     vocab_rows = weight.shape[0]
     owned_blocks = vocab_rows // BLK
     vocab_pos = lax.axis_index("vocab")
@@ -30,8 +33,7 @@
     owned = block_ids - first_block
     onehot = (owned[:, :, None] == block_range[None, None, :]).astype(jnp.bfloat16)
     shaped = tile_cols.reshape(block_count, BLK, slot_count, BLK)
-    placed = jnp.einsum("bkv,btkc->btvc", onehot, shaped, preferred_element_type=jnp.float32)
-    target = placed
+    target = jnp.einsum("bkv,btkc->btvc", onehot, shaped, preferred_element_type=jnp.float32)
     row_mass = jnp.sum(tile_cols, axis=1, dtype=jnp.float32)
     target = target.reshape(token_count, vocab_rows)
     grad_logits = (
@@ -58,12 +60,386 @@
     return (grad_hidden, grad_weight)
 
 
+def swap(x, axis, bits):
+    return lax.ppermute(x, axis, [(i, i ^ bits) for i in range(lax.axis_size(axis))])
+
+
+ANY = pl.BlockSpec(memory_space=pl.ANY)
+WHOLE = pl.BlockSpec(memory_space=pltpu.VMEM)
+SCALARS = pl.BlockSpec(memory_space=pltpu.SMEM)
+MIB = 2**20
+
+
+def in_hbm(x):
+    return pltpu.with_memory_space_constraint(x, pltpu.HBM)
+
+
+def place_on_mesh():
+    me = lax.axis_index("vocab")
+    return me // 2, lax.rem(me, 2)
+
+
+def as_row(column):
+    n = column.shape[0]
+    same = lax.broadcasted_iota(jnp.int32, (n, n), 0) == lax.broadcasted_iota(jnp.int32, (n, n), 1)
+    return jnp.sum(jnp.where(same, column, 0.0), axis=0, keepdims=True)
+
+
+def as_column(row):
+    n = row.shape[1]
+    same = lax.broadcasted_iota(jnp.int32, (n, n), 0) == lax.broadcasted_iota(jnp.int32, (n, n), 1)
+    return jnp.sum(jnp.where(same, row, 0.0), axis=1, keepdims=True)
+
+
+def merge(stats):
+    top = stats[0][0:1]
+    for x in stats[1:]:
+        top = jnp.maximum(top, x[0:1])
+    total = sum(x[1:2] * jnp.exp(x[0:1] - top) for x in stats)
+    mass = sum(x[2:3] for x in stats)
+    return top, total, mass
+
+
+def cost(flops, ops):
+    return pl.CostEstimate(
+        flops=flops, bytes_accessed=sum(op.size * 2 for op in ops), transcendentals=0
+    )
+
+
+def logits_and_stats(own, other, rows, weight, mass, quarter, parts=4):
+    half, width = own.shape
+    chips = half // rows
+    tokens = 2 * half
+    vocab_rows = weight.shape[0]
+    step = vocab_rows // parts
+    groups = width // quarter
+
+    def body(*refs):
+        piece_refs, refs = refs[:2], refs[2:]
+        weight_ref, mass_ref, out_ref, stats_ref, refs = *refs[:4], refs[4:]
+        cols_refs, refs = refs[:groups], refs[groups:]
+        held, held_weight, sems, piece_sems, cols_sems = refs
+        chip, core = place_on_mesh()
+        data_pos = lax.axis_index("dp")
+        loads = []
+        for h in range(2):
+            for j in range(chips):
+                start = ((chip ^ j) * 2 + (core ^ h)) * rows
+                n = h * chips + j
+                loads.append(
+                    pltpu.make_async_copy(
+                        piece_refs[h].at[pl.ds(j * rows, rows)],
+                        held.at[pl.ds(pl.multiple_of(start, rows), rows)],
+                        piece_sems.at[n],
+                    )
+                )
+                loads[n].start()
+        copies = []
+        for k in range(parts):
+            some = pl.ds(k * step, step)
+            copies.append(
+                pltpu.make_async_copy(weight_ref.at[some], held_weight.at[some], sems.at[k])
+            )
+            copies[k].start()
+        for load in loads:
+            load.wait()
+        stores = []
+        for r in range(groups):
+            column = pl.multiple_of((data_pos ^ r) * quarter, quarter)
+            for j in range(chips):
+                start = ((chip ^ j) * 2 + core) * rows
+                stores.append(
+                    pltpu.make_async_copy(
+                        held.at[pl.ds(pl.multiple_of(start, rows), rows), pl.ds(column, quarter)],
+                        cols_refs[r].at[pl.ds(j * rows, rows)],
+                        cols_sems.at[r, j],
+                    )
+                )
+                stores[-1].start()
+        for k in range(parts):
+            copies[k].wait()
+            out_ref[:, k * step : (k + 1) * step] = lax.dot_general(
+                held[...],
+                held_weight[k * step : (k + 1) * step],
+                (((1,), (1,)), ((), ())),
+                preferred_element_type=jnp.float32,
+            )
+        top = jnp.max(out_ref[...], axis=1, keepdims=True)
+        total = jnp.sum(jnp.exp(out_ref[...] - top), axis=1, keepdims=True)
+        stats_ref[0:1] = as_row(top)
+        stats_ref[1:2] = as_row(total)
+        stats_ref[2:3] = mass_ref[...]
+        stats_ref[3:8] = jnp.zeros((5, tokens), jnp.float32)
+        for store in stores:
+            store.wait()
+
+    ops = [own, other, in_hbm(weight), mass]
+    return pl.pallas_call(
+        body,
+        out_shape=[
+            jax.ShapeDtypeStruct((tokens, vocab_rows), jnp.float32),
+            jax.ShapeDtypeStruct((8, tokens), jnp.float32),
+        ]
+        + [jax.ShapeDtypeStruct((half, quarter), weight.dtype)] * groups,
+        in_specs=[ANY] * 3 + [WHOLE],
+        out_specs=[WHOLE, WHOLE] + [ANY] * groups,
+        scratch_shapes=[
+            pltpu.VMEM((tokens, width), weight.dtype),
+            pltpu.VMEM(weight.shape, weight.dtype),
+            pltpu.SemaphoreType.DMA((parts,)),
+            pltpu.SemaphoreType.DMA((2 * chips,)),
+            pltpu.SemaphoreType.DMA((groups, chips)),
+        ],
+        compiler_params=pltpu.CompilerParams(vmem_limit_bytes=32 * MIB),
+        cost_estimate=cost(2 * tokens * weight.size, ops),
+    )(*ops)
+
+
+def merge_pair(a, b):
+    def body(a_ref, b_ref, out_ref):
+        for k, row in enumerate(merge([a_ref[...], b_ref[...]])):
+            out_ref[k : k + 1] = row
+        out_ref[3:8] = jnp.zeros((5, a.shape[1]), jnp.float32)
+
+    return pl.pallas_call(
+        body,
+        out_shape=jax.ShapeDtypeStruct(a.shape, a.dtype),
+        in_specs=[WHOLE, WHOLE],
+        out_specs=WHOLE,
+        compiler_params=pltpu.CompilerParams(vmem_limit_bytes=MIB),
+        cost_estimate=cost(0, (a, b)),
+    )(a, b)
+
+
+def place_tiles(slots, listed, mine, sibling):
+    chips, rows, columns = sibling.shape
+    per = columns // BLK
+    owned = slots.shape[0] // (2 * chips)
+
+    def body(slots_ref, listed_ref, *refs):
+        mine_refs, sibling_ref = refs[:chips], refs[chips]
+        outs, held = refs[chips + 1 : 2 * chips + 1], refs[2 * chips + 1]
+        start = pl.multiple_of(place_on_mesh()[1] * rows, rows)
+        for j in range(chips):
+            held[j] = mine_refs[j][pl.ds(start, rows), :]
+            held[chips + j] = sibling_ref[j]
+        for r in range(chips):
+            for c in range(2):
+                for v in range(owned):
+                    n = (r * 2 + c) * owned + v
+                    slot = slots_ref[n]
+                    column = pl.multiple_of(lax.rem(slot, per) * BLK, BLK)
+                    tile = held[slot // per, :, pl.ds(column, BLK)]
+                    outs[r][c * rows : (c + 1) * rows, v * BLK : (v + 1) * BLK] = jnp.where(
+                        listed_ref[n] > 0, tile, jnp.zeros_like(tile)
+                    )
+
+    shape = jax.ShapeDtypeStruct((2 * rows, owned * BLK), sibling.dtype)
+    return pl.pallas_call(
+        body,
+        out_shape=[shape] * chips,
+        in_specs=[SCALARS] * 2 + [WHOLE] * (chips + 1),
+        out_specs=[WHOLE] * chips,
+        scratch_shapes=[pltpu.VMEM((2 * chips, rows, columns), sibling.dtype)],
+        compiler_params=pltpu.CompilerParams(vmem_limit_bytes=16 * MIB),
+        cost_estimate=cost(0, (sibling, sibling)),
+    )(slots, listed, *mine, sibling)
+
+
+def logit_grads(logits, stats, mine, sibling, weight, after, parts=8):
+    chips, rows, vocab_rows = sibling.shape
+    tokens = logits.shape[0]
+    half = chips * rows
+    width = weight.shape[1]
+    step = width // parts
+    count = len(stats)
+
+    def body(logits_ref, *refs):
+        stats_refs, refs = refs[:count], refs[count:]
+        mine_refs, refs = refs[:chips], refs[chips:]
+        sibling_ref, weight_ref, refs = refs[0], refs[1], refs[2 + len(after) :]
+        out_ref, own_ref, other_ref, held, held_weight, columns, sems = refs
+        copies = []
+        for k in range(parts):
+            some = pl.ds(k * step, step)
+            copies.append(
+                pltpu.make_async_copy(
+                    weight_ref.at[:, some], held_weight.at[:, some], sems.at[k]
+                )
+            )
+            copies[k].start()
+        top, total, mass = merge([ref[...] for ref in stats_refs])
+        columns[:, 0:1] = as_column(top)
+        columns[:, 1:2] = as_column(loss_scale * mass / total)
+        chip, core = place_on_mesh()
+        mine_start = pl.multiple_of(core * rows, rows)
+        for h in range(2):
+            for j in range(chips):
+                start = ((chip ^ j) * 2 + (core ^ h)) * rows
+                part = pl.ds(pl.multiple_of(start, rows), rows)
+                tiles = sibling_ref[j] if h else mine_refs[j][pl.ds(mine_start, rows), :]
+                grads = (
+                    columns[part, 1:2] * jnp.exp(logits_ref[part, :] - columns[part, 0:1])
+                    - loss_scale * tiles.astype(jnp.float32)
+                ).astype(held.dtype)
+                held[(h * chips + j) * rows : (h * chips + j + 1) * rows] = grads
+        for k in range(parts):
+            copies[k].wait()
+            some = slice(k * step, (k + 1) * step)
+            share = jnp.dot(held[...], held_weight[:, some], preferred_element_type=jnp.float32)
+            own_ref[:, some] = share[:half]
+            other_ref[:, some] = share[half:].astype(other_ref.dtype)
+        out_ref[...] = held[...].T
+
+    ops = (logits, *stats, *mine, sibling, in_hbm(weight))
+    return pl.pallas_call(
+        body,
+        out_shape=[
+            jax.ShapeDtypeStruct((vocab_rows, tokens), jnp.bfloat16),
+            jax.ShapeDtypeStruct((half, width), jnp.float32),
+            jax.ShapeDtypeStruct((half, width), jnp.bfloat16),
+        ],
+        in_specs=[WHOLE] * (len(ops) - 1) + [ANY] * (1 + len(after)),
+        out_specs=[WHOLE] * 3,
+        scratch_shapes=[
+            pltpu.VMEM((tokens, vocab_rows), jnp.bfloat16),
+            pltpu.VMEM(weight.shape, weight.dtype),
+            pltpu.VMEM((tokens, 128), jnp.float32),
+            pltpu.SemaphoreType.DMA((parts,)),
+        ],
+        compiler_params=pltpu.CompilerParams(vmem_limit_bytes=32 * MIB),
+        cost_estimate=cost(2 * weight.size * tokens, ops),
+    )(*ops, *after)
+
+
+def weight_grad(grads, own_cols, other_cols):
+    counts = [len(parts) for parts in grads]
+    flat = [part for parts in grads for part in parts]
+    groups = len(grads)
+    vocab_rows = sum(part.shape[0] for part in grads[0])
+    half, columns = own_cols[0].shape
+
+    def body(*refs):
+        own_refs, other_refs = refs[len(flat) : -1][:groups], refs[len(flat) : -1][groups:]
+        out_ref = refs[-1]
+        total = None
+        for r in range(groups):
+            at = sum(counts[:r])
+            parts = [ref[...] for ref in refs[at : at + counts[r]]]
+            rows = jnp.concatenate(parts) if counts[r] > 1 else parts[0]
+            for n, ref in enumerate((own_refs[r], other_refs[r])):
+                term = jnp.dot(
+                    rows[:, n * half : (n + 1) * half], ref[...], preferred_element_type=jnp.float32
+                )
+                total = term if total is None else total + term
+        out_ref[...] = total.astype(out_ref.dtype)
+
+    ops = [*flat, *own_cols, *other_cols]
+    return pl.pallas_call(
+        body,
+        out_shape=jax.ShapeDtypeStruct((vocab_rows, columns), jnp.bfloat16),
+        in_specs=[WHOLE] * len(ops),
+        out_specs=WHOLE,
+        compiler_params=pltpu.CompilerParams(vmem_limit_bytes=24 * MIB),
+        cost_estimate=cost(2 * groups * vocab_rows * 2 * half * columns, ops),
+    )(*ops)
+
+
+def shards(hidden, weight, teacher, block_ids):
+    vocab_size = lax.axis_size("vocab")
+    data_size = lax.axis_size("dp")
+    rows, width = hidden.shape
+    owned_blocks = weight.shape[0] // BLK
+    chips = vocab_size // 2
+    me = lax.axis_index("vocab")
+    chip, core = place_on_mesh()
+
+    pieces = [hidden]
+    while 2 * len(pieces) < chips:
+        pieces = pieces + [swap(piece, "vocab", 2 * len(pieces)) for piece in pieces]
+    far = swap(hidden, "vocab", 2 * len(pieces))
+
+    def between_chips(parts):
+        return [parts[0]] + [swap(parts[r], "vocab", 2 * r) for r in range(1, chips)]
+
+    def between_cores(parts):
+        given = [lax.dynamic_slice_in_dim(part, (1 - core) * rows, rows) for part in parts]
+        return swap(jnp.stack(given), "vocab", 1)
+
+    far, late_teacher = lax.optimization_barrier((far, teacher))
+    pieces = pieces + [far] + [swap(far, "vocab", 2 * j) for j in range(1, len(pieces))]
+    own = jnp.concatenate(pieces)
+    other = swap(own, "vocab", 1)
+    got = between_chips(
+        [lax.dynamic_slice_in_dim(late_teacher, (chip ^ r) * 2 * rows, 2 * rows) for r in range(chips)]
+    )
+    my_ids = lax.dynamic_index_in_dim(block_ids, me * rows // BLK, keepdims=False)
+    per = teacher.shape[1] // BLK
+    owners = jnp.stack([(chip ^ r) * 2 + c for r in range(chips) for c in range(2)])
+    blocks = (owners[:, None] * owned_blocks + jnp.arange(owned_blocks)[None, :]).reshape(-1)
+    match = my_ids[None, :] == blocks[:, None]
+    listed = jnp.any(match, axis=1).astype(jnp.int32)
+    slots = jnp.argmax(match, axis=1).astype(jnp.int32)
+    source = slots // per
+    place = ((source % 2) ^ core) * chips + ((source // 2) ^ chip)
+    placed = place_tiles(place * per + slots % per, listed, got, between_cores(got))
+    tiles = between_chips(placed)
+
+    mass = jnp.sum(teacher, axis=1, dtype=jnp.float32)[None, :]
+    logits, stats, *cols = logits_and_stats(
+        own, other, rows, weight, mass, width // data_size
+    )
+
+    tiles, stats = lax.optimization_barrier((tiles, stats))
+    stats = merge_pair(stats, swap(stats, "vocab", 1))
+    *cols, stats = lax.optimization_barrier((*cols, stats))
+    own_cols = [cols[0]] + [swap(cols[r], "dp", r) for r in range(1, data_size)]
+    other_cols = [swap(x, "vocab", 1) for x in own_cols]
+    bits = 2
+    while 2 * bits < vocab_size:
+        stats = merge_pair(stats, swap(stats, "vocab", bits))
+        bits *= 2
+    all_stats = [stats, swap(stats, "vocab", bits)]
+    grad_logits, share, rest = logit_grads(
+        logits, all_stats, tiles, between_cores(tiles), weight, own_cols
+    )
+
+    share = share + swap(rest, "vocab", 1).astype(jnp.float32)
+    shares = [share[j * rows : (j + 1) * rows] for j in range(chips)]
+    count = 1
+    while count < chips:
+        for base in range(0, chips, 2 * count):
+            sent = swap(shares[base + count].astype(jnp.bfloat16), "vocab", 2 * count)
+            shares[base] = shares[base] + sent.astype(jnp.float32)
+        count *= 2
+
+    middle = grad_logits.shape[0] // 2
+    all_grads = [[grad_logits]]
+    bits = 1
+    while bits < data_size:
+        known = [jnp.concatenate(parts) if len(parts) > 1 else parts[0] for parts in all_grads]
+        all_grads.append([swap(grad_logits, "dp", bits)])
+        for r in range(1, bits):
+            near, far = known[r], all_grads[bits][0]
+            all_grads.append([swap(near[:middle], "dp", bits), swap(far[middle:], "dp", r)])
+        bits *= 2
+    grad_weight = weight_grad(all_grads, own_cols, other_cols)
+    return (shares[0].astype(jnp.bfloat16), grad_weight)
+
+
 def solution(mesh):
     placed = (P(("dp", "vocab"), None), P("vocab", None), P("dp", "vocab"), P("dp", None))
-    return jax.shard_map(
-        shards,
-        mesh=mesh,
-        in_specs=placed,
-        out_specs=(P(("dp", "vocab"), None), P("vocab", "dp")),
-        check_vma=False,
-    )
+
+    def run(hidden, weight, teacher, block_ids):
+        rows = hidden.shape[0] // (mesh.shape["dp"] * mesh.shape["vocab"])
+        paired = all(size & (size - 1) == 0 for size in mesh.shape.values())
+        form = shards if paired and rows % TILE_ROWS == 0 else plain_shards
+        return jax.shard_map(
+            form,
+            mesh=mesh,
+            in_specs=placed,
+            out_specs=(P(("dp", "vocab"), None), P("vocab", "dp")),
+            check_vma=False,
+        )(hidden, weight, teacher, block_ids)
+
+    return run

time: 208 us -> 110 us (0.53)
  blocking collectives: 70.6 us -> 0 us
  waiting for transfers between devices: 86.9 us -> 49.2 us
  starting transfers between devices: 0.16 us -> 35.8 us
  matrix products: 20.3 us -> 0 us
  Pallas kernels: 0 us -> 19.4 us
  between operations: 13.8 us -> 0.94 us
  local copies, waits for them, and re-layouts: 11.1 us -> 2.53 us
  other arithmetic: 4.69 us -> 2.33 us
    ppermute x0 -> x30, waiting for transfers between devices: none -> 49.2 us  [swap(): lax.ppermute(x, axis, [(i, i ^ bits) for i in range(lax.axis_size(axis))])]
    all_gather x3 -> x0, waiting for transfers between devices: 44 us -> none  [the longest x1 32.1 us: shards(): full_hidden = lax.all_gather(hidden, 'vocab', axis=0, tiled=True)]
    reduce_scatter x1 -> x0, waiting for transfers between devices: 41.5 us -> none  [shards(): lax.psum_scatter(jnp.dot(grad_logits, weight, preferred_element_type=jnp....]
    all_to_all x1 -> x0, blocking collectives: 40.5 us -> none  [shards(): lax.all_to_all(split_hidden, 'dp', split_axis=1, concat_axis=0, tiled=True)]
    ppermute x0 -> x30, starting transfers between devices: none -> 35.8 us  [swap(): lax.ppermute(x, axis, [(i, i ^ bits) for i in range(lax.axis_size(axis))])]
    dot_general x4 -> x0, matrix products: 20.3 us -> none  [the longest x1 7.83 us: shards(): jnp.dot(grad_logits, weight, preferred_element_type=jnp.float32)]
    pallas_call x0 -> x6, Pallas kernels: none -> 19.4 us  [the longest x1 7.33 us: logits_and_stats(): pl.pallas_call(body, out_shape=[jax.ShapeDtypeStruct((tokens, vocab_rows)...]
    pmax x1 -> x0, blocking collectives: 16 us -> none  [shards(): row_top = lax.pmax(jnp.max(logits, axis=1), 'vocab')]
  transfers between devices with their start and end apart: 4 -> 30, of which waited for: 3 -> 16; matrix products, arithmetic and copies ran while one was open for 13% -> 4% of each run, Pallas kernels for 0% -> 13%
where the time goes in v2:
time: 110 us
  waiting for transfers between devices  49.2 us (45%)
  starting transfers between devices  35.8 us (33%)
  Pallas kernels  19.4 us (18%)
  local copies, waits for them, and re-layouts  2.53 us (2%)
  other arithmetic  2.33 us (2%)
    ppermute x30, waiting for transfers between devices, swap(): lax.ppermute(x, axis, [(i, i ^ bits) for i in range(lax.axis_size(axis))])  49.2 us
    ppermute x30, starting transfers between devices, swap(): lax.ppermute(x, axis, [(i, i ^ bits) for i in range(lax.axis_size(axis))])  35.8 us
    pallas_call x1, Pallas kernels, logits_and_stats(): pl.pallas_call(body, out_shape=[jax.ShapeDtypeStruct((tokens, vocab_rows)...  7.33 us
    pallas_call x1, Pallas kernels, weight_grad(): pl.pallas_call(body, out_shape=jax.ShapeDtypeStruct((vocab_rows, columns)...  5.83 us
    pallas_call x1, Pallas kernels, logit_grads(): pl.pallas_call(body, out_shape=[jax.ShapeDtypeStruct((vocab_rows, tokens)...  5.13 us
  transfers between devices with their start and end apart: 30, of which 16 were waited for; matrix products, arithmetic and copies ran while one was open for 4% of the time, Pallas kernels for 13%

profile of v2, /device:TPU:0, one launch (start us, length us, event | category | flops | bytes accessed | tf_op | source)
XLA Modules:
  0.0 110.1 jit_solution(126422991849137205)
XLA Ops:
  0.6 0.0 copy-start
  0.6 0.0 copy-start.1
  0.7 3.1 %collective-permute-start = (bf16[32,4096]{1,0:T(8,128)(2,1)}, bf16[32,4096]{1,0:T(8,128)(2,1)S(1)}, u32[]{:S(2)}, u32[]{:S(2)}) collective-permute-start(bf16[32,4096]{1,0:T(8,128)(2,1)} %param.4), channel_id=1, source_target_pairs={{0,2},{1,3},{2,0},{3,1},{4,6},{5,7},{6,4},{7,5},{8,10},{9,11},{10,... | collective-permute-start | bytes 786440 | tf_op jit(solution)/shard_map/ppermute | solution.py:64
  3.7 2.6 %collective-permute-start.1 = (bf16[32,4096]{1,0:T(8,128)(2,1)}, bf16[32,4096]{1,0:T(8,128)(2,1)S(1)}, u32[]{:S(2)}, u32[]{:S(2)}) collective-permute-start(bf16[32,4096]{1,0:T(8,128)(2,1)} %param.4), channel_id=1, source_target_pairs={{0,4},{1,5},{2,6},{3,7},{4,0},{5,1},{6,2},{7,3},{8,12},{9,13},{10,... | collective-permute-start | bytes 786440 | tf_op jit(solution)/shard_map/ppermute | solution.py:64
  6.3 1.0 constant_dynamic-update-slice_fusion.3
  7.4 0.1 stack.65
  7.5 0.1 iota_add_fusion
  7.6 0.1 add.100
  7.6 0.7 compare_reduce_fusion.1
  8.3 10.0 %collective-permute-done.1 = bf16[32,4096]{1,0:T(8,128)(2,1)S(1)} collective-permute-done((bf16[32,4096]{1,0:T(8,128)(2,1)}, bf16[32,4096]{1,0:T(8,128)(2,1)S(1)}, u32[]{:S(2)}, u32[]{:S(2)}) %collective-permute-start.1) | collective-permute-done | bytes 262176 | tf_op jit(solution)/shard_map/ppermute | solution.py:64
  18.3 0.4 collective-permute-start.2
  18.7 1.1 %constant_dynamic-slice_fusion = (bf16[64,1024]{1,0:T(8,128)(2,1)S(1)}, bf16[64,1024]{1,0:T(8,128)(2,1)S(1)}, bf16[64,1024]{1,0:T(8,128)(2,1)S(1)}, bf16[64,1024]{1,0:T(8,128)(2,1)S(1)}) fusion(bf16[256,1024]{1,0:T(8,128)(2,1)} %param.6, s32[]{:T(128)S(6)} %select_n.70, s32[]{:T(128)S(6)} %select_n.69, s32[]{:T(128)S(6)} %select_n.68, s32[]{:T(128)S(6)} %select_n.67), kind=kLoop, calls=%fused_computation.24 | loop fusion | bytes 1048592 | tf_op jit(solution)/shard_map/dynamic_slice | solution.py:374
  19.9 2.2 %collective-permute-start.6 = (bf16[64,1024]{1,0:T(8,128)(2,1)S(1)}, bf16[64,1024]{1,0:T(8,128)(2,1)S(1)}, u32[]{:S(2)}, u32[]{:S(2)}) collective-permute-start(bf16[64,1024]{1,0:T(8,128)(2,1)S(1)} %get-tuple-element.58), channel_id=1, source_target_pairs={{0,6},{1,7},{2,4},{3,5},{4,2},{5,3},{6,0},{7,1},{8,14},{9,15},{10,... | collective-permute-start | bytes 393224 | tf_op jit(solution)/shard_map/ppermute | solution.py:64
  22.1 4.0 %collective-permute-done.2 = bf16[32,4096]{1,0:T(8,128)(2,1)S(1)} collective-permute-done((bf16[32,4096]{1,0:T(8,128)(2,1)S(1)}, bf16[32,4096]{1,0:T(8,128)(2,1)S(1)}, u32[]{:S(2)}, u32[]{:S(2)}) %collective-permute-start.2) | collective-permute-done | bytes 262176 | tf_op jit(solution)/shard_map/ppermute | solution.py:64
  26.1 0.1 collective-permute-start.3
  26.2 0.1 convert_reduce_fusion
  26.3 1.2 %collective-permute-start.4 = (bf16[64,1024]{1,0:T(8,128)(2,1)S(1)}, bf16[64,1024]{1,0:T(8,128)(2,1)S(1)}, u32[]{:S(2)}, u32[]{:S(2)}) collective-permute-start(bf16[64,1024]{1,0:T(8,128)(2,1)S(1)} %get-tuple-element.60), channel_id=1, source_target_pairs={{0,2},{1,3},{2,0},{3,1},{4,6},{5,7},{6,4},{7,5},{8,10},{9,11},{10,... | collective-permute-start | bytes 393224 | tf_op jit(solution)/shard_map/ppermute | solution.py:64
  27.6 1.9 %collective-permute-start.5 = (bf16[64,1024]{1,0:T(8,128)(2,1)S(1)}, bf16[64,1024]{1,0:T(8,128)(2,1)S(1)}, u32[]{:S(2)}, u32[]{:S(2)}) collective-permute-start(bf16[64,1024]{1,0:T(8,128)(2,1)S(1)} %get-tuple-element.59), channel_id=1, source_target_pairs={{0,4},{1,5},{2,6},{3,7},{4,0},{5,1},{6,2},{7,3},{8,12},{9,13},{10,... | collective-permute-start | bytes 393224 | tf_op jit(solution)/shard_map/ppermute | solution.py:64
  29.6 0.0 collective-permute-done.6.refs_3_
  29.6 7.4 %collective-permute-done.5.refs_2_ = bf16[64,1024]{1,0:T(8,128)(2,1)S(1)} collective-permute-done((bf16[64,1024]{1,0:T(8,128)(2,1)S(1)}, bf16[64,1024]{1,0:T(8,128)(2,1)S(1)}, u32[]{:S(2)}, u32[]{:S(2)}) %collective-permute-start.5) | collective-permute-done | bytes 131104 | tf_op jit(solution)/shard_map/ppermute | solution.py:64
  37.0 0.0 collective-permute-done.4.refs_1_
  37.0 0.1 collective-permute-start.7
  37.1 0.2 compare_reduce_fusion
  37.3 1.3 %collective-permute-done.7.refs_4_ = bf16[4,32,1024]{2,1,0:T(8,128)(2,1)S(1)} collective-permute-done((bf16[4,32,1024]{2,1,0:T(8,128)(2,1)S(1)}, bf16[4,32,1024]{2,1,0:T(8,128)(2,1)S(1)}, u32[]{:S(2)}, u32[]{:S(2)}) %collective-permute-start.7) | collective-permute-done | bytes 262176 | tf_op jit(solution)/shard_map/ppermute | solution.py:64
  38.6 1.0 shard_map.60
  39.7 0.1 collective-permute-start.8
  39.8 2.3 %collective-permute-start.9 = (bf16[64,1024]{1,0:T(8,128)(2,1)S(1)}, bf16[64,1024]{1,0:T(8,128)(2,1)S(1)}, u32[]{:S(2)}, u32[]{:S(2)}) collective-permute-start(bf16[64,1024]{1,0:T(8,128)(2,1)S(1)} %get-tuple-element.38), channel_id=1, source_target_pairs={{0,4},{1,5},{2,6},{3,7},{4,0},{5,1},{6,2},{7,3},{8,12},{9,13},{10,... | collective-permute-start | bytes 393224 | tf_op jit(solution)/shard_map/ppermute | solution.py:64
  42.0 2.1 %collective-permute-start.10 = (bf16[64,1024]{1,0:T(8,128)(2,1)S(1)}, bf16[64,1024]{1,0:T(8,128)(2,1)S(1)}, u32[]{:S(2)}, u32[]{:S(2)}) collective-permute-start(bf16[64,1024]{1,0:T(8,128)(2,1)S(1)} %get-tuple-element.39), channel_id=1, source_target_pairs={{0,6},{1,7},{2,4},{3,5},{4,2},{5,3},{6,0},{7,1},{8,14},{9,15},{10,... | collective-permute-start | bytes 393224 | tf_op jit(solution)/shard_map/ppermute | solution.py:64
  44.1 7.3 %shard_map.59 = (f32[256,1024]{1,0:T(8,128)S(1)}, f32[8,256]{1,0:T(8,128)S(1)}, bf16[128,1024]{1,0:T(8,128)(2,1)S(1)}, bf16[128,1024]{1,0:T(8,128)(2,1)S(1)}, bf...) custom-call(bf16[128,4096]{1,0:T(8,128)(2,1)S(1)} %constant_dynamic-update-slice_fusion.refs_0_, ...), custom_call_target="tpu_custom_call" | custom-call | flops 2147483648 | bytes 10486272 | tf_op jit(solution)/shard_map/pallas_call | solution.py:177
  51.5 1.2 %collective-permute-done.9.refs_4_ = bf16[64,1024]{1,0:T(8,128)(2,1)S(1)} collective-permute-done((bf16[64,1024]{1,0:T(8,128)(2,1)S(1)}, bf16[64,1024]{1,0:T(8,128)(2,1)S(1)}, u32[]{:S(2)}, u32[]{:S(2)}) %collective-permute-start.9) | collective-permute-done | bytes 131104 | tf_op jit(solution)/shard_map/ppermute | solution.py:64
  52.7 0.0 collective-permute-done.10.refs_5_
  52.7 0.0 collective-permute-start.11
  52.8 0.6 collective-permute-start.14
  53.4 0.5 collective-permute-done.11.b_ref
  53.9 1.6 %collective-permute-start.15 = (bf16[128,1024]{1,0:T(8,128)(2,1)S(1)}, bf16[128,1024]{1,0:T(8,128)(2,1)S(1)}, u32[]{:S(2)}, u32[]{:S(2)}) collective-permute-start(bf16[128,1024]{1,0:T(8,128)(2,1)S(1)} %get-tuple-element.48), channel_id=1, source_target_pairs={{0,8},{8,0},{16,24},{24,16},{1,9},{9,1},{17,25},{25,17},{2,10},{10... | collective-permute-start | bytes 786440 | tf_op jit(solution)/shard_map/ppermute | solution.py:64
  55.5 1.5 %collective-permute-start.16 = (bf16[128,1024]{1,0:T(8,128)(2,1)S(1)}, bf16[128,1024]{1,0:T(8,128)(2,1)S(1)}, u32[]{:S(2)}, u32[]{:S(2)}) collective-permute-start(bf16[128,1024]{1,0:T(8,128)(2,1)S(1)} %get-tuple-element.49), channel_id=1, source_target_pairs={{0,16},{8,24},{16,0},{24,8},{1,17},{9,25},{17,1},{25,9},{2,18},{10... | collective-permute-start | bytes 786440 | tf_op jit(solution)/shard_map/ppermute | solution.py:64
  57.0 0.5 collective-permute-start.17
  57.5 2.6 %collective-permute-start.12 = (f32[8,256]{1,0:T(8,128)S(1)}, f32[8,256]{1,0:T(8,128)S(1)}, u32[]{:S(2)}, u32[]{:S(2)}) collective-permute-start(f32[8,256]{1,0:T(8,128)S(1)} %shard_map.61.a_ref), channel_id=1, source_target_pairs={{0,2},{1,3},{2,0},{3,1},{4,6},{5,7},{6,4},{7,5},{8,10},{9,11},{10,... | collective-permute-start | bytes 24584 | tf_op jit(solution)/shard_map/ppermute | solution.py:64
  60.0 1.6 %collective-permute-done.12.b_ref = f32[8,256]{1,0:T(8,128)S(1)} collective-permute-done((f32[8,256]{1,0:T(8,128)S(1)}, f32[8,256]{1,0:T(8,128)S(1)}, u32[]{:S(2)}, u32[]{:S(2)}) %collective-permute-start.12) | collective-permute-done | bytes 8224 | tf_op jit(solution)/shard_map/ppermute | solution.py:64
  61.7 2.4 %collective-permute-start.13 = (f32[8,256]{1,0:T(8,128)S(1)}, f32[8,256]{1,0:T(8,128)S(1)}, u32[]{:S(2)}, u32[]{:S(2)}) collective-permute-start(f32[8,256]{1,0:T(8,128)S(1)} %shard_map.62.refs_0_), channel_id=1, source_target_pairs={{0,4},{1,5},{2,6},{3,7},{4,0},{5,1},{6,2},{7,3},{8,12},{9,13},{10,... | collective-permute-start | bytes 24584 | tf_op jit(solution)/shard_map/ppermute | solution.py:64
  64.1 2.3 %collective-permute-done.13.refs_1_ = f32[8,256]{1,0:T(8,128)S(1)} collective-permute-done((f32[8,256]{1,0:T(8,128)S(1)}, f32[8,256]{1,0:T(8,128)S(1)}, u32[]{:S(2)}, u32[]{:S(2)}) %collective-permute-start.13) | collective-permute-done | bytes 8224 | tf_op jit(solution)/shard_map/ppermute | solution.py:64
  66.3 0.0 collective-permute-done.14.refs_6_
  66.3 0.0 collective-permute-done.15.refs_9_.refs_6_
  66.3 2.9 %collective-permute-done.16.refs_10_.refs_7_ = bf16[128,1024]{1,0:T(8,128)(2,1)S(1)} collective-permute-done((bf16[128,1024]{1,0:T(8,128)(2,1)S(1)}, bf16[128,1024]{1,0:T(8,128)(2,1)S(1)}, u32[]{:S(2)}, u32[]{:S(2)}) %collective-permute-start.16) | collective-permute-done | bytes 262176 | tf_op jit(solution)/shard_map/ppermute | solution.py:64
  69.2 5.1 %shard_map.63 = (bf16[1024,256]{1,0:T(8,128)(2,1)S(1)}, f32[128,4096]{1,0:T(8,128)S(1)}, bf16[128,4096]{1,0:T(8,128)(2,1)S(1)}) custom-call(f32[256,1024]{1,0:T(8,128)S(1)} %get-tuple-element.29.logits_ref, f32[8,256]{1,0:T(8,128)S(1)} %shard_map.62.refs_0_, f32[8,256]{1,0:T(8,128)S(1)} %collective-permute-done.13.refs_1_, ...), custom_call_target="tpu_custom_call" | custom-call | flops 2147483648 | bytes 9707520 | tf_op jit(solution)/shard_map/pallas_call | solution.py:295
  74.3 0.1 collective-permute-start.18
  74.4 0.5 collective-permute-start.26
  74.9 1.2 %collective-permute-start.22 = (bf16[1024,256]{1,0:T(8,128)(2,1)S(1)}, bf16[1024,256]{1,0:T(8,128)(2,1)S(1)}, u32[]{:S(2)}, u32[]{:S(2)}) collective-permute-start(bf16[1024,256]{1,0:T(8,128)(2,1)S(1)} %get-tuple-element.53.refs_0_), channel_id=1, source_target_pairs={{0,8},{8,0},{16,24},{24,16},{1,9},{9,1},{17,25},{25,17},{2,10},{10... | collective-permute-start | bytes 1572872 | tf_op jit(solution)/shard_map/ppermute | solution.py:64
  76.1 0.8 collective-permute-start.23
  77.0 0.1 collective-permute-done.18
  77.1 0.3 fusion.8
  77.4 2.6 %collective-permute-start.20 = (bf16[32,4096]{1,0:T(8,128)(2,1)S(1)}, bf16[32,4096]{1,0:T(8,128)(2,1)S(1)}, u32[]{:S(2)}, u32[]{:S(2)}) collective-permute-start(bf16[32,4096]{1,0:T(8,128)(2,1)S(1)} %get-tuple-element.57), channel_id=1, source_target_pairs={{0,2},{1,3},{2,0},{3,1},{4,6},{5,7},{6,4},{7,5},{8,10},{9,11},{10,... | collective-permute-start | bytes 786440 | tf_op jit(solution)/shard_map/ppermute | solution.py:64
  80.0 8.8 %collective-permute-done.22.refs_1_ = bf16[1024,256]{1,0:T(8,128)(2,1)S(1)} collective-permute-done((bf16[1024,256]{1,0:T(8,128)(2,1)S(1)}, bf16[1024,256]{1,0:T(8,128)(2,1)S(1)}, u32[]{:S(2)}, u32[]{:S(2)}) %collective-permute-start.22) | collective-permute-done | bytes 524320 | tf_op jit(solution)/shard_map/ppermute | solution.py:64
  88.8 0.9 collective-permute-done.23.refs_2_
  89.8 1.2 %collective-permute-start.24 = (bf16[512,256]{1,0:T(8,128)(2,1)S(1)}, bf16[512,256]{1,0:T(8,128)(2,1)S(1)}, u32[]{:S(2)}, u32[]{:S(2)}) collective-permute-start(bf16[512,256]{1,0:T(8,128)(2,1)S(1)} %slice.30), channel_id=1, source_target_pairs={{0,16},{8,24},{16,0},{24,8},{1,17},{9,25},{17,1},{25,9},{2,18},{10... | collective-permute-start | bytes 786440 | tf_op jit(solution)/shard_map/ppermute | solution.py:64
  91.0 1.1 %collective-permute-start.25 = (bf16[512,256]{1,0:T(8,128)(2,1)S(1)}, bf16[512,256]{1,0:T(8,128)(2,1)S(1)}, u32[]{:S(2)}, u32[]{:S(2)}) collective-permute-start(bf16[512,256]{1,0:T(8,128)(2,1)S(1)} %slice.31), channel_id=1, source_target_pairs={{0,8},{8,0},{16,24},{24,16},{1,9},{9,1},{17,25},{25,17},{2,10},{10... | collective-permute-start | bytes 786440 | tf_op jit(solution)/shard_map/ppermute | solution.py:64
  92.2 2.6 %collective-permute-start.19 = (bf16[32,4096]{1,0:T(8,128)(2,1)S(1)}, bf16[32,4096]{1,0:T(8,128)(2,1)S(1)}, u32[]{:S(2)}, u32[]{:S(2)}) collective-permute-start(bf16[32,4096]{1,0:T(8,128)(2,1)S(1)} %get-tuple-element.56), channel_id=1, source_target_pairs={{0,2},{1,3},{2,0},{3,1},{4,6},{5,7},{6,4},{7,5},{8,10},{9,11},{10,... | collective-permute-start | bytes 786440 | tf_op jit(solution)/shard_map/ppermute | solution.py:64
  94.9 0.4 collective-permute-start.21
  95.2 3.3 %collective-permute-done.24.refs_3_ = bf16[512,256]{1,0:T(8,128)(2,1)S(1)} collective-permute-done((bf16[512,256]{1,0:T(8,128)(2,1)S(1)}, bf16[512,256]{1,0:T(8,128)(2,1)S(1)}, u32[]{:S(2)}, u32[]{:S(2)}) %collective-permute-start.24) | collective-permute-done | bytes 262176 | tf_op jit(solution)/shard_map/ppermute | solution.py:64
  98.6 0.5 collective-permute-done.25.refs_4_
  99.1 5.8 %shard_map.64 = bf16[1024,1024]{1,0:T(8,128)(2,1)} custom-call(bf16[1024,256]{1,0:T(8,128)(2,1)S(1)} %get-tuple-element.53.refs_0_, bf16[1024,256]{1,0:T(8,128)(2,1)S(1)} %collective-permute-done.22.refs_1_, bf16[1024,256]{1,0:T(8,128)(2,1)S(1)} %collective-permute-done.23.refs_2_, bf16[512,256]{1,0:T(8,128)(2,1)S(1)} %collective-permute-done.24.refs_3_, ...), custom_call_target="tpu_custom_call" | custom-call | flops 2147483648 | bytes 4194304 | tf_op jit(solution)/shard_map/pallas_call | solution.py:338
  105.0 1.1 collective-permute-done.19
  106.1 3.3 %collective-permute-done.21 = bf16[32,4096]{1,0:T(8,128)(2,1)S(1)} collective-permute-done((bf16[32,4096]{1,0:T(8,128)(2,1)S(1)}, bf16[32,4096]{1,0:T(8,128)(2,1)S(1)}, u32[]{:S(2)}, u32[]{:S(2)}) %collective-permute-start.21) | collective-permute-done | bytes 262176 | tf_op jit(solution)/shard_map/ppermute | solution.py:64
  109.3 0.8 fusion.2
  (35 shorter events, 0.4 us)
Async XLA Ops:
  0.6 6.9 %copy-start = (s32[2,64]{1,0:T(2,128)S(1)}, s32[2,64]{1,0:T(2,128)}, u32[]{:S(2)}) copy-start(s32[2,64]{1,0:T(2,128)} %param.7) | copy-start | bytes 1540
  0.6 25.5 %copy-start.1 = (bf16[256,1024]{1,0:T(8,128)(2,1)S(1)}, bf16[256,1024]{1,0:T(8,128)(2,1)}, u32[]{:S(2)}) copy-start(bf16[256,1024]{1,0:T(8,128)(2,1)} %param.6) | copy-start | bytes 1572868
  0.7 21.4 %collective-permute-start = (bf16[32,4096]{1,0:T(8,128)(2,1)}, bf16[32,4096]{1,0:T(8,128)(2,1)S(1)}, u32[]{:S(2)}, u32[]{:S(2)}) collective-permute-start(bf16[32,4096]{1,0:T(8,128)(2,1)} %param.4), channel_id=1, source_target_pairs={{0,2},{1,3},{2,0},{3,1},{4,6},{5,7},{6,4},{7,5},{8,10},{9,11},{10,... | collective-permute-start | bytes 786440 | tf_op jit(solution)/shard_map/ppermute | solution.py:64
  3.7 14.6 %collective-permute-start.1 = (bf16[32,4096]{1,0:T(8,128)(2,1)}, bf16[32,4096]{1,0:T(8,128)(2,1)S(1)}, u32[]{:S(2)}, u32[]{:S(2)}) collective-permute-start(bf16[32,4096]{1,0:T(8,128)(2,1)} %param.4), channel_id=1, source_target_pairs={{0,4},{1,5},{2,6},{3,7},{4,0},{5,1},{6,2},{7,3},{8,12},{9,13},{10,... | collective-permute-start | bytes 786440 | tf_op jit(solution)/shard_map/ppermute | solution.py:64
  18.3 7.8 %collective-permute-start.2 = (bf16[32,4096]{1,0:T(8,128)(2,1)S(1)}, bf16[32,4096]{1,0:T(8,128)(2,1)S(1)}, u32[]{:S(2)}, u32[]{:S(2)}) collective-permute-start(bf16[32,4096]{1,0:T(8,128)(2,1)S(1)} %collective-permute-done.1), channel_id=1, source_target_pairs={{0,2},{1,3},{2,0},{3,1},{4,6},{5,7},{6,4},{7,5},{8,10},{9,11},{10,... | collective-permute-start | bytes 786440 | tf_op jit(solution)/shard_map/ppermute | solution.py:64
  19.9 9.7 %collective-permute-start.6 = (bf16[64,1024]{1,0:T(8,128)(2,1)S(1)}, bf16[64,1024]{1,0:T(8,128)(2,1)S(1)}, u32[]{:S(2)}, u32[]{:S(2)}) collective-permute-start(bf16[64,1024]{1,0:T(8,128)(2,1)S(1)} %get-tuple-element.58), channel_id=1, source_target_pairs={{0,6},{1,7},{2,4},{3,5},{4,2},{5,3},{6,0},{7,1},{8,14},{9,15},{10,... | collective-permute-start | bytes 393224 | tf_op jit(solution)/shard_map/ppermute | solution.py:64
  26.1 18.0 %collective-permute-start.3 = (bf16[128,4096]{1,0:T(8,128)(2,1)S(1)}, bf16[128,4096]{1,0:T(8,128)(2,1)S(1)}, u32[]{:S(2)}, u32[]{:S(2)}) collective-permute-start(bf16[128,4096]{1,0:T(8,128)(2,1)S(1)} %constant_dynamic-update-slice_fusion.refs_0_), channel_id=1, source_target_pairs={{0,1},{1,0},{2,3},{3,2},{4,5},{5,4},{6,7},{7,6},{8,9},{9,8},{10,11... | collective-permute-start | bytes 3145736 | tf_op jit(solution)/shard_map/ppermute | solution.py:64
  26.3 10.6 %collective-permute-start.4 = (bf16[64,1024]{1,0:T(8,128)(2,1)S(1)}, bf16[64,1024]{1,0:T(8,128)(2,1)S(1)}, u32[]{:S(2)}, u32[]{:S(2)}) collective-permute-start(bf16[64,1024]{1,0:T(8,128)(2,1)S(1)} %get-tuple-element.60), channel_id=1, source_target_pairs={{0,2},{1,3},{2,0},{3,1},{4,6},{5,7},{6,4},{7,5},{8,10},{9,11},{10,... | collective-permute-start | bytes 393224 | tf_op jit(solution)/shard_map/ppermute | solution.py:64
  27.6 9.4 %collective-permute-start.5 = (bf16[64,1024]{1,0:T(8,128)(2,1)S(1)}, bf16[64,1024]{1,0:T(8,128)(2,1)S(1)}, u32[]{:S(2)}, u32[]{:S(2)}) collective-permute-start(bf16[64,1024]{1,0:T(8,128)(2,1)S(1)} %get-tuple-element.59), channel_id=1, source_target_pairs={{0,4},{1,5},{2,6},{3,7},{4,0},{5,1},{6,2},{7,3},{8,12},{9,13},{10,... | collective-permute-start | bytes 393224 | tf_op jit(solution)/shard_map/ppermute | solution.py:64
  37.0 1.6 %collective-permute-start.7 = (bf16[4,32,1024]{2,1,0:T(8,128)(2,1)S(1)}, bf16[4,32,1024]{2,1,0:T(8,128)(2,1)S(1)}, u32[]{:S(2)}, u32[]{:S(2)}) collective-permute-start(bf16[4,32,1024]{2,1,0:T(8,128)(2,1)S(1)} %pad_maximum_fusion), channel_id=1, source_target_pairs={{0,1},{1,0},{2,3},{3,2},{4,5},{5,4},{6,7},{7,6},{8,9},{9,8},{10,11... | collective-permute-start | bytes 786440 | tf_op jit(solution)/shard_map/ppermute | solution.py:64
  39.7 11.8 %collective-permute-start.8 = (bf16[64,1024]{1,0:T(8,128)(2,1)S(1)}, bf16[64,1024]{1,0:T(8,128)(2,1)S(1)}, u32[]{:S(2)}, u32[]{:S(2)}) collective-permute-start(bf16[64,1024]{1,0:T(8,128)(2,1)S(1)} %get-tuple-element.37), channel_id=1, source_target_pairs={{0,2},{1,3},{2,0},{3,1},{4,6},{5,7},{6,4},{7,5},{8,10},{9,11},{10,... | collective-permute-start | bytes 393224 | tf_op jit(solution)/shard_map/ppermute | solution.py:64
  39.8 13.0 %collective-permute-start.9 = (bf16[64,1024]{1,0:T(8,128)(2,1)S(1)}, bf16[64,1024]{1,0:T(8,128)(2,1)S(1)}, u32[]{:S(2)}, u32[]{:S(2)}) collective-permute-start(bf16[64,1024]{1,0:T(8,128)(2,1)S(1)} %get-tuple-element.38), channel_id=1, source_target_pairs={{0,4},{1,5},{2,6},{3,7},{4,0},{5,1},{6,2},{7,3},{8,12},{9,13},{10,... | collective-permute-start | bytes 393224 | tf_op jit(solution)/shard_map/ppermute | solution.py:64
  42.0 10.7 %collective-permute-start.10 = (bf16[64,1024]{1,0:T(8,128)(2,1)S(1)}, bf16[64,1024]{1,0:T(8,128)(2,1)S(1)}, u32[]{:S(2)}, u32[]{:S(2)}) collective-permute-start(bf16[64,1024]{1,0:T(8,128)(2,1)S(1)} %get-tuple-element.39), channel_id=1, source_target_pairs={{0,6},{1,7},{2,4},{3,5},{4,2},{5,3},{6,0},{7,1},{8,14},{9,15},{10,... | collective-permute-start | bytes 393224 | tf_op jit(solution)/shard_map/ppermute | solution.py:64
  52.7 1.2 %collective-permute-start.11 = (f32[8,256]{1,0:T(8,128)S(1)}, f32[8,256]{1,0:T(8,128)S(1)}, u32[]{:S(2)}, u32[]{:S(2)}) collective-permute-start(f32[8,256]{1,0:T(8,128)S(1)} %get-tuple-element.41.a_ref), channel_id=1, source_target_pairs={{0,1},{1,0},{2,3},{3,2},{4,5},{5,4},{6,7},{7,6},{8,9},{9,8},{10,11... | collective-permute-start | bytes 24584 | tf_op jit(solution)/shard_map/ppermute | solution.py:64
  52.8 13.5 %collective-permute-start.14 = (bf16[4,32,1024]{2,1,0:T(8,128)(2,1)S(1)}, bf16[4,32,1024]{2,1,0:T(8,128)(2,1)S(1)}, u32[]{:S(2)}, u32[]{:S(2)}) collective-permute-start(bf16[4,32,1024]{2,1,0:T(8,128)(2,1)S(1)} %pad_maximum_fusion.1), channel_id=1, source_target_pairs={{0,1},{1,0},{2,3},{3,2},{4,5},{5,4},{6,7},{7,6},{8,9},{9,8},{10,11... | collective-permute-start | bytes 786440 | tf_op jit(solution)/shard_map/ppermute | solution.py:64
  53.9 12.4 %collective-permute-start.15 = (bf16[128,1024]{1,0:T(8,128)(2,1)S(1)}, bf16[128,1024]{1,0:T(8,128)(2,1)S(1)}, u32[]{:S(2)}, u32[]{:S(2)}) collective-permute-start(bf16[128,1024]{1,0:T(8,128)(2,1)S(1)} %get-tuple-element.48), channel_id=1, source_target_pairs={{0,8},{8,0},{16,24},{24,16},{1,9},{9,1},{17,25},{25,17},{2,10},{10... | collective-permute-start | bytes 786440 | tf_op jit(solution)/shard_map/ppermute | solution.py:64
  55.5 13.7 %collective-permute-start.16 = (bf16[128,1024]{1,0:T(8,128)(2,1)S(1)}, bf16[128,1024]{1,0:T(8,128)(2,1)S(1)}, u32[]{:S(2)}, u32[]{:S(2)}) collective-permute-start(bf16[128,1024]{1,0:T(8,128)(2,1)S(1)} %get-tuple-element.49), channel_id=1, source_target_pairs={{0,16},{8,24},{16,0},{24,8},{1,17},{9,25},{17,1},{25,9},{2,18},{10... | collective-permute-start | bytes 786440 | tf_op jit(solution)/shard_map/ppermute | solution.py:64
  57.0 12.2 %collective-permute-start.17 = (bf16[128,1024]{1,0:T(8,128)(2,1)S(1)}, bf16[128,1024]{1,0:T(8,128)(2,1)S(1)}, u32[]{:S(2)}, u32[]{:S(2)}) collective-permute-start(bf16[128,1024]{1,0:T(8,128)(2,1)S(1)} %get-tuple-element.50), channel_id=1, source_target_pairs={{0,24},{8,16},{16,8},{24,0},{1,25},{9,17},{17,9},{25,1},{2,26},{10... | collective-permute-start | bytes 786440 | tf_op jit(solution)/shard_map/ppermute | solution.py:64
  57.5 4.2 %collective-permute-start.12 = (f32[8,256]{1,0:T(8,128)S(1)}, f32[8,256]{1,0:T(8,128)S(1)}, u32[]{:S(2)}, u32[]{:S(2)}) collective-permute-start(f32[8,256]{1,0:T(8,128)S(1)} %shard_map.61.a_ref), channel_id=1, source_target_pairs={{0,2},{1,3},{2,0},{3,1},{4,6},{5,7},{6,4},{7,5},{8,10},{9,11},{10,... | collective-permute-start | bytes 24584 | tf_op jit(solution)/shard_map/ppermute | solution.py:64
  61.7 4.6 %collective-permute-start.13 = (f32[8,256]{1,0:T(8,128)S(1)}, f32[8,256]{1,0:T(8,128)S(1)}, u32[]{:S(2)}, u32[]{:S(2)}) collective-permute-start(f32[8,256]{1,0:T(8,128)S(1)} %shard_map.62.refs_0_), channel_id=1, source_target_pairs={{0,4},{1,5},{2,6},{3,7},{4,0},{5,1},{6,2},{7,3},{8,12},{9,13},{10,... | collective-permute-start | bytes 24584 | tf_op jit(solution)/shard_map/ppermute | solution.py:64
  74.3 2.7 %collective-permute-start.18 = (bf16[128,4096]{1,0:T(8,128)(2,1)S(1)}, bf16[128,4096]{1,0:T(8,128)(2,1)S(1)}, u32[]{:S(2)}, u32[]{:S(2)}) collective-permute-start(bf16[128,4096]{1,0:T(8,128)(2,1)S(1)} %get-tuple-element.52), channel_id=1, source_target_pairs={{0,1},{1,0},{2,3},{3,2},{4,5},{5,4},{6,7},{7,6},{8,9},{9,8},{10,11... | collective-permute-start | bytes 3145736 | tf_op jit(solution)/shard_map/ppermute | solution.py:64
  74.4 15.4 %collective-permute-start.26 = (bf16[128,1024]{1,0:T(8,128)(2,1)S(1)}, bf16[128,1024]{1,0:T(8,128)(2,1)S(1)}, u32[]{:S(2)}, u32[]{:S(2)}) collective-permute-start(bf16[128,1024]{1,0:T(8,128)(2,1)S(1)} %get-tuple-element.47.refs_8_.refs_5_), channel_id=1, source_target_pairs={{0,1},{1,0},{2,3},{3,2},{4,5},{5,4},{6,7},{7,6},{8,9},{9,8},{10,11... | collective-permute-start | bytes 786440 | tf_op jit(solution)/shard_map/ppermute | solution.py:64
  74.9 13.9 %collective-permute-start.22 = (bf16[1024,256]{1,0:T(8,128)(2,1)S(1)}, bf16[1024,256]{1,0:T(8,128)(2,1)S(1)}, u32[]{:S(2)}, u32[]{:S(2)}) collective-permute-start(bf16[1024,256]{1,0:T(8,128)(2,1)S(1)} %get-tuple-element.53.refs_0_), channel_id=1, source_target_pairs={{0,8},{8,0},{16,24},{24,16},{1,9},{9,1},{17,25},{25,17},{2,10},{10... | collective-permute-start | bytes 1572872 | tf_op jit(solution)/shard_map/ppermute | solution.py:64
  76.1 13.6 %collective-permute-start.23 = (bf16[1024,256]{1,0:T(8,128)(2,1)S(1)}, bf16[1024,256]{1,0:T(8,128)(2,1)S(1)}, u32[]{:S(2)}, u32[]{:S(2)}) collective-permute-start(bf16[1024,256]{1,0:T(8,128)(2,1)S(1)} %get-tuple-element.53.refs_0_), channel_id=1, source_target_pairs={{0,16},{8,24},{16,0},{24,8},{1,17},{9,25},{17,1},{25,9},{2,18},{10... | collective-permute-start | bytes 1572872 | tf_op jit(solution)/shard_map/ppermute | solution.py:64
  77.4 13.6 %collective-permute-start.20 = (bf16[32,4096]{1,0:T(8,128)(2,1)S(1)}, bf16[32,4096]{1,0:T(8,128)(2,1)S(1)}, u32[]{:S(2)}, u32[]{:S(2)}) collective-permute-start(bf16[32,4096]{1,0:T(8,128)(2,1)S(1)} %get-tuple-element.57), channel_id=1, source_target_pairs={{0,2},{1,3},{2,0},{3,1},{4,6},{5,7},{6,4},{7,5},{8,10},{9,11},{10,... | collective-permute-start | bytes 786440 | tf_op jit(solution)/shard_map/ppermute | solution.py:64
  80.0 12.2 %collective-permute-start.27 = (bf16[128,1024]{1,0:T(8,128)(2,1)S(1)}, bf16[128,1024]{1,0:T(8,128)(2,1)S(1)}, u32[]{:S(2)}, u32[]{:S(2)}) collective-permute-start(bf16[128,1024]{1,0:T(8,128)(2,1)S(1)} %collective-permute-done.15.refs_9_.refs_6_), channel_id=1, source_target_pairs={{0,1},{1,0},{2,3},{3,2},{4,5},{5,4},{6,7},{7,6},{8,9},{9,8},{10,11... | collective-permute-start | bytes 786440 | tf_op jit(solution)/shard_map/ppermute | solution.py:64
  88.8 6.1 %collective-permute-start.28 = (bf16[128,1024]{1,0:T(8,128)(2,1)S(1)}, bf16[128,1024]{1,0:T(8,128)(2,1)S(1)}, u32[]{:S(2)}, u32[]{:S(2)}) collective-permute-start(bf16[128,1024]{1,0:T(8,128)(2,1)S(1)} %collective-permute-done.16.refs_10_.refs_7_), channel_id=1, source_target_pairs={{0,1},{1,0},{2,3},{3,2},{4,5},{5,4},{6,7},{7,6},{8,9},{9,8},{10,11... | collective-permute-start | bytes 786440 | tf_op jit(solution)/shard_map/ppermute | solution.py:64
  89.8 5.5 %collective-permute-start.29 = (bf16[128,1024]{1,0:T(8,128)(2,1)S(1)}, bf16[128,1024]{1,0:T(8,128)(2,1)S(1)}, u32[]{:S(2)}, u32[]{:S(2)}) collective-permute-start(bf16[128,1024]{1,0:T(8,128)(2,1)S(1)} %collective-permute-done.17.refs_11_.refs_8_), channel_id=1, source_target_pairs={{0,1},{1,0},{2,3},{3,2},{4,5},{5,4},{6,7},{7,6},{8,9},{9,8},{10,11... | collective-permute-start | bytes 786440 | tf_op jit(solution)/shard_map/ppermute | solution.py:64
  89.8 8.8 %collective-permute-start.24 = (bf16[512,256]{1,0:T(8,128)(2,1)S(1)}, bf16[512,256]{1,0:T(8,128)(2,1)S(1)}, u32[]{:S(2)}, u32[]{:S(2)}) collective-permute-start(bf16[512,256]{1,0:T(8,128)(2,1)S(1)} %slice.30), channel_id=1, source_target_pairs={{0,16},{8,24},{16,0},{24,8},{1,17},{9,25},{17,1},{25,9},{2,18},{10... | collective-permute-start | bytes 786440 | tf_op jit(solution)/shard_map/ppermute | solution.py:64
  91.0 8.1 %collective-permute-start.25 = (bf16[512,256]{1,0:T(8,128)(2,1)S(1)}, bf16[512,256]{1,0:T(8,128)(2,1)S(1)}, u32[]{:S(2)}, u32[]{:S(2)}) collective-permute-start(bf16[512,256]{1,0:T(8,128)(2,1)S(1)} %slice.31), channel_id=1, source_target_pairs={{0,8},{8,0},{16,24},{24,16},{1,9},{9,1},{17,25},{25,17},{2,10},{10... | collective-permute-start | bytes 786440 | tf_op jit(solution)/shard_map/ppermute | solution.py:64
  92.2 13.8 %collective-permute-start.19 = (bf16[32,4096]{1,0:T(8,128)(2,1)S(1)}, bf16[32,4096]{1,0:T(8,128)(2,1)S(1)}, u32[]{:S(2)}, u32[]{:S(2)}) collective-permute-start(bf16[32,4096]{1,0:T(8,128)(2,1)S(1)} %get-tuple-element.56), channel_id=1, source_target_pairs={{0,2},{1,3},{2,0},{3,1},{4,6},{5,7},{6,4},{7,5},{8,10},{9,11},{10,... | collective-permute-start | bytes 786440 | tf_op jit(solution)/shard_map/ppermute | solution.py:64
  94.9 14.4 %collective-permute-start.21 = (bf16[32,4096]{1,0:T(8,128)(2,1)S(1)}, bf16[32,4096]{1,0:T(8,128)(2,1)S(1)}, u32[]{:S(2)}, u32[]{:S(2)}) collective-permute-start(bf16[32,4096]{1,0:T(8,128)(2,1)S(1)} %fusion), channel_id=1, source_target_pairs={{0,4},{1,5},{2,6},{3,7},{4,0},{5,1},{6,2},{7,3},{8,12},{9,13},{10,... | collective-permute-start | bytes 786440 | tf_op jit(solution)/shard_map/ppermute | solution.py:64

commit v3 on v2

--- a/solution.py
+++ b/solution.py
@@ -106,21 +106,18 @@
     )
 
 
-def logits_and_stats(own, other, rows, weight, mass, quarter, parts=4):
+def logits_and_stats(own, other, rows, weight, mass, parts=8, ahead=4):
     half, width = own.shape
     chips = half // rows
     tokens = 2 * half
     vocab_rows = weight.shape[0]
     step = vocab_rows // parts
-    groups = width // quarter
 
     def body(*refs):
         piece_refs, refs = refs[:2], refs[2:]
         weight_ref, mass_ref, out_ref, stats_ref, refs = *refs[:4], refs[4:]
-        cols_refs, refs = refs[:groups], refs[groups:]
-        held, held_weight, sems, piece_sems, cols_sems = refs
+        held, held_weight, sems, piece_sems = refs
         chip, core = place_on_mesh()
-        data_pos = lax.axis_index("dp")
         loads = []
         for h in range(2):
             for j in range(chips):
@@ -140,38 +137,28 @@
             copies.append(
                 pltpu.make_async_copy(weight_ref.at[some], held_weight.at[some], sems.at[k])
             )
+        for k in range(ahead):
             copies[k].start()
         for load in loads:
             load.wait()
-        stores = []
-        for r in range(groups):
-            column = pl.multiple_of((data_pos ^ r) * quarter, quarter)
-            for j in range(chips):
-                start = ((chip ^ j) * 2 + core) * rows
-                stores.append(
-                    pltpu.make_async_copy(
-                        held.at[pl.ds(pl.multiple_of(start, rows), rows), pl.ds(column, quarter)],
-                        cols_refs[r].at[pl.ds(j * rows, rows)],
-                        cols_sems.at[r, j],
-                    )
-                )
-                stores[-1].start()
         for k in range(parts):
             copies[k].wait()
-            out_ref[:, k * step : (k + 1) * step] = lax.dot_general(
-                held[...],
-                held_weight[k * step : (k + 1) * step],
-                (((1,), (1,)), ((), ())),
-                preferred_element_type=jnp.float32,
-            )
+            if k + ahead < parts:
+                copies[k + ahead].start()
+            if (k + 1) % ahead == 0:
+                some = slice((k + 1 - ahead) * step, (k + 1) * step)
+                out_ref[:, some] = lax.dot_general(
+                    held[...],
+                    held_weight[some],
+                    (((1,), (1,)), ((), ())),
+                    preferred_element_type=jnp.float32,
+                )
         top = jnp.max(out_ref[...], axis=1, keepdims=True)
         total = jnp.sum(jnp.exp(out_ref[...] - top), axis=1, keepdims=True)
         stats_ref[0:1] = as_row(top)
         stats_ref[1:2] = as_row(total)
         stats_ref[2:3] = mass_ref[...]
         stats_ref[3:8] = jnp.zeros((5, tokens), jnp.float32)
-        for store in stores:
-            store.wait()
 
     ops = [own, other, in_hbm(weight), mass]
     return pl.pallas_call(
@@ -179,24 +166,50 @@
         out_shape=[
             jax.ShapeDtypeStruct((tokens, vocab_rows), jnp.float32),
             jax.ShapeDtypeStruct((8, tokens), jnp.float32),
-        ]
-        + [jax.ShapeDtypeStruct((half, quarter), weight.dtype)] * groups,
+        ],
         in_specs=[ANY] * 3 + [WHOLE],
-        out_specs=[WHOLE, WHOLE] + [ANY] * groups,
+        out_specs=[WHOLE, WHOLE],
         scratch_shapes=[
             pltpu.VMEM((tokens, width), weight.dtype),
             pltpu.VMEM(weight.shape, weight.dtype),
             pltpu.SemaphoreType.DMA((parts,)),
             pltpu.SemaphoreType.DMA((2 * chips,)),
-            pltpu.SemaphoreType.DMA((groups, chips)),
         ],
         compiler_params=pltpu.CompilerParams(vmem_limit_bytes=32 * MIB),
         cost_estimate=cost(2 * tokens * weight.size, ops),
     )(*ops)
 
 
-def merge_pair(a, b):
-    def body(a_ref, b_ref, out_ref):
+def cut_columns(own, quarter):
+    groups = own.shape[1] // quarter
+
+    def body(own_ref, *refs):
+        outs, sems = refs[:groups], refs[groups]
+        data_pos = lax.axis_index("dp")
+        moves = []
+        for r in range(groups):
+            column = pl.multiple_of((data_pos ^ r) * quarter, quarter)
+            moves.append(
+                pltpu.make_async_copy(own_ref.at[:, pl.ds(column, quarter)], outs[r], sems.at[r])
+            )
+            moves[r].start()
+        for move in moves:
+            move.wait()
+
+    return pl.pallas_call(
+        body,
+        out_shape=[jax.ShapeDtypeStruct((own.shape[0], quarter), own.dtype)] * groups,
+        in_specs=[ANY],
+        out_specs=[ANY] * groups,
+        scratch_shapes=[pltpu.SemaphoreType.DMA((groups,))],
+        compiler_params=pltpu.CompilerParams(vmem_limit_bytes=MIB),
+        cost_estimate=cost(0, (own,)),
+    )(own)
+
+
+def merge_pair(a, b, after=()):
+    def body(a_ref, b_ref, *refs):
+        out_ref = refs[-1]
         for k, row in enumerate(merge([a_ref[...], b_ref[...]])):
             out_ref[k : k + 1] = row
         out_ref[3:8] = jnp.zeros((5, a.shape[1]), jnp.float32)
@@ -204,11 +217,27 @@
     return pl.pallas_call(
         body,
         out_shape=jax.ShapeDtypeStruct(a.shape, a.dtype),
-        in_specs=[WHOLE, WHOLE],
+        in_specs=[WHOLE, WHOLE] + [ANY] * len(after),
         out_specs=WHOLE,
         compiler_params=pltpu.CompilerParams(vmem_limit_bytes=MIB),
         cost_estimate=cost(0, (a, b)),
-    )(a, b)
+    )(a, b, *after)
+
+
+def siblings_part_after(parts, rows, after):
+    def body(*refs):
+        start = pl.multiple_of((1 - place_on_mesh()[1]) * rows, rows)
+        for j in range(len(parts)):
+            refs[-1][j] = refs[j][pl.ds(start, rows), :]
+
+    return pl.pallas_call(
+        body,
+        out_shape=jax.ShapeDtypeStruct((len(parts), rows, parts[0].shape[1]), parts[0].dtype),
+        in_specs=[WHOLE] * len(parts) + [ANY] * len(after),
+        out_specs=WHOLE,
+        compiler_params=pltpu.CompilerParams(vmem_limit_bytes=4 * MIB),
+        cost_estimate=cost(0, parts),
+    )(*parts, *after)
 
 
 def place_tiles(slots, listed, mine, sibling):
@@ -246,7 +275,7 @@
     )(slots, listed, *mine, sibling)
 
 
-def logit_grads(logits, stats, mine, sibling, weight, after, parts=8):
+def logit_grads(logits, stats, mine, sibling, weight, cols, parts=8):
     chips, rows, vocab_rows = sibling.shape
     tokens = logits.shape[0]
     half = chips * rows
@@ -257,8 +286,13 @@
     def body(logits_ref, *refs):
         stats_refs, refs = refs[:count], refs[count:]
         mine_refs, refs = refs[:chips], refs[chips:]
-        sibling_ref, weight_ref, refs = refs[0], refs[1], refs[2 + len(after) :]
-        out_ref, own_ref, other_ref, held, held_weight, columns, sems = refs
+        sibling_ref, weight_ref, refs = refs[0], refs[1], refs[2:]
+        cols_refs, refs = refs[: len(cols)], refs[len(cols) :]
+        out_ref, own_ref, other_ref, stacked_ref, held_weight, columns, sems, cols_sems = refs
+        moves = [
+            pltpu.make_async_copy(ref, stacked_ref.at[r], cols_sems.at[r])
+            for r, ref in enumerate(cols_refs)
+        ]
         copies = []
         for k in range(parts):
             some = pl.ds(k * step, step)
@@ -268,6 +302,8 @@
                 )
             )
             copies[k].start()
+        for move in moves:
+            move.start()
         top, total, mass = merge([ref[...] for ref in stats_refs])
         columns[:, 0:1] = as_column(top)
         columns[:, 1:2] = as_column(loss_scale * mass / total)
@@ -281,68 +317,62 @@
                 grads = (
                     columns[part, 1:2] * jnp.exp(logits_ref[part, :] - columns[part, 0:1])
                     - loss_scale * tiles.astype(jnp.float32)
-                ).astype(held.dtype)
-                held[(h * chips + j) * rows : (h * chips + j + 1) * rows] = grads
+                ).astype(out_ref.dtype)
+                out_ref[(h * chips + j) * rows : (h * chips + j + 1) * rows] = grads
         for k in range(parts):
             copies[k].wait()
             some = slice(k * step, (k + 1) * step)
-            share = jnp.dot(held[...], held_weight[:, some], preferred_element_type=jnp.float32)
+            share = jnp.dot(out_ref[...], held_weight[:, some], preferred_element_type=jnp.float32)
             own_ref[:, some] = share[:half]
             other_ref[:, some] = share[half:].astype(other_ref.dtype)
-        out_ref[...] = held[...].T
+        for move in moves:
+            move.wait()
 
     ops = (logits, *stats, *mine, sibling, in_hbm(weight))
     return pl.pallas_call(
         body,
         out_shape=[
-            jax.ShapeDtypeStruct((vocab_rows, tokens), jnp.bfloat16),
+            jax.ShapeDtypeStruct((tokens, vocab_rows), jnp.bfloat16),
             jax.ShapeDtypeStruct((half, width), jnp.float32),
             jax.ShapeDtypeStruct((half, width), jnp.bfloat16),
+            jax.ShapeDtypeStruct((len(cols), *cols[0].shape), cols[0].dtype),
         ],
-        in_specs=[WHOLE] * (len(ops) - 1) + [ANY] * (1 + len(after)),
-        out_specs=[WHOLE] * 3,
+        in_specs=[WHOLE] * (len(ops) - 1) + [ANY] * (1 + len(cols)),
+        out_specs=[WHOLE] * 3 + [ANY],
         scratch_shapes=[
-            pltpu.VMEM((tokens, vocab_rows), jnp.bfloat16),
             pltpu.VMEM(weight.shape, weight.dtype),
             pltpu.VMEM((tokens, 128), jnp.float32),
             pltpu.SemaphoreType.DMA((parts,)),
+            pltpu.SemaphoreType.DMA((len(cols),)),
         ],
         compiler_params=pltpu.CompilerParams(vmem_limit_bytes=32 * MIB),
         cost_estimate=cost(2 * weight.size * tokens, ops),
-    )(*ops, *after)
-
-
-def weight_grad(grads, own_cols, other_cols):
-    counts = [len(parts) for parts in grads]
+    )(*ops, *cols)
+
+
+def weight_grad(grads, own_cols, other_cols, after):
     flat = [part for parts in grads for part in parts]
-    groups = len(grads)
-    vocab_rows = sum(part.shape[0] for part in grads[0])
-    half, columns = own_cols[0].shape
+    vocab_rows = flat[0].shape[1]
+    columns = own_cols.shape[2]
+    tokens = sum(part.shape[0] for part in flat)
 
     def body(*refs):
-        own_refs, other_refs = refs[len(flat) : -1][:groups], refs[len(flat) : -1][groups:]
-        out_ref = refs[-1]
-        total = None
-        for r in range(groups):
-            at = sum(counts[:r])
-            parts = [ref[...] for ref in refs[at : at + counts[r]]]
-            rows = jnp.concatenate(parts) if counts[r] > 1 else parts[0]
-            for n, ref in enumerate((own_refs[r], other_refs[r])):
-                term = jnp.dot(
-                    rows[:, n * half : (n + 1) * half], ref[...], preferred_element_type=jnp.float32
-                )
-                total = term if total is None else total + term
-        out_ref[...] = total.astype(out_ref.dtype)
-
-    ops = [*flat, *own_cols, *other_cols]
+        rows = jnp.concatenate([ref[...] for ref in refs[: len(flat)]])
+        cols_refs = refs[len(flat) : len(flat) + 2]
+        cols = jnp.concatenate([ref[r] for r in range(own_cols.shape[0]) for ref in cols_refs])
+        refs[-1][...] = lax.dot_general(
+            rows, cols, (((0,), (0,)), ((), ())), preferred_element_type=jnp.float32
+        ).astype(refs[-1].dtype)
+
+    ops = [*flat, own_cols, other_cols]
     return pl.pallas_call(
         body,
         out_shape=jax.ShapeDtypeStruct((vocab_rows, columns), jnp.bfloat16),
-        in_specs=[WHOLE] * len(ops),
+        in_specs=[WHOLE] * len(ops) + [ANY] * len(after),
         out_specs=WHOLE,
         compiler_params=pltpu.CompilerParams(vmem_limit_bytes=24 * MIB),
-        cost_estimate=cost(2 * groups * vocab_rows * 2 * half * columns, ops),
-    )(*ops)
+        cost_estimate=cost(2 * tokens * vocab_rows * columns, ops),
+    )(*ops, *after)
 
 
 def shards(hidden, weight, teacher, block_ids):
@@ -362,17 +392,17 @@
     def between_chips(parts):
         return [parts[0]] + [swap(parts[r], "vocab", 2 * r) for r in range(1, chips)]
 
-    def between_cores(parts):
+    def siblings_part(parts):
         given = [lax.dynamic_slice_in_dim(part, (1 - core) * rows, rows) for part in parts]
-        return swap(jnp.stack(given), "vocab", 1)
-
-    far, late_teacher = lax.optimization_barrier((far, teacher))
+        return jnp.stack(given)
+
     pieces = pieces + [far] + [swap(far, "vocab", 2 * j) for j in range(1, len(pieces))]
+    got = between_chips(
+        [lax.dynamic_slice_in_dim(teacher, (chip ^ r) * 2 * rows, 2 * rows) for r in range(chips)]
+    )
+    pieces, got = lax.optimization_barrier((pieces, got))
     own = jnp.concatenate(pieces)
     other = swap(own, "vocab", 1)
-    got = between_chips(
-        [lax.dynamic_slice_in_dim(late_teacher, (chip ^ r) * 2 * rows, 2 * rows) for r in range(chips)]
-    )
     my_ids = lax.dynamic_index_in_dim(block_ids, me * rows // BLK, keepdims=False)
     per = teacher.shape[1] // BLK
     owners = jnp.stack([(chip ^ r) * 2 + c for r in range(chips) for c in range(2)])
@@ -382,33 +412,34 @@
     slots = jnp.argmax(match, axis=1).astype(jnp.int32)
     source = slots // per
     place = ((source % 2) ^ core) * chips + ((source // 2) ^ chip)
-    placed = place_tiles(place * per + slots % per, listed, got, between_cores(got))
+    placed = place_tiles(
+        place * per + slots % per, listed, got, swap(siblings_part(got), "vocab", 1)
+    )
     tiles = between_chips(placed)
 
     mass = jnp.sum(teacher, axis=1, dtype=jnp.float32)[None, :]
-    logits, stats, *cols = logits_and_stats(
-        own, other, rows, weight, mass, width // data_size
-    )
-
-    tiles, stats = lax.optimization_barrier((tiles, stats))
+    logits, stats = logits_and_stats(own, other, rows, weight, mass)
+
+    cols = cut_columns(own, width // data_size)
+    own_cols = [cols[0]] + [swap(cols[r], "dp", r) for r in range(1, data_size)]
+
     stats = merge_pair(stats, swap(stats, "vocab", 1))
-    *cols, stats = lax.optimization_barrier((*cols, stats))
-    own_cols = [cols[0]] + [swap(cols[r], "dp", r) for r in range(1, data_size)]
-    other_cols = [swap(x, "vocab", 1) for x in own_cols]
     bits = 2
     while 2 * bits < vocab_size:
         stats = merge_pair(stats, swap(stats, "vocab", bits))
         bits *= 2
     all_stats = [stats, swap(stats, "vocab", bits)]
-    grad_logits, share, rest = logit_grads(
-        logits, all_stats, tiles, between_cores(tiles), weight, own_cols
+    other_tiles = swap(siblings_part_after(tiles, rows, [stats]), "vocab", 1)
+    grad_logits, share, rest, own_cols = logit_grads(
+        logits, all_stats, tiles, other_tiles, weight, own_cols
     )
+    other_cols = swap(own_cols, "vocab", 1)
 
     share = share + swap(rest, "vocab", 1).astype(jnp.float32)
     shares = [share[j * rows : (j + 1) * rows] for j in range(chips)]
     count = 1
     while count < chips:
-        for base in range(0, chips, 2 * count):
+        for base in range(chips - 2 * count, -1, -2 * count):
             sent = swap(shares[base + count].astype(jnp.bfloat16), "vocab", 2 * count)
             shares[base] = shares[base] + sent.astype(jnp.float32)
         count *= 2
@@ -423,7 +454,7 @@
             near, far = known[r], all_grads[bits][0]
             all_grads.append([swap(near[:middle], "dp", bits), swap(far[middle:], "dp", r)])
         bits *= 2
-    grad_weight = weight_grad(all_grads, own_cols, other_cols)
+    grad_weight = weight_grad(all_grads, own_cols, other_cols, [shares[0]])
     return (shares[0].astype(jnp.bfloat16), grad_weight)
 
 

time: 110 us -> 99.8 us (0.907)
  Pallas kernels: 19.4 us -> 15.2 us
  starting transfers between devices: 35.8 us -> 31.6 us
  waiting for transfers between devices: 49.2 us -> 47.2 us
    ppermute x30 -> x27, starting transfers between devices: 35.8 us -> 31.6 us  [swap(): lax.ppermute(x, axis, [(i, i ^ bits) for i in range(lax.axis_size(axis))])]
    pallas_call x1, Pallas kernels: 5.83 us -> 3.69 us  [weight_grad(): pl.pallas_call(body, out_shape=jax.ShapeDtypeStruct((vocab_rows, columns)...]
    ppermute x30 -> x27, waiting for transfers between devices: 49.2 us -> 47.2 us  [swap(): lax.ppermute(x, axis, [(i, i ^ bits) for i in range(lax.axis_size(axis))])]
    pallas_call x1, Pallas kernels: 7.33 us -> 5.45 us  [logits_and_stats(): pl.pallas_call(body, out_shape=[jax.ShapeDtypeStruct((tokens, vocab_rows)...]
    pallas_call x1 -> x3, Pallas kernels: 5.13 us -> 5.01 us  [the longest x1 4.87 us: logit_grads(): pl.pallas_call(body, out_shape=[jax.ShapeDtypeStruct((tokens, vocab_rows)...]
  transfers between devices with their start and end apart: 30 -> 27, of which waited for: 16 -> 14; matrix products, arithmetic and copies ran while one was open for 4% -> 3% of each run, Pallas kernels for 13% -> 7%
where the time goes in v3:
time: 99.8 us; the launch traced here: 99.6 us
  waiting for transfers between devices  47.2 us (47%)
  starting transfers between devices  31.6 us (32%)
  Pallas kernels  15.2 us (15%)
  local copies, waits for them, and re-layouts  2.44 us (2%)
  other arithmetic  2.31 us (2%)
    ppermute x27, waiting for transfers between devices, swap(): lax.ppermute(x, axis, [(i, i ^ bits) for i in range(lax.axis_size(axis))])  47.2 us
    ppermute x27, starting transfers between devices, swap(): lax.ppermute(x, axis, [(i, i ^ bits) for i in range(lax.axis_size(axis))])  31.6 us
    pallas_call x1, Pallas kernels, logits_and_stats(): pl.pallas_call(body, out_shape=[jax.ShapeDtypeStruct((tokens, vocab_rows)...  5.45 us
    pallas_call x1, Pallas kernels, logit_grads(): pl.pallas_call(body, out_shape=[jax.ShapeDtypeStruct((tokens, vocab_rows)...  4.87 us
    pallas_call x1, Pallas kernels, weight_grad(): pl.pallas_call(body, out_shape=jax.ShapeDtypeStruct((vocab_rows, columns)...  3.69 us
  transfers between devices with their start and end apart: 27, of which 14 were waited for; matrix products, arithmetic and copies ran while one was open for 3% of the time, Pallas kernels for 7%

profile of v3, /device:TPU:0, one launch (start us, length us, event | category | flops | bytes accessed | tf_op | source)
XLA Modules:
  0.0 99.6 jit_solution(9289636624521487418)
XLA Ops:
  0.6 0.0 copy-start
  0.7 4.1 %collective-permute-start.1 = (bf16[32,4096]{1,0:T(8,128)(2,1)}, bf16[32,4096]{1,0:T(8,128)(2,1)S(1)}, u32[]{:S(2)}, u32[]{:S(2)}) collective-permute-start(bf16[32,4096]{1,0:T(8,128)(2,1)} %param.4), channel_id=1, source_target_pairs={{0,4},{1,5},{2,6},{3,7},{4,0},{5,1},{6,2},{7,3},{8,12},{9,13},{10,... | collective-permute-start | bytes 786440 | tf_op jit(solution)/shard_map/ppermute | solution.py:64
  4.8 1.6 %collective-permute-start = (bf16[32,4096]{1,0:T(8,128)(2,1)}, bf16[32,4096]{1,0:T(8,128)(2,1)S(1)}, u32[]{:S(2)}, u32[]{:S(2)}) collective-permute-start(bf16[32,4096]{1,0:T(8,128)(2,1)} %param.4), channel_id=1, source_target_pairs={{0,2},{1,3},{2,0},{3,1},{4,6},{5,7},{6,4},{7,5},{8,10},{9,11},{10,... | collective-permute-start | bytes 786440 | tf_op jit(solution)/shard_map/ppermute | solution.py:64
  6.3 1.1 %constant_dynamic-slice_fusion.1 = (bf16[64,1024]{1,0:T(8,128)(2,1)S(1)}, bf16[64,1024]{1,0:T(8,128)(2,1)S(1)}, bf16[64,1024]{1,0:T(8,128)(2,1)S(1)}, bf16[64,1024]{1,0:T(8,128)(2,1)S(1)}) fusion(bf16[256,1024]{1,0:T(8,128)(2,1)} %param.6, s32[]{:T(128)S(6)} %select_n.56, s32[]{:T(128)S(6)} %select_n.55, s32[]{:T(128)S(6)} %select_n.54, s32[]{:T(128)S(6)} %select_n.53), kind=kLoop, calls=%fused_computation.19 | loop fusion | bytes 1048592 | tf_op jit(solution)/shard_map/dynamic_slice | solution.py:401
  7.5 0.5 collective-permute-start.3
  8.0 0.1 collective-permute-start.4
  8.1 3.9 %collective-permute-start.5 = (bf16[64,1024]{1,0:T(8,128)(2,1)S(1)}, bf16[64,1024]{1,0:T(8,128)(2,1)S(1)}, u32[]{:S(2)}, u32[]{:S(2)}) collective-permute-start(bf16[64,1024]{1,0:T(8,128)(2,1)S(1)} %get-tuple-element.54), channel_id=1, source_target_pairs={{0,6},{1,7},{2,4},{3,5},{4,2},{5,3},{6,0},{7,1},{8,14},{9,15},{10,... | collective-permute-start | bytes 393224 | tf_op jit(solution)/shard_map/ppermute | solution.py:64
  11.9 0.1 stack.50
  12.0 5.8 %collective-permute-done.1 = bf16[32,4096]{1,0:T(8,128)(2,1)S(1)} collective-permute-done((bf16[32,4096]{1,0:T(8,128)(2,1)}, bf16[32,4096]{1,0:T(8,128)(2,1)S(1)}, u32[]{:S(2)}, u32[]{:S(2)}) %collective-permute-start.1) | collective-permute-done | bytes 262176 | tf_op jit(solution)/shard_map/ppermute | solution.py:64
  17.8 0.0 collective-permute-start.2
  17.9 0.1 iota_add_fusion
  17.9 0.1 add.98
  18.0 8.6 %collective-permute-done.3.refs_1_ = bf16[64,1024]{1,0:T(8,128)(2,1)S(1)} collective-permute-done((bf16[64,1024]{1,0:T(8,128)(2,1)S(1)}, bf16[64,1024]{1,0:T(8,128)(2,1)S(1)}, u32[]{:S(2)}, u32[]{:S(2)}) %collective-permute-start.3) | collective-permute-done | bytes 131104 | tf_op jit(solution)/shard_map/ppermute | solution.py:64
  26.6 0.0 collective-permute-done.4.refs_2_
  26.6 1.0 %collective-permute-done.5.refs_3_ = bf16[64,1024]{1,0:T(8,128)(2,1)S(1)} collective-permute-done((bf16[64,1024]{1,0:T(8,128)(2,1)S(1)}, bf16[64,1024]{1,0:T(8,128)(2,1)S(1)}, u32[]{:S(2)}, u32[]{:S(2)}) %collective-permute-start.5) | collective-permute-done | bytes 131104 | tf_op jit(solution)/shard_map/ppermute | solution.py:64
  27.6 0.0 collective-permute-done
  27.6 3.6 %collective-permute-done.2 = bf16[32,4096]{1,0:T(8,128)(2,1)S(1)} collective-permute-done((bf16[32,4096]{1,0:T(8,128)(2,1)S(1)}, bf16[32,4096]{1,0:T(8,128)(2,1)S(1)}, u32[]{:S(2)}, u32[]{:S(2)}) %collective-permute-start.2) | collective-permute-done | bytes 262176 | tf_op jit(solution)/shard_map/ppermute | solution.py:64
  31.2 1.0 constant_dynamic-update-slice_fusion.3
  32.3 0.1 collective-permute-start.6
  32.4 0.1 convert_reduce_fusion
  32.5 0.7 compare_reduce_fusion.1
  33.3 0.6 collective-permute-start.10
  33.9 0.2 compare_reduce_fusion
  34.1 1.3 %collective-permute-done.10.refs_4_ = bf16[4,32,1024]{2,1,0:T(8,128)(2,1)S(1)} collective-permute-done((bf16[4,32,1024]{2,1,0:T(8,128)(2,1)S(1)}, bf16[4,32,1024]{2,1,0:T(8,128)(2,1)S(1)}, u32[]{:S(2)}, u32[]{:S(2)}) %collective-permute-start.10) | collective-permute-done | bytes 262176 | tf_op jit(solution)/shard_map/ppermute | solution.py:64
  35.4 1.0 %shard_map.62 = (bf16[64,1024]{1,0:T(8,128)(2,1)S(1)}, bf16[64,1024]{1,0:T(8,128)(2,1)S(1)}, bf16[64,1024]{1,0:T(8,128)(2,1)S(1)}, bf16[64,1024]{1,0:T(8,128)(2,1)S(1)}) custom-call(s32[64]{0:T(128)S(1)} %fusion.2.slots_ref, s32[64]{0:T(128)S(1)} %convert_element_type.27.listed_ref, bf16[64,1024]{1,0:T(8,128)(2,1)S(1)} %get-tuple-element.32.refs_0_, ...), custom_call_target="tpu_custom_call" | custom-call | bytes 524288 | tf_op jit(solution)/shard_map/pallas_call | solution.py:267
  36.4 1.6 %collective-permute-start.11 = (bf16[64,1024]{1,0:T(8,128)(2,1)S(1)}, bf16[64,1024]{1,0:T(8,128)(2,1)S(1)}, u32[]{:S(2)}, u32[]{:S(2)}) collective-permute-start(bf16[64,1024]{1,0:T(8,128)(2,1)S(1)} %get-tuple-element.37), channel_id=1, source_target_pairs={{0,2},{1,3},{2,0},{3,1},{4,6},{5,7},{6,4},{7,5},{8,10},{9,11},{10,... | collective-permute-start | bytes 393224 | tf_op jit(solution)/shard_map/ppermute | solution.py:64
  38.0 1.6 %collective-permute-start.12 = (bf16[64,1024]{1,0:T(8,128)(2,1)S(1)}, bf16[64,1024]{1,0:T(8,128)(2,1)S(1)}, u32[]{:S(2)}, u32[]{:S(2)}) collective-permute-start(bf16[64,1024]{1,0:T(8,128)(2,1)S(1)} %get-tuple-element.38), channel_id=1, source_target_pairs={{0,4},{1,5},{2,6},{3,7},{4,0},{5,1},{6,2},{7,3},{8,12},{9,13},{10,... | collective-permute-start | bytes 393224 | tf_op jit(solution)/shard_map/ppermute | solution.py:64
  39.6 1.3 %collective-permute-start.13 = (bf16[64,1024]{1,0:T(8,128)(2,1)S(1)}, bf16[64,1024]{1,0:T(8,128)(2,1)S(1)}, u32[]{:S(2)}, u32[]{:S(2)}) collective-permute-start(bf16[64,1024]{1,0:T(8,128)(2,1)S(1)} %get-tuple-element.39), channel_id=1, source_target_pairs={{0,6},{1,7},{2,4},{3,5},{4,2},{5,3},{6,0},{7,1},{8,14},{9,15},{10,... | collective-permute-start | bytes 393224 | tf_op jit(solution)/shard_map/ppermute | solution.py:64
  40.9 0.0 collective-permute-done.6.refs_1_
  40.9 5.4 %shard_map.59 = (f32[256,1024]{1,0:T(8,128)S(1)}, f32[8,256]{1,0:T(8,128)S(1)}) custom-call(bf16[128,4096]{1,0:T(8,128)(2,1)S(1)} %constant_dynamic-update-slice_fusion.refs_0_.own_ref, bf16[128,4096]{1,0:T(8,128)(2,1)S(1)} %collective-permute-done.6.refs_1_, bf16[1024,4096]{1,0:T(8,128)(2,1)} %refs_7_.1, f32[1,256]{1,0:T(1,128)S(1)} %bitcast.19), custom_call_target="tpu_custom_call" | custom-call | flops 2147483648 | bytes 10486272 | tf_op jit(solution)/shard_map/pallas_call | solution.py:164
  46.3 0.1 collective-permute-start.7
  46.4 1.2 %collective-permute-done.7.b_ref = f32[8,256]{1,0:T(8,128)S(1)} collective-permute-done((f32[8,256]{1,0:T(8,128)S(1)}, f32[8,256]{1,0:T(8,128)S(1)}, u32[]{:S(2)}, u32[]{:S(2)}) %collective-permute-start.7) | collective-permute-done | bytes 8224 | tf_op jit(solution)/shard_map/ppermute | solution.py:64
  47.6 0.7 collective-permute-start.8
  48.3 0.1 shard_map.64
  48.4 1.6 %collective-permute-start.15 = (bf16[128,1024]{1,0:T(8,128)(2,1)S(1)}, bf16[128,1024]{1,0:T(8,128)(2,1)S(1)}, u32[]{:S(2)}, u32[]{:S(2)}) collective-permute-start(bf16[128,1024]{1,0:T(8,128)(2,1)S(1)} %get-tuple-element.41), channel_id=1, source_target_pairs={{0,8},{8,0},{16,24},{24,16},{1,9},{9,1},{17,25},{25,17},{2,10},{10... | collective-permute-start | bytes 786440 | tf_op jit(solution)/shard_map/ppermute | solution.py:64
  50.0 1.3 %collective-permute-done.8.b_ref = f32[8,256]{1,0:T(8,128)S(1)} collective-permute-done((f32[8,256]{1,0:T(8,128)S(1)}, f32[8,256]{1,0:T(8,128)S(1)}, u32[]{:S(2)}, u32[]{:S(2)}) %collective-permute-start.8) | collective-permute-done | bytes 8224 | tf_op jit(solution)/shard_map/ppermute | solution.py:64
  51.3 1.6 %collective-permute-start.16 = (bf16[128,1024]{1,0:T(8,128)(2,1)S(1)}, bf16[128,1024]{1,0:T(8,128)(2,1)S(1)}, u32[]{:S(2)}, u32[]{:S(2)}) collective-permute-start(bf16[128,1024]{1,0:T(8,128)(2,1)S(1)} %get-tuple-element.42), channel_id=1, source_target_pairs={{0,16},{8,24},{16,0},{24,8},{1,17},{9,25},{17,1},{25,9},{2,18},{10... | collective-permute-start | bytes 786440 | tf_op jit(solution)/shard_map/ppermute | solution.py:64
  52.9 1.5 %collective-permute-start.17 = (bf16[128,1024]{1,0:T(8,128)(2,1)S(1)}, bf16[128,1024]{1,0:T(8,128)(2,1)S(1)}, u32[]{:S(2)}, u32[]{:S(2)}) collective-permute-start(bf16[128,1024]{1,0:T(8,128)(2,1)S(1)} %get-tuple-element.43), channel_id=1, source_target_pairs={{0,24},{8,16},{16,8},{24,0},{1,25},{9,17},{17,9},{25,1},{2,26},{10... | collective-permute-start | bytes 786440 | tf_op jit(solution)/shard_map/ppermute | solution.py:64
  54.4 0.0 collective-permute-done.12.refs_2_.refs_4_
  54.4 0.0 collective-permute-done.13.refs_3_.refs_5_
  54.4 0.1 collective-permute-start.14
  54.5 1.1 %collective-permute-start.9 = (f32[8,256]{1,0:T(8,128)S(1)}, f32[8,256]{1,0:T(8,128)S(1)}, u32[]{:S(2)}, u32[]{:S(2)}) collective-permute-start(f32[8,256]{1,0:T(8,128)S(1)} %shard_map.61.refs_4_.refs_0_), channel_id=1, source_target_pairs={{0,4},{1,5},{2,6},{3,7},{4,0},{5,1},{6,2},{7,3},{8,12},{9,13},{10,... | collective-permute-start | bytes 24584 | tf_op jit(solution)/shard_map/ppermute | solution.py:64
  55.6 2.1 %collective-permute-done.15.refs_9_ = bf16[128,1024]{1,0:T(8,128)(2,1)S(1)} collective-permute-done((bf16[128,1024]{1,0:T(8,128)(2,1)S(1)}, bf16[128,1024]{1,0:T(8,128)(2,1)S(1)}, u32[]{:S(2)}, u32[]{:S(2)}) %collective-permute-start.15) | collective-permute-done | bytes 262176 | tf_op jit(solution)/shard_map/ppermute | solution.py:64
  57.7 6.9 %collective-permute-done.16.refs_10_ = bf16[128,1024]{1,0:T(8,128)(2,1)S(1)} collective-permute-done((bf16[128,1024]{1,0:T(8,128)(2,1)S(1)}, bf16[128,1024]{1,0:T(8,128)(2,1)S(1)}, u32[]{:S(2)}, u32[]{:S(2)}) %collective-permute-start.16) | collective-permute-done | bytes 262176 | tf_op jit(solution)/shard_map/ppermute | solution.py:64
  64.5 0.0 collective-permute-done.14.refs_6_
  64.5 4.9 %shard_map.65 = (bf16[256,1024]{1,0:T(8,128)(2,1)S(1)}, f32[128,4096]{1,0:T(8,128)S(1)}, bf16[128,4096]{1,0:T(8,128)(2,1)S(1)}, bf16[4,128,1024]{2,1,0:T(8,128)(2,1)S(1)}) custom-call(f32[256,1024]{1,0:T(8,128)S(1)} %get-tuple-element.29.logits_ref, f32[8,256]{1,0:T(8,128)S(1)} %shard_map.61.refs_4_.refs_0_, f32[8,256]{1,0:T(8,128)S(1)} %collective-permute-done.9.refs_1_, ...), custom_call_target="tpu_custom_call" | custom-call | flops 2147483648 | bytes 9707520 | tf_op jit(solution)/shard_map/pallas_call | solution.py:332
  69.4 0.1 collective-permute-start.18
  69.5 2.6 %collective-permute-done.18 = bf16[128,4096]{1,0:T(8,128)(2,1)S(1)} collective-permute-done((bf16[128,4096]{1,0:T(8,128)(2,1)S(1)}, bf16[128,4096]{1,0:T(8,128)(2,1)S(1)}, u32[]{:S(2)}, u32[]{:S(2)}) %collective-permute-start.18) | collective-permute-done | bytes 1048608 | tf_op jit(solution)/shard_map/ppermute | solution.py:64
  72.2 0.3 fusion.9
  72.5 0.4 collective-permute-start.20
  72.9 1.4 %collective-permute-start.22 = (bf16[256,1024]{1,0:T(8,128)(2,1)S(1)}, bf16[256,1024]{1,0:T(8,128)(2,1)S(1)}, u32[]{:S(2)}, u32[]{:S(2)}) collective-permute-start(bf16[256,1024]{1,0:T(8,128)(2,1)S(1)} %get-tuple-element.46.refs_0_), channel_id=1, source_target_pairs={{0,8},{8,0},{16,24},{24,16},{1,9},{9,1},{17,25},{25,17},{2,10},{10... | collective-permute-start | bytes 1572872 | tf_op jit(solution)/shard_map/ppermute | solution.py:64
  74.3 1.5 %collective-permute-start.23 = (bf16[256,1024]{1,0:T(8,128)(2,1)S(1)}, bf16[256,1024]{1,0:T(8,128)(2,1)S(1)}, u32[]{:S(2)}, u32[]{:S(2)}) collective-permute-start(bf16[256,1024]{1,0:T(8,128)(2,1)S(1)} %get-tuple-element.46.refs_0_), channel_id=1, source_target_pairs={{0,16},{8,24},{16,0},{24,8},{1,17},{9,25},{17,1},{25,9},{2,18},{10... | collective-permute-start | bytes 1572872 | tf_op jit(solution)/shard_map/ppermute | solution.py:64
  75.9 1.8 %collective-permute-start.19 = (bf16[32,4096]{1,0:T(8,128)(2,1)S(1)}, bf16[32,4096]{1,0:T(8,128)(2,1)S(1)}, u32[]{:S(2)}, u32[]{:S(2)}) collective-permute-start(bf16[32,4096]{1,0:T(8,128)(2,1)S(1)} %get-tuple-element.52), channel_id=1, source_target_pairs={{0,2},{1,3},{2,0},{3,1},{4,6},{5,7},{6,4},{7,5},{8,10},{9,11},{10,... | collective-permute-start | bytes 786440 | tf_op jit(solution)/shard_map/ppermute | solution.py:64
  77.7 4.1 %collective-permute-done.20 = bf16[32,4096]{1,0:T(8,128)(2,1)S(1)} collective-permute-done((bf16[32,4096]{1,0:T(8,128)(2,1)S(1)}, bf16[32,4096]{1,0:T(8,128)(2,1)S(1)}, u32[]{:S(2)}, u32[]{:S(2)}) %collective-permute-start.20) | collective-permute-done | bytes 262176 | tf_op jit(solution)/shard_map/ppermute | solution.py:64
  81.8 1.4 %collective-permute-start.21 = (bf16[32,4096]{1,0:T(8,128)(2,1)S(1)}, bf16[32,4096]{1,0:T(8,128)(2,1)S(1)}, u32[]{:S(2)}, u32[]{:S(2)}) collective-permute-start(bf16[32,4096]{1,0:T(8,128)(2,1)S(1)} %fusion), channel_id=1, source_target_pairs={{0,4},{1,5},{2,6},{3,7},{4,0},{5,1},{6,2},{7,3},{8,12},{9,13},{10,... | collective-permute-start | bytes 786440 | tf_op jit(solution)/shard_map/ppermute | solution.py:64
  83.2 0.0 collective-permute-start.26
  83.2 3.4 %collective-permute-done.22.refs_1_ = bf16[256,1024]{1,0:T(8,128)(2,1)S(1)} collective-permute-done((bf16[256,1024]{1,0:T(8,128)(2,1)S(1)}, bf16[256,1024]{1,0:T(8,128)(2,1)S(1)}, u32[]{:S(2)}, u32[]{:S(2)}) %collective-permute-start.22) | collective-permute-done | bytes 524320 | tf_op jit(solution)/shard_map/ppermute | solution.py:64
  86.7 1.6 %collective-permute-start.24 = (bf16[128,1024]{1,0:T(8,128)(2,1)S(1)}, bf16[128,1024]{1,0:T(8,128)(2,1)S(1)}, u32[]{:S(2)}, u32[]{:S(2)}) collective-permute-start(bf16[128,1024]{1,0:T(8,128)(2,1)S(1)} %slice.30), channel_id=1, source_target_pairs={{0,16},{8,24},{16,0},{24,8},{1,17},{9,25},{17,1},{25,9},{2,18},{10... | collective-permute-start | bytes 786440 | tf_op jit(solution)/shard_map/ppermute | solution.py:64
  88.3 0.0 collective-permute-done.23.refs_2_
  88.3 1.6 %collective-permute-start.25 = (bf16[128,1024]{1,0:T(8,128)(2,1)S(1)}, bf16[128,1024]{1,0:T(8,128)(2,1)S(1)}, u32[]{:S(2)}, u32[]{:S(2)}) collective-permute-start(bf16[128,1024]{1,0:T(8,128)(2,1)S(1)} %slice.31), channel_id=1, source_target_pairs={{0,8},{8,0},{16,24},{24,16},{1,9},{9,1},{17,25},{25,17},{2,10},{10... | collective-permute-start | bytes 786440 | tf_op jit(solution)/shard_map/ppermute | solution.py:64
  89.9 0.2 collective-permute-done.19
  90.1 5.0 %collective-permute-done.21 = bf16[32,4096]{1,0:T(8,128)(2,1)S(1)} collective-permute-done((bf16[32,4096]{1,0:T(8,128)(2,1)S(1)}, bf16[32,4096]{1,0:T(8,128)(2,1)S(1)}, u32[]{:S(2)}, u32[]{:S(2)}) %collective-permute-start.21) | collective-permute-done | bytes 262176 | tf_op jit(solution)/shard_map/ppermute | solution.py:64
  95.1 0.8 fusion.7
  95.9 3.7 %shard_map.66 = bf16[1024,1024]{1,0:T(8,128)(2,1)} custom-call(bf16[256,1024]{1,0:T(8,128)(2,1)S(1)} %get-tuple-element.46.refs_0_, bf16[256,1024]{1,0:T(8,128)(2,1)S(1)} %collective-permute-done.22.refs_1_, bf16[256,1024]{1,0:T(8,128)(2,1)S(1)} %collective-permute-done.23.refs_2_, bf16[128,1024]{1,0:T(8,128)(2,1)S(1)} %collective-permute-done.24.refs_3_, ...), custom_call_target="tpu_custom_call" | custom-call | flops 2147483648 | bytes 4194304 | tf_op jit(solution)/shard_map/pallas_call | solution.py:368
  (26 shorter events, 0.4 us)
Async XLA Ops:
  0.6 17.4 %copy-start = (s32[2,64]{1,0:T(2,128)S(1)}, s32[2,64]{1,0:T(2,128)}, u32[]{:S(2)}) copy-start(s32[2,64]{1,0:T(2,128)} %param.7) | copy-start | bytes 1540
  0.6 31.7 %copy-start.1 = (bf16[256,1024]{1,0:T(8,128)(2,1)S(1)}, bf16[256,1024]{1,0:T(8,128)(2,1)}, u32[]{:S(2)}) copy-start(bf16[256,1024]{1,0:T(8,128)(2,1)} %param.6) | copy-start | bytes 1572868
  0.7 17.2 %collective-permute-start.1 = (bf16[32,4096]{1,0:T(8,128)(2,1)}, bf16[32,4096]{1,0:T(8,128)(2,1)S(1)}, u32[]{:S(2)}, u32[]{:S(2)}) collective-permute-start(bf16[32,4096]{1,0:T(8,128)(2,1)} %param.4), channel_id=1, source_target_pairs={{0,4},{1,5},{2,6},{3,7},{4,0},{5,1},{6,2},{7,3},{8,12},{9,13},{10,... | collective-permute-start | bytes 786440 | tf_op jit(solution)/shard_map/ppermute | solution.py:64
  4.8 22.8 %collective-permute-start = (bf16[32,4096]{1,0:T(8,128)(2,1)}, bf16[32,4096]{1,0:T(8,128)(2,1)S(1)}, u32[]{:S(2)}, u32[]{:S(2)}) collective-permute-start(bf16[32,4096]{1,0:T(8,128)(2,1)} %param.4), channel_id=1, source_target_pairs={{0,2},{1,3},{2,0},{3,1},{4,6},{5,7},{6,4},{7,5},{8,10},{9,11},{10,... | collective-permute-start | bytes 786440 | tf_op jit(solution)/shard_map/ppermute | solution.py:64
  7.5 19.1 %collective-permute-start.3 = (bf16[64,1024]{1,0:T(8,128)(2,1)S(1)}, bf16[64,1024]{1,0:T(8,128)(2,1)S(1)}, u32[]{:S(2)}, u32[]{:S(2)}) collective-permute-start(bf16[64,1024]{1,0:T(8,128)(2,1)S(1)} %get-tuple-element.56), channel_id=1, source_target_pairs={{0,2},{1,3},{2,0},{3,1},{4,6},{5,7},{6,4},{7,5},{8,10},{9,11},{10,... | collective-permute-start | bytes 393224 | tf_op jit(solution)/shard_map/ppermute | solution.py:64
  8.0 18.6 %collective-permute-start.4 = (bf16[64,1024]{1,0:T(8,128)(2,1)S(1)}, bf16[64,1024]{1,0:T(8,128)(2,1)S(1)}, u32[]{:S(2)}, u32[]{:S(2)}) collective-permute-start(bf16[64,1024]{1,0:T(8,128)(2,1)S(1)} %get-tuple-element.55), channel_id=1, source_target_pairs={{0,4},{1,5},{2,6},{3,7},{4,0},{5,1},{6,2},{7,3},{8,12},{9,13},{10,... | collective-permute-start | bytes 393224 | tf_op jit(solution)/shard_map/ppermute | solution.py:64
  8.1 19.5 %collective-permute-start.5 = (bf16[64,1024]{1,0:T(8,128)(2,1)S(1)}, bf16[64,1024]{1,0:T(8,128)(2,1)S(1)}, u32[]{:S(2)}, u32[]{:S(2)}) collective-permute-start(bf16[64,1024]{1,0:T(8,128)(2,1)S(1)} %get-tuple-element.54), channel_id=1, source_target_pairs={{0,6},{1,7},{2,4},{3,5},{4,2},{5,3},{6,0},{7,1},{8,14},{9,15},{10,... | collective-permute-start | bytes 393224 | tf_op jit(solution)/shard_map/ppermute | solution.py:64
  17.8 13.4 %collective-permute-start.2 = (bf16[32,4096]{1,0:T(8,128)(2,1)S(1)}, bf16[32,4096]{1,0:T(8,128)(2,1)S(1)}, u32[]{:S(2)}, u32[]{:S(2)}) collective-permute-start(bf16[32,4096]{1,0:T(8,128)(2,1)S(1)} %collective-permute-done.1), channel_id=1, source_target_pairs={{0,2},{1,3},{2,0},{3,1},{4,6},{5,7},{6,4},{7,5},{8,10},{9,11},{10,... | collective-permute-start | bytes 786440 | tf_op jit(solution)/shard_map/ppermute | solution.py:64
  32.3 8.6 %collective-permute-start.6 = (bf16[128,4096]{1,0:T(8,128)(2,1)S(1)}, bf16[128,4096]{1,0:T(8,128)(2,1)S(1)}, u32[]{:S(2)}, u32[]{:S(2)}) collective-permute-start(bf16[128,4096]{1,0:T(8,128)(2,1)S(1)} %constant_dynamic-update-slice_fusion.refs_0_.own_ref), channel_id=1, source_target_pairs={{0,1},{1,0},{2,3},{3,2},{4,5},{5,4},{6,7},{7,6},{8,9},{9,8},{10,11... | collective-permute-start | bytes 3145736 | tf_op jit(solution)/shard_map/ppermute | solution.py:64
  33.3 2.1 %collective-permute-start.10 = (bf16[4,32,1024]{2,1,0:T(8,128)(2,1)S(1)}, bf16[4,32,1024]{2,1,0:T(8,128)(2,1)S(1)}, u32[]{:S(2)}, u32[]{:S(2)}) collective-permute-start(bf16[4,32,1024]{2,1,0:T(8,128)(2,1)S(1)} %pad_maximum_fusion), channel_id=1, source_target_pairs={{0,1},{1,0},{2,3},{3,2},{4,5},{5,4},{6,7},{7,6},{8,9},{9,8},{10,11... | collective-permute-start | bytes 786440 | tf_op jit(solution)/shard_map/ppermute | solution.py:64
  36.4 16.5 %collective-permute-start.11 = (bf16[64,1024]{1,0:T(8,128)(2,1)S(1)}, bf16[64,1024]{1,0:T(8,128)(2,1)S(1)}, u32[]{:S(2)}, u32[]{:S(2)}) collective-permute-start(bf16[64,1024]{1,0:T(8,128)(2,1)S(1)} %get-tuple-element.37), channel_id=1, source_target_pairs={{0,2},{1,3},{2,0},{3,1},{4,6},{5,7},{6,4},{7,5},{8,10},{9,11},{10,... | collective-permute-start | bytes 393224 | tf_op jit(solution)/shard_map/ppermute | solution.py:64
  38.0 16.4 %collective-permute-start.12 = (bf16[64,1024]{1,0:T(8,128)(2,1)S(1)}, bf16[64,1024]{1,0:T(8,128)(2,1)S(1)}, u32[]{:S(2)}, u32[]{:S(2)}) collective-permute-start(bf16[64,1024]{1,0:T(8,128)(2,1)S(1)} %get-tuple-element.38), channel_id=1, source_target_pairs={{0,4},{1,5},{2,6},{3,7},{4,0},{5,1},{6,2},{7,3},{8,12},{9,13},{10,... | collective-permute-start | bytes 393224 | tf_op jit(solution)/shard_map/ppermute | solution.py:64
  39.6 14.8 %collective-permute-start.13 = (bf16[64,1024]{1,0:T(8,128)(2,1)S(1)}, bf16[64,1024]{1,0:T(8,128)(2,1)S(1)}, u32[]{:S(2)}, u32[]{:S(2)}) collective-permute-start(bf16[64,1024]{1,0:T(8,128)(2,1)S(1)} %get-tuple-element.39), channel_id=1, source_target_pairs={{0,6},{1,7},{2,4},{3,5},{4,2},{5,3},{6,0},{7,1},{8,14},{9,15},{10,... | collective-permute-start | bytes 393224 | tf_op jit(solution)/shard_map/ppermute | solution.py:64
  46.3 1.2 %collective-permute-start.7 = (f32[8,256]{1,0:T(8,128)S(1)}, f32[8,256]{1,0:T(8,128)S(1)}, u32[]{:S(2)}, u32[]{:S(2)}) collective-permute-start(f32[8,256]{1,0:T(8,128)S(1)} %get-tuple-element.30.a_ref), channel_id=1, source_target_pairs={{0,1},{1,0},{2,3},{3,2},{4,5},{5,4},{6,7},{7,6},{8,9},{9,8},{10,11... | collective-permute-start | bytes 24584 | tf_op jit(solution)/shard_map/ppermute | solution.py:64
  47.6 3.7 %collective-permute-start.8 = (f32[8,256]{1,0:T(8,128)S(1)}, f32[8,256]{1,0:T(8,128)S(1)}, u32[]{:S(2)}, u32[]{:S(2)}) collective-permute-start(f32[8,256]{1,0:T(8,128)S(1)} %shard_map.60.a_ref), channel_id=1, source_target_pairs={{0,2},{1,3},{2,0},{3,1},{4,6},{5,7},{6,4},{7,5},{8,10},{9,11},{10,... | collective-permute-start | bytes 24584 | tf_op jit(solution)/shard_map/ppermute | solution.py:64
  48.4 9.3 %collective-permute-start.15 = (bf16[128,1024]{1,0:T(8,128)(2,1)S(1)}, bf16[128,1024]{1,0:T(8,128)(2,1)S(1)}, u32[]{:S(2)}, u32[]{:S(2)}) collective-permute-start(bf16[128,1024]{1,0:T(8,128)(2,1)S(1)} %get-tuple-element.41), channel_id=1, source_target_pairs={{0,8},{8,0},{16,24},{24,16},{1,9},{9,1},{17,25},{25,17},{2,10},{10... | collective-permute-start | bytes 786440 | tf_op jit(solution)/shard_map/ppermute | solution.py:64
  51.3 13.2 %collective-permute-start.16 = (bf16[128,1024]{1,0:T(8,128)(2,1)S(1)}, bf16[128,1024]{1,0:T(8,128)(2,1)S(1)}, u32[]{:S(2)}, u32[]{:S(2)}) collective-permute-start(bf16[128,1024]{1,0:T(8,128)(2,1)S(1)} %get-tuple-element.42), channel_id=1, source_target_pairs={{0,16},{8,24},{16,0},{24,8},{1,17},{9,25},{17,1},{25,9},{2,18},{10... | collective-permute-start | bytes 786440 | tf_op jit(solution)/shard_map/ppermute | solution.py:64
  52.9 11.6 %collective-permute-start.17 = (bf16[128,1024]{1,0:T(8,128)(2,1)S(1)}, bf16[128,1024]{1,0:T(8,128)(2,1)S(1)}, u32[]{:S(2)}, u32[]{:S(2)}) collective-permute-start(bf16[128,1024]{1,0:T(8,128)(2,1)S(1)} %get-tuple-element.43), channel_id=1, source_target_pairs={{0,24},{8,16},{16,8},{24,0},{1,25},{9,17},{17,9},{25,1},{2,26},{10... | collective-permute-start | bytes 786440 | tf_op jit(solution)/shard_map/ppermute | solution.py:64
  54.4 10.1 %collective-permute-start.14 = (bf16[4,32,1024]{2,1,0:T(8,128)(2,1)S(1)}, bf16[4,32,1024]{2,1,0:T(8,128)(2,1)S(1)}, u32[]{:S(2)}, u32[]{:S(2)}) collective-permute-start(bf16[4,32,1024]{2,1,0:T(8,128)(2,1)S(1)} %shard_map.63), channel_id=1, source_target_pairs={{0,1},{1,0},{2,3},{3,2},{4,5},{5,4},{6,7},{7,6},{8,9},{9,8},{10,11... | collective-permute-start | bytes 786440 | tf_op jit(solution)/shard_map/ppermute | solution.py:64
  54.5 10.0 %collective-permute-start.9 = (f32[8,256]{1,0:T(8,128)S(1)}, f32[8,256]{1,0:T(8,128)S(1)}, u32[]{:S(2)}, u32[]{:S(2)}) collective-permute-start(f32[8,256]{1,0:T(8,128)S(1)} %shard_map.61.refs_4_.refs_0_), channel_id=1, source_target_pairs={{0,4},{1,5},{2,6},{3,7},{4,0},{5,1},{6,2},{7,3},{8,12},{9,13},{10,... | collective-permute-start | bytes 24584 | tf_op jit(solution)/shard_map/ppermute | solution.py:64
  69.4 2.7 %collective-permute-start.18 = (bf16[128,4096]{1,0:T(8,128)(2,1)S(1)}, bf16[128,4096]{1,0:T(8,128)(2,1)S(1)}, u32[]{:S(2)}, u32[]{:S(2)}) collective-permute-start(bf16[128,4096]{1,0:T(8,128)(2,1)S(1)} %get-tuple-element.45), channel_id=1, source_target_pairs={{0,1},{1,0},{2,3},{3,2},{4,5},{5,4},{6,7},{7,6},{8,9},{9,8},{10,11... | collective-permute-start | bytes 3145736 | tf_op jit(solution)/shard_map/ppermute | solution.py:64
  72.5 9.2 %collective-permute-start.20 = (bf16[32,4096]{1,0:T(8,128)(2,1)S(1)}, bf16[32,4096]{1,0:T(8,128)(2,1)S(1)}, u32[]{:S(2)}, u32[]{:S(2)}) collective-permute-start(bf16[32,4096]{1,0:T(8,128)(2,1)S(1)} %get-tuple-element.53), channel_id=1, source_target_pairs={{0,2},{1,3},{2,0},{3,1},{4,6},{5,7},{6,4},{7,5},{8,10},{9,11},{10,... | collective-permute-start | bytes 786440 | tf_op jit(solution)/shard_map/ppermute | solution.py:64
  72.9 13.7 %collective-permute-start.22 = (bf16[256,1024]{1,0:T(8,128)(2,1)S(1)}, bf16[256,1024]{1,0:T(8,128)(2,1)S(1)}, u32[]{:S(2)}, u32[]{:S(2)}) collective-permute-start(bf16[256,1024]{1,0:T(8,128)(2,1)S(1)} %get-tuple-element.46.refs_0_), channel_id=1, source_target_pairs={{0,8},{8,0},{16,24},{24,16},{1,9},{9,1},{17,25},{25,17},{2,10},{10... | collective-permute-start | bytes 1572872 | tf_op jit(solution)/shard_map/ppermute | solution.py:64
  74.3 14.0 %collective-permute-start.23 = (bf16[256,1024]{1,0:T(8,128)(2,1)S(1)}, bf16[256,1024]{1,0:T(8,128)(2,1)S(1)}, u32[]{:S(2)}, u32[]{:S(2)}) collective-permute-start(bf16[256,1024]{1,0:T(8,128)(2,1)S(1)} %get-tuple-element.46.refs_0_), channel_id=1, source_target_pairs={{0,16},{8,24},{16,0},{24,8},{1,17},{9,25},{17,1},{25,9},{2,18},{10... | collective-permute-start | bytes 1572872 | tf_op jit(solution)/shard_map/ppermute | solution.py:64
  75.9 14.2 %collective-permute-start.19 = (bf16[32,4096]{1,0:T(8,128)(2,1)S(1)}, bf16[32,4096]{1,0:T(8,128)(2,1)S(1)}, u32[]{:S(2)}, u32[]{:S(2)}) collective-permute-start(bf16[32,4096]{1,0:T(8,128)(2,1)S(1)} %get-tuple-element.52), channel_id=1, source_target_pairs={{0,2},{1,3},{2,0},{3,1},{4,6},{5,7},{6,4},{7,5},{8,10},{9,11},{10,... | collective-permute-start | bytes 786440 | tf_op jit(solution)/shard_map/ppermute | solution.py:64
  81.8 13.3 %collective-permute-start.21 = (bf16[32,4096]{1,0:T(8,128)(2,1)S(1)}, bf16[32,4096]{1,0:T(8,128)(2,1)S(1)}, u32[]{:S(2)}, u32[]{:S(2)}) collective-permute-start(bf16[32,4096]{1,0:T(8,128)(2,1)S(1)} %fusion), channel_id=1, source_target_pairs={{0,4},{1,5},{2,6},{3,7},{4,0},{5,1},{6,2},{7,3},{8,12},{9,13},{10,... | collective-permute-start | bytes 786440 | tf_op jit(solution)/shard_map/ppermute | solution.py:64
  83.2 12.7 %collective-permute-start.26 = (bf16[4,128,1024]{2,1,0:T(8,128)(2,1)S(1)}, bf16[4,128,1024]{2,1,0:T(8,128)(2,1)S(1)}, u32[]{:S(2)}, u32[]{:S(2)}) collective-permute-start(bf16[4,128,1024]{2,1,0:T(8,128)(2,1)S(1)} %get-tuple-element.47.refs_5_), channel_id=1, source_target_pairs={{0,1},{1,0},{2,3},{3,2},{4,5},{5,4},{6,7},{7,6},{8,9},{9,8},{10,11... | collective-permute-start | bytes 3145736 | tf_op jit(solution)/shard_map/ppermute | solution.py:64
  86.7 9.3 %collective-permute-start.24 = (bf16[128,1024]{1,0:T(8,128)(2,1)S(1)}, bf16[128,1024]{1,0:T(8,128)(2,1)S(1)}, u32[]{:S(2)}, u32[]{:S(2)}) collective-permute-start(bf16[128,1024]{1,0:T(8,128)(2,1)S(1)} %slice.30), channel_id=1, source_target_pairs={{0,16},{8,24},{16,0},{24,8},{1,17},{9,25},{17,1},{25,9},{2,18},{10... | collective-permute-start | bytes 786440 | tf_op jit(solution)/shard_map/ppermute | solution.py:64
  88.3 7.6 %collective-permute-start.25 = (bf16[128,1024]{1,0:T(8,128)(2,1)S(1)}, bf16[128,1024]{1,0:T(8,128)(2,1)S(1)}, u32[]{:S(2)}, u32[]{:S(2)}) collective-permute-start(bf16[128,1024]{1,0:T(8,128)(2,1)S(1)} %slice.31), channel_id=1, source_target_pairs={{0,8},{8,0},{16,24},{24,16},{1,9},{9,1},{17,25},{25,17},{2,10},{10... | collective-permute-start | bytes 786440 | tf_op jit(solution)/shard_map/ppermute | solution.py:64

commit v4 on v3

--- a/solution.py
+++ b/solution.py
@@ -7,6 +7,7 @@
 
 BLK = 128
 TILE_ROWS = 16
+CORES = 2
 
 
 loss_scale = 1024.0
@@ -106,7 +107,7 @@
     )
 
 
-def logits_and_stats(own, other, rows, weight, mass, parts=8, ahead=4):
+def logits_and_stats(own, other, rows, weight, mass, quarter, parts=8, ahead=4):
     half, width = own.shape
     chips = half // rows
     tokens = 2 * half
@@ -116,8 +117,20 @@
     def body(*refs):
         piece_refs, refs = refs[:2], refs[2:]
         weight_ref, mass_ref, out_ref, stats_ref, refs = *refs[:4], refs[4:]
-        held, held_weight, sems, piece_sems = refs
+        kept_ref, near_ref, far_ref, held, held_weight, sems, piece_sems, cols_sems = refs
         chip, core = place_on_mesh()
+        data_pos = lax.axis_index("dp")
+        stores = []
+
+        def store(h, group, target):
+            column = pl.multiple_of(group * quarter, quarter)
+            stores.append(
+                pltpu.make_async_copy(
+                    piece_refs[h].at[:, pl.ds(column, quarter)], target, cols_sems.at[len(stores)]
+                )
+            )
+            stores[-1].start()
+
         loads = []
         for h in range(2):
             for j in range(chips):
@@ -139,6 +152,11 @@
             )
         for k in range(ahead):
             copies[k].start()
+        for h in range(2):
+            part = pl.ds(pl.multiple_of((core ^ h) * half, half), half)
+            store(h, data_pos ^ (core + 1), near_ref.at[part])
+            store(h, data_pos, kept_ref.at[part])
+        store(0, data_pos ^ 3, far_ref)
         for load in loads:
             load.wait()
         for k in range(parts):
@@ -147,64 +165,62 @@
                 copies[k + ahead].start()
             if (k + 1) % ahead == 0:
                 some = slice((k + 1 - ahead) * step, (k + 1) * step)
-                out_ref[:, some] = lax.dot_general(
+                values = lax.dot_general(
                     held[...],
                     held_weight[some],
                     (((1,), (1,)), ((), ())),
                     preferred_element_type=jnp.float32,
                 )
-        top = jnp.max(out_ref[...], axis=1, keepdims=True)
-        total = jnp.sum(jnp.exp(out_ref[...] - top), axis=1, keepdims=True)
+                out_ref[:, some] = values
+                part_top = jnp.max(values, axis=1, keepdims=True)
+                part_total = jnp.sum(jnp.exp(values - part_top), axis=1, keepdims=True)
+                if k + 1 == ahead:
+                    top, total = part_top, part_total
+                else:
+                    new_top = jnp.maximum(top, part_top)
+                    total = total * jnp.exp(top - new_top)
+                    total = total + part_total * jnp.exp(part_top - new_top)
+                    top = new_top
         stats_ref[0:1] = as_row(top)
         stats_ref[1:2] = as_row(total)
         stats_ref[2:3] = mass_ref[...]
         stats_ref[3:8] = jnp.zeros((5, tokens), jnp.float32)
-
+        for one in stores:
+            one.wait()
+
+    both = jax.ShapeDtypeStruct((tokens, quarter), own.dtype)
     ops = [own, other, in_hbm(weight), mass]
     return pl.pallas_call(
         body,
         out_shape=[
             jax.ShapeDtypeStruct((tokens, vocab_rows), jnp.float32),
             jax.ShapeDtypeStruct((8, tokens), jnp.float32),
+            both,
+            both,
+            jax.ShapeDtypeStruct((half, quarter), own.dtype),
         ],
         in_specs=[ANY] * 3 + [WHOLE],
-        out_specs=[WHOLE, WHOLE],
+        out_specs=[WHOLE, WHOLE] + [ANY] * 3,
         scratch_shapes=[
             pltpu.VMEM((tokens, width), weight.dtype),
             pltpu.VMEM(weight.shape, weight.dtype),
             pltpu.SemaphoreType.DMA((parts,)),
             pltpu.SemaphoreType.DMA((2 * chips,)),
+            pltpu.SemaphoreType.DMA((5,)),
         ],
         compiler_params=pltpu.CompilerParams(vmem_limit_bytes=32 * MIB),
         cost_estimate=cost(2 * tokens * weight.size, ops),
     )(*ops)
 
 
-def cut_columns(own, quarter):
-    groups = own.shape[1] // quarter
-
-    def body(own_ref, *refs):
-        outs, sems = refs[:groups], refs[groups]
-        data_pos = lax.axis_index("dp")
-        moves = []
-        for r in range(groups):
-            column = pl.multiple_of((data_pos ^ r) * quarter, quarter)
-            moves.append(
-                pltpu.make_async_copy(own_ref.at[:, pl.ds(column, quarter)], outs[r], sems.at[r])
-            )
-            moves[r].start()
-        for move in moves:
-            move.wait()
-
-    return pl.pallas_call(
-        body,
-        out_shape=[jax.ShapeDtypeStruct((own.shape[0], quarter), own.dtype)] * groups,
-        in_specs=[ANY],
-        out_specs=[ANY] * groups,
-        scratch_shapes=[pltpu.SemaphoreType.DMA((groups,))],
-        compiler_params=pltpu.CompilerParams(vmem_limit_bytes=MIB),
-        cost_estimate=cost(0, (own,)),
-    )(own)
+def swap_by_core(x):
+    count = lax.axis_size("vocab")
+    pairs = [
+        (d * count + v, (d ^ (v % 2 + 1)) * count + v)
+        for d in range(lax.axis_size("dp"))
+        for v in range(count)
+    ]
+    return lax.ppermute(x, ("dp", "vocab"), pairs)
 
 
 def merge_pair(a, b, after=()):
@@ -275,7 +291,7 @@
     )(slots, listed, *mine, sibling)
 
 
-def logit_grads(logits, stats, mine, sibling, weight, cols, parts=8):
+def logit_grads(logits, stats, mine, sibling, weight, cols, after, parts=8):
     chips, rows, vocab_rows = sibling.shape
     tokens = logits.shape[0]
     half = chips * rows
@@ -287,12 +303,13 @@
         stats_refs, refs = refs[:count], refs[count:]
         mine_refs, refs = refs[:chips], refs[chips:]
         sibling_ref, weight_ref, refs = refs[0], refs[1], refs[2:]
-        cols_refs, refs = refs[: len(cols)], refs[len(cols) :]
+        cols_refs, refs = refs[: len(cols)], refs[len(cols) + len(after) :]
         out_ref, own_ref, other_ref, stacked_ref, held_weight, columns, sems, cols_sems = refs
-        moves = [
-            pltpu.make_async_copy(ref, stacked_ref.at[r], cols_sems.at[r])
-            for r, ref in enumerate(cols_refs)
-        ]
+        moves = []
+        for r, ref in enumerate(cols_refs):
+            at = sum(x.shape[0] for x in cols[:r])
+            target = stacked_ref.at[at : at + cols[r].shape[0]]
+            moves.append(pltpu.make_async_copy(ref, target, cols_sems.at[r]))
         copies = []
         for k in range(parts):
             some = pl.ds(k * step, step)
@@ -335,9 +352,9 @@
             jax.ShapeDtypeStruct((tokens, vocab_rows), jnp.bfloat16),
             jax.ShapeDtypeStruct((half, width), jnp.float32),
             jax.ShapeDtypeStruct((half, width), jnp.bfloat16),
-            jax.ShapeDtypeStruct((len(cols), *cols[0].shape), cols[0].dtype),
+            jax.ShapeDtypeStruct((sum(x.shape[0] for x in cols), cols[0].shape[1]), cols[0].dtype),
         ],
-        in_specs=[WHOLE] * (len(ops) - 1) + [ANY] * (1 + len(cols)),
+        in_specs=[WHOLE] * (len(ops) - 1) + [ANY] * (1 + len(cols) + len(after)),
         out_specs=[WHOLE] * 3 + [ANY],
         scratch_shapes=[
             pltpu.VMEM(weight.shape, weight.dtype),
@@ -347,31 +364,81 @@
         ],
         compiler_params=pltpu.CompilerParams(vmem_limit_bytes=32 * MIB),
         cost_estimate=cost(2 * weight.size * tokens, ops),
-    )(*ops, *cols)
-
-
-def weight_grad(grads, own_cols, other_cols, after):
-    flat = [part for parts in grads for part in parts]
-    vocab_rows = flat[0].shape[1]
-    columns = own_cols.shape[2]
-    tokens = sum(part.shape[0] for part in flat)
+    )(*ops, *cols, *after)
+
+
+def ordered_columns(kept, mine, sibling):
+    tokens = kept.shape[0]
+    half = tokens // 2
+    first = place_on_mesh()[1] == 0
+    a, b = mine[:tokens], sibling[:tokens]
+    cols = []
+    for group in (kept[...], jnp.where(first, a, b), jnp.where(first, b, a)):
+        low, high = group[:half], group[half:]
+        cols += [jnp.where(first, low, high), jnp.where(first, high, low)]
+    return jnp.concatenate(cols)
+
+
+def weight_grad_part(grads, kept, mine, sibling):
+    vocab_rows = grads[0].shape[1]
+    tokens, columns = kept.shape
 
     def body(*refs):
-        rows = jnp.concatenate([ref[...] for ref in refs[: len(flat)]])
-        cols_refs = refs[len(flat) : len(flat) + 2]
-        cols = jnp.concatenate([ref[r] for r in range(own_cols.shape[0]) for ref in cols_refs])
-        refs[-1][...] = lax.dot_general(
-            rows, cols, (((0,), (0,)), ((), ())), preferred_element_type=jnp.float32
-        ).astype(refs[-1].dtype)
-
-    ops = [*flat, own_cols, other_cols]
+        kept_ref, mine_ref, sibling_ref, out_ref = refs[len(grads) :]
+        out_ref[...] = lax.dot_general(
+            jnp.concatenate([ref[...] for ref in refs[: len(grads)]]),
+            ordered_columns(kept_ref, mine_ref, sibling_ref),
+            (((0,), (0,)), ((), ())),
+            preferred_element_type=jnp.float32,
+        )
+
+    ops = [*grads, kept, mine, sibling]
+    return pl.pallas_call(
+        body,
+        out_shape=jax.ShapeDtypeStruct((vocab_rows, columns), jnp.float32),
+        in_specs=[WHOLE] * len(ops),
+        out_specs=WHOLE,
+        compiler_params=pltpu.CompilerParams(vmem_limit_bytes=24 * MIB),
+        cost_estimate=cost(6 * tokens * vocab_rows * columns, ops),
+    )(*ops)
+
+
+def weight_grad_rest(partial, grads, mine, sibling, after, parts=4):
+    vocab_rows, columns = partial.shape
+    step = vocab_rows // parts
+    count = sum(x.shape[0] for x in grads)
+    start = mine.shape[0] - count // 2
+
+    def body(partial_ref, *refs):
+        grads_refs, refs = refs[: len(grads)], refs[len(grads) :]
+        mine_ref, sibling_ref, refs = refs[0], refs[1], refs[2 + len(after) :]
+        out_ref, done, sems = refs
+        stores = []
+        rows = jnp.concatenate([ref[...] for ref in grads_refs])
+        cols = jnp.concatenate([mine_ref[start:], sibling_ref[start:]])
+        for k in range(parts):
+            some = slice(k * step, (k + 1) * step)
+            term = lax.dot_general(
+                rows[:, some], cols, (((0,), (0,)), ((), ())), preferred_element_type=jnp.float32
+            )
+            done[some] = (partial_ref[some] + term).astype(done.dtype)
+            stores.append(pltpu.make_async_copy(done.at[some], out_ref.at[some], sems.at[k]))
+            stores[k].start()
+        for store in stores:
+            store.wait()
+
+    ops = [partial, *grads, mine, sibling]
     return pl.pallas_call(
         body,
         out_shape=jax.ShapeDtypeStruct((vocab_rows, columns), jnp.bfloat16),
         in_specs=[WHOLE] * len(ops) + [ANY] * len(after),
-        out_specs=WHOLE,
-        compiler_params=pltpu.CompilerParams(vmem_limit_bytes=24 * MIB),
-        cost_estimate=cost(2 * tokens * vocab_rows * columns, ops),
+        out_specs=ANY,
+        scratch_shapes=[
+            pltpu.VMEM(partial.shape, jnp.bfloat16),
+            pltpu.SemaphoreType.DMA((parts,)),
+        ],
+        compiler_params=pltpu.CompilerParams(vmem_limit_bytes=16 * MIB),
+        cost_estimate=cost(2 * count * vocab_rows * columns, ops),
     )(*ops, *after)
 
 
@@ -418,10 +485,11 @@
     tiles = between_chips(placed)
 
     mass = jnp.sum(teacher, axis=1, dtype=jnp.float32)[None, :]
-    logits, stats = logits_and_stats(own, other, rows, weight, mass)
-
-    cols = cut_columns(own, width // data_size)
-    own_cols = [cols[0]] + [swap(cols[r], "dp", r) for r in range(1, data_size)]
+
+    logits, stats, kept, near, far = logits_and_stats(
+        own, other, rows, weight, mass, width // data_size
+    )
+    own_cols = [swap_by_core(near), swap(far, "dp", data_size - 1)]
 
     stats = merge_pair(stats, swap(stats, "vocab", 1))
     bits = 2
@@ -430,8 +498,10 @@
         bits *= 2
     all_stats = [stats, swap(stats, "vocab", bits)]
     other_tiles = swap(siblings_part_after(tiles, rows, [stats]), "vocab", 1)
+    spare = other_tiles[0, :TILE_ROWS, :BLK]
+    spare = swap(spare, "vocab", 1)
     grad_logits, share, rest, own_cols = logit_grads(
-        logits, all_stats, tiles, other_tiles, weight, own_cols
+        logits, all_stats, tiles, other_tiles, weight, own_cols, [spare]
     )
     other_cols = swap(own_cols, "vocab", 1)
 
@@ -443,19 +513,14 @@
             sent = swap(shares[base + count].astype(jnp.bfloat16), "vocab", 2 * count)
             shares[base] = shares[base] + sent.astype(jnp.float32)
         count *= 2
+    grad_hidden = shares[0].astype(jnp.bfloat16)
 
     middle = grad_logits.shape[0] // 2
-    all_grads = [[grad_logits]]
-    bits = 1
-    while bits < data_size:
-        known = [jnp.concatenate(parts) if len(parts) > 1 else parts[0] for parts in all_grads]
-        all_grads.append([swap(grad_logits, "dp", bits)])
-        for r in range(1, bits):
-            near, far = known[r], all_grads[bits][0]
-            all_grads.append([swap(near[:middle], "dp", bits), swap(far[middle:], "dp", r)])
-        bits *= 2
-    grad_weight = weight_grad(all_grads, own_cols, other_cols, [shares[0]])
-    return (shares[0].astype(jnp.bfloat16), grad_weight)
+    near, far = swap(grad_logits, "dp", 1), swap(grad_logits, "dp", 2)
+    last = [swap(near[:middle], "dp", 2), swap(far[middle:], "dp", 1)]
+    partial = weight_grad_part([grad_logits, near, far], kept, own_cols, other_cols)
+    grad_weight = weight_grad_rest(partial, last, own_cols, other_cols, [grad_hidden])
+    return (grad_hidden, grad_weight)
 
 
 def solution(mesh):
@@ -463,8 +528,10 @@
 
     def run(hidden, weight, teacher, block_ids):
         rows = hidden.shape[0] // (mesh.shape["dp"] * mesh.shape["vocab"])
-        paired = all(size & (size - 1) == 0 for size in mesh.shape.values())
-        form = shards if paired and rows % TILE_ROWS == 0 else plain_shards
+        count = mesh.shape["vocab"]
+        fits = count & (count - 1) == 0 and count > 2 and mesh.shape["dp"] == CORES**2
+        fits = fits and rows % TILE_ROWS == 0 and BLK % rows == 0 and count * rows % (2 * BLK) == 0
+        form = shards if fits else plain_shards
         return jax.shard_map(
             form,
             mesh=mesh,

time: 99.8 us -> 94.4 us (0.946)
  waiting for transfers between devices: 47.2 us -> 43 us
    ppermute x27 -> x26, waiting for transfers between devices: 47.2 us -> 43 us  [swap(): lax.ppermute(x, axis, [(i, i ^ bits) for i in range(lax.axis_size(axis))])]
    ppermute x27 -> x26, starting transfers between devices: 31.6 us -> 29.6 us  [swap(): lax.ppermute(x, axis, [(i, i ^ bits) for i in range(lax.axis_size(axis))])]
    ppermute x0 -> x1, starting transfers between devices: none -> 1.72 us  [swap_by_core(): return lax.ppermute(x, ('dp', 'vocab'), pairs)]
  transfers between devices with their start and end apart: 27 -> 27, of which waited for: 14 -> 14; matrix products, arithmetic and copies ran while one was open for 3% -> 3% of each run, Pallas kernels for 7% -> 9%
where the time goes in v4:
time: 94.4 us; the launch traced here: 94.2 us
  waiting for transfers between devices  43 us (46%)
  starting transfers between devices  31.3 us (33%)
  Pallas kernels  14.9 us (16%)
  local copies, waits for them, and re-layouts  2.45 us (3%)
  other arithmetic  1.61 us (2%)
    ppermute x26, waiting for transfers between devices, swap(): lax.ppermute(x, axis, [(i, i ^ bits) for i in range(lax.axis_size(axis))])  43 us
    ppermute x26, starting transfers between devices, swap(): lax.ppermute(x, axis, [(i, i ^ bits) for i in range(lax.axis_size(axis))])  29.6 us
    pallas_call x1, Pallas kernels, logits_and_stats(): pl.pallas_call(body, out_shape=[jax.ShapeDtypeStruct((tokens, vocab_rows)...  5.44 us
    pallas_call x1, Pallas kernels, logit_grads(): pl.pallas_call(body, out_shape=[jax.ShapeDtypeStruct((tokens, vocab_rows)...  4.84 us
  transfers between devices with their start and end apart: 27, of which 14 were waited for; matrix products, arithmetic and copies ran while one was open for 3% of the time, Pallas kernels for 9%

profile of v4, /device:TPU:0, one launch (start us, length us, event | category | flops | bytes accessed | tf_op | source)
XLA Modules:
  0.0 94.2 jit_solution(12639856637786757578)
XLA Ops:
  0.6 0.0 copy-start
  0.7 3.1 %collective-permute-start = (bf16[32,4096]{1,0:T(8,128)(2,1)}, bf16[32,4096]{1,0:T(8,128)(2,1)S(1)}, u32[]{:S(2)}, u32[]{:S(2)}) collective-permute-start(bf16[32,4096]{1,0:T(8,128)(2,1)} %param.4), channel_id=1, source_target_pairs={{0,2},{1,3},{2,0},{3,1},{4,6},{5,7},{6,4},{7,5},{8,10},{9,11},{10,... | collective-permute-start | bytes 786440 | tf_op jit(solution)/shard_map/ppermute | solution.py:65
  3.7 2.6 %collective-permute-start.1 = (bf16[32,4096]{1,0:T(8,128)(2,1)}, bf16[32,4096]{1,0:T(8,128)(2,1)S(1)}, u32[]{:S(2)}, u32[]{:S(2)}) collective-permute-start(bf16[32,4096]{1,0:T(8,128)(2,1)} %param.4), channel_id=1, source_target_pairs={{0,4},{1,5},{2,6},{3,7},{4,0},{5,1},{6,2},{7,3},{8,12},{9,13},{10,... | collective-permute-start | bytes 786440 | tf_op jit(solution)/shard_map/ppermute | solution.py:65
  6.3 1.1 %constant_dynamic-slice_fusion.1 = (bf16[64,1024]{1,0:T(8,128)(2,1)S(1)}, bf16[64,1024]{1,0:T(8,128)(2,1)S(1)}, bf16[64,1024]{1,0:T(8,128)(2,1)S(1)}, bf16[64,1024]{1,0:T(8,128)(2,1)S(1)}) fusion(bf16[256,1024]{1,0:T(8,128)(2,1)} %param.6, s32[]{:T(128)S(6)} %select_n.56, s32[]{:T(128)S(6)} %select_n.55, s32[]{:T(128)S(6)} %select_n.54, s32[]{:T(128)S(6)} %select_n.53), kind=kLoop, calls=%fused_computation.21 | loop fusion | bytes 1048592 | tf_op jit(solution)/shard_map/dynamic_slice | solution.py:468
  7.5 0.5 collective-permute-start.3
  8.0 0.0 collective-permute-start.4
  8.0 3.9 %collective-permute-start.5 = (bf16[64,1024]{1,0:T(8,128)(2,1)S(1)}, bf16[64,1024]{1,0:T(8,128)(2,1)S(1)}, u32[]{:S(2)}, u32[]{:S(2)}) collective-permute-start(bf16[64,1024]{1,0:T(8,128)(2,1)S(1)} %get-tuple-element.50), channel_id=1, source_target_pairs={{0,6},{1,7},{2,4},{3,5},{4,2},{5,3},{6,0},{7,1},{8,14},{9,15},{10,... | collective-permute-start | bytes 393224 | tf_op jit(solution)/shard_map/ppermute | solution.py:65
  11.9 0.1 stack.50
  12.0 7.8 %collective-permute-done.1 = bf16[32,4096]{1,0:T(8,128)(2,1)S(1)} collective-permute-done((bf16[32,4096]{1,0:T(8,128)(2,1)}, bf16[32,4096]{1,0:T(8,128)(2,1)S(1)}, u32[]{:S(2)}, u32[]{:S(2)}) %collective-permute-start.1) | collective-permute-done | bytes 262176 | tf_op jit(solution)/shard_map/ppermute | solution.py:65
  19.8 0.2 collective-permute-start.2
  20.0 0.1 iota_add_fusion
  20.1 0.1 add.98
  20.2 1.0 %collective-permute-done.3.refs_1_ = bf16[64,1024]{1,0:T(8,128)(2,1)S(1)} collective-permute-done((bf16[64,1024]{1,0:T(8,128)(2,1)S(1)}, bf16[64,1024]{1,0:T(8,128)(2,1)S(1)}, u32[]{:S(2)}, u32[]{:S(2)}) %collective-permute-start.3) | collective-permute-done | bytes 131104 | tf_op jit(solution)/shard_map/ppermute | solution.py:65
  21.2 6.9 %collective-permute-done.4.refs_2_ = bf16[64,1024]{1,0:T(8,128)(2,1)S(1)} collective-permute-done((bf16[64,1024]{1,0:T(8,128)(2,1)S(1)}, bf16[64,1024]{1,0:T(8,128)(2,1)S(1)}, u32[]{:S(2)}, u32[]{:S(2)}) %collective-permute-start.4) | collective-permute-done | bytes 131104 | tf_op jit(solution)/shard_map/ppermute | solution.py:65
  28.1 0.0 collective-permute-done.5.refs_3_
  28.1 0.0 collective-permute-done
  28.1 1.8 %collective-permute-done.2 = bf16[32,4096]{1,0:T(8,128)(2,1)S(1)} collective-permute-done((bf16[32,4096]{1,0:T(8,128)(2,1)S(1)}, bf16[32,4096]{1,0:T(8,128)(2,1)S(1)}, u32[]{:S(2)}, u32[]{:S(2)}) %collective-permute-start.2) | collective-permute-done | bytes 262176 | tf_op jit(solution)/shard_map/ppermute | solution.py:65
  29.9 1.0 %constant_dynamic-update-slice_fusion.3 = bf16[128,4096]{1,0:T(8,128)(2,1)S(1)} fusion(bf16[32,4096]{1,0:T(8,128)(2,1)} %param.4), kind=kLoop, calls=%fused_computation.17 | loop fusion | bytes 524288
  31.0 0.1 collective-permute-start.6
  31.1 0.1 convert_reduce_fusion
  31.2 0.7 compare_reduce_fusion.1
  32.0 0.6 collective-permute-start.10
  32.6 0.2 compare_reduce_fusion
  32.8 1.3 %collective-permute-done.10.refs_4_ = bf16[4,32,1024]{2,1,0:T(8,128)(2,1)S(1)} collective-permute-done((bf16[4,32,1024]{2,1,0:T(8,128)(2,1)S(1)}, bf16[4,32,1024]{2,1,0:T(8,128)(2,1)S(1)}, u32[]{:S(2)}, u32[]{:S(2)}) %collective-permute-start.10) | collective-permute-done | bytes 262176 | tf_op jit(solution)/shard_map/ppermute | solution.py:65
  34.1 1.0 %shard_map.62 = (bf16[64,1024]{1,0:T(8,128)(2,1)S(1)}, bf16[64,1024]{1,0:T(8,128)(2,1)S(1)}, bf16[64,1024]{1,0:T(8,128)(2,1)S(1)}, bf16[64,1024]{1,0:T(8,128)(2,1)S(1)}) custom-call(s32[64]{0:T(128)S(1)} %fusion.3.slots_ref, s32[64]{0:T(128)S(1)} %convert_element_type.27.listed_ref, bf16[64,1024]{1,0:T(8,128)(2,1)S(1)} %get-tuple-element.31.refs_0_, ...), custom_call_target="tpu_custom_call" | custom-call | bytes 524288 | tf_op jit(solution)/shard_map/pallas_call | solution.py:283
  35.1 1.9 %collective-permute-start.11 = (bf16[64,1024]{1,0:T(8,128)(2,1)S(1)}, bf16[64,1024]{1,0:T(8,128)(2,1)S(1)}, u32[]{:S(2)}, u32[]{:S(2)}) collective-permute-start(bf16[64,1024]{1,0:T(8,128)(2,1)S(1)} %get-tuple-element.36), channel_id=1, source_target_pairs={{0,2},{1,3},{2,0},{3,1},{4,6},{5,7},{6,4},{7,5},{8,10},{9,11},{10,... | collective-permute-start | bytes 393224 | tf_op jit(solution)/shard_map/ppermute | solution.py:65
  37.0 2.5 %collective-permute-start.12 = (bf16[64,1024]{1,0:T(8,128)(2,1)S(1)}, bf16[64,1024]{1,0:T(8,128)(2,1)S(1)}, u32[]{:S(2)}, u32[]{:S(2)}) collective-permute-start(bf16[64,1024]{1,0:T(8,128)(2,1)S(1)} %get-tuple-element.37), channel_id=1, source_target_pairs={{0,4},{1,5},{2,6},{3,7},{4,0},{5,1},{6,2},{7,3},{8,12},{9,13},{10,... | collective-permute-start | bytes 393224 | tf_op jit(solution)/shard_map/ppermute | solution.py:65
  39.5 0.1 collective-permute-start.13
  39.6 5.4 %shard_map.59 = (f32[256,1024]{1,0:T(8,128)S(1)}, f32[8,256]{1,0:T(8,128)S(1)}, bf16[256,1024]{1,0:T(8,128)(2,1)S(1)}, bf16[256,1024]{1,0:T(8,128)(2,1)S(1)}, bf16[128,1024]{1,0:T(8,128)(2,1)S(1)}) custom-call(bf16[128,4096]{1,0:T(8,128)(2,1)S(1)} %constant_dynamic-update-slice_fusion.refs_0_, bf16[128,4096]{1,0:T(8,128)(2,1)S(1)} %collective-permute-done.6.refs_1_, ...), custom_call_target="tpu_custom_call" | custom-call | flops 2147483648 | bytes 10486272 | tf_op jit(solution)/shard_map/pallas_call | solution.py:193
  45.0 1.7 %collective-permute-start.15 = (bf16[256,1024]{1,0:T(8,128)(2,1)S(1)}, bf16[256,1024]{1,0:T(8,128)(2,1)S(1)}, u32[]{:S(2)}, u32[]{:S(2)}) collective-permute-start(bf16[256,1024]{1,0:T(8,128)(2,1)S(1)} %get-tuple-element.39), channel_id=1, source_target_pairs={{0,8},{1,17},{2,10},{3,19},{4,12},{5,21},{6,14},{7,23},{8,0},{9,25... | collective-permute-start | bytes 1572872 | tf_op jit(solution)/shard_map/ppermute | solution.py:223
  46.7 1.2 %collective-permute-done.7.b_ref = f32[8,256]{1,0:T(8,128)S(1)} collective-permute-done((f32[8,256]{1,0:T(8,128)S(1)}, f32[8,256]{1,0:T(8,128)S(1)}, u32[]{:S(2)}, u32[]{:S(2)}) %collective-permute-start.7) | collective-permute-done | bytes 8224 | tf_op jit(solution)/shard_map/ppermute | solution.py:65
  47.9 0.8 collective-permute-start.8
  48.8 2.9 %collective-permute-done.8.b_ref = f32[8,256]{1,0:T(8,128)S(1)} collective-permute-done((f32[8,256]{1,0:T(8,128)S(1)}, f32[8,256]{1,0:T(8,128)S(1)}, u32[]{:S(2)}, u32[]{:S(2)}) %collective-permute-start.8) | collective-permute-done | bytes 8224 | tf_op jit(solution)/shard_map/ppermute | solution.py:65
  51.7 0.0 collective-permute-done.11.refs_1_.refs_3_
  51.7 0.0 collective-permute-done.13.refs_3_.refs_5_
  51.7 0.1 collective-permute-start.14
  51.8 1.6 %collective-permute-start.16 = (bf16[128,1024]{1,0:T(8,128)(2,1)S(1)}, bf16[128,1024]{1,0:T(8,128)(2,1)S(1)}, u32[]{:S(2)}, u32[]{:S(2)}) collective-permute-start(bf16[128,1024]{1,0:T(8,128)(2,1)S(1)} %get-tuple-element.40), channel_id=1, source_target_pairs={{0,24},{8,16},{16,8},{24,0},{1,25},{9,17},{17,9},{25,1},{2,26},{10... | collective-permute-start | bytes 786440 | tf_op jit(solution)/shard_map/ppermute | solution.py:65
  53.4 2.4 %collective-permute-start.9 = (f32[8,256]{1,0:T(8,128)S(1)}, f32[8,256]{1,0:T(8,128)S(1)}, u32[]{:S(2)}, u32[]{:S(2)}) collective-permute-start(f32[8,256]{1,0:T(8,128)S(1)} %shard_map.61.refs_4_.refs_0_), channel_id=1, source_target_pairs={{0,4},{1,5},{2,6},{3,7},{4,0},{5,1},{6,2},{7,3},{8,12},{9,13},{10,... | collective-permute-start | bytes 24584 | tf_op jit(solution)/shard_map/ppermute | solution.py:65
  55.8 0.0 collective-permute-start.17
  55.8 2.1 %collective-permute-done.9.refs_1_ = f32[8,256]{1,0:T(8,128)S(1)} collective-permute-done((f32[8,256]{1,0:T(8,128)S(1)}, f32[8,256]{1,0:T(8,128)S(1)}, u32[]{:S(2)}, u32[]{:S(2)}) %collective-permute-start.9) | collective-permute-done | bytes 8224 | tf_op jit(solution)/shard_map/ppermute | solution.py:65
  57.9 3.5 %collective-permute-done.16.refs_9_ = bf16[128,1024]{1,0:T(8,128)(2,1)S(1)} collective-permute-done((bf16[128,1024]{1,0:T(8,128)(2,1)S(1)}, bf16[128,1024]{1,0:T(8,128)(2,1)S(1)}, u32[]{:S(2)}, u32[]{:S(2)}) %collective-permute-start.16) | collective-permute-done | bytes 262176 | tf_op jit(solution)/shard_map/ppermute | solution.py:65
  61.4 0.0 collective-permute-done.17.refs_10_
  61.4 0.0 collective-permute-done.15.refs_8_
  61.4 4.8 %shard_map.64 = (bf16[256,1024]{1,0:T(8,128)(2,1)S(1)}, f32[128,4096]{1,0:T(8,128)S(1)}, bf16[128,4096]{1,0:T(8,128)(2,1)S(1)}, bf16[384,1024]{1,0:T(8,128)(2,1)S(1)}) custom-call(f32[256,1024]{1,0:T(8,128)S(1)} %get-tuple-element.28.logits_ref, f32[8,256]{1,0:T(8,128)S(1)} %shard_map.61.refs_4_.refs_0_, f32[8,256]{1,0:T(8,128)S(1)} %collective-permute-done.9.refs_1_, ...), custom_call_target="tpu_custom_call" | custom-call | flops 2147483648 | bytes 9707520 | tf_op jit(solution)/shard_map/pallas_call | solution.py:349
  66.3 0.1 collective-permute-start.18
  66.4 2.6 %collective-permute-done.18 = bf16[128,4096]{1,0:T(8,128)(2,1)S(1)} collective-permute-done((bf16[128,4096]{1,0:T(8,128)(2,1)S(1)}, bf16[128,4096]{1,0:T(8,128)(2,1)S(1)}, u32[]{:S(2)}, u32[]{:S(2)}) %collective-permute-start.18) | collective-permute-done | bytes 1048608 | tf_op jit(solution)/shard_map/ppermute | solution.py:65
  69.0 0.3 fusion.8
  69.4 0.8 collective-permute-start.20
  70.2 1.2 %collective-permute-start.22 = (bf16[256,1024]{1,0:T(8,128)(2,1)S(1)}, bf16[256,1024]{1,0:T(8,128)(2,1)S(1)}, u32[]{:S(2)}, u32[]{:S(2)}) collective-permute-start(bf16[256,1024]{1,0:T(8,128)(2,1)S(1)} %get-tuple-element.43.refs_0_), channel_id=1, source_target_pairs={{0,8},{8,0},{16,24},{24,16},{1,9},{9,1},{17,25},{25,17},{2,10},{10... | collective-permute-start | bytes 1572872 | tf_op jit(solution)/shard_map/ppermute | solution.py:65
  71.4 1.5 %collective-permute-start.23 = (bf16[256,1024]{1,0:T(8,128)(2,1)S(1)}, bf16[256,1024]{1,0:T(8,128)(2,1)S(1)}, u32[]{:S(2)}, u32[]{:S(2)}) collective-permute-start(bf16[256,1024]{1,0:T(8,128)(2,1)S(1)} %get-tuple-element.43.refs_0_), channel_id=1, source_target_pairs={{0,16},{8,24},{16,0},{24,8},{1,17},{9,25},{17,1},{25,9},{2,18},{10... | collective-permute-start | bytes 1572872 | tf_op jit(solution)/shard_map/ppermute | solution.py:65
  73.0 0.0 collective-permute-start.24
  73.0 0.6 collective-permute-start.19
  73.5 5.1 %collective-permute-done.20 = bf16[32,4096]{1,0:T(8,128)(2,1)S(1)} collective-permute-done((bf16[32,4096]{1,0:T(8,128)(2,1)S(1)}, bf16[32,4096]{1,0:T(8,128)(2,1)S(1)}, u32[]{:S(2)}, u32[]{:S(2)}) %collective-permute-start.20) | collective-permute-done | bytes 262176 | tf_op jit(solution)/shard_map/ppermute | solution.py:65
  78.7 2.2 %collective-permute-start.21 = (bf16[32,4096]{1,0:T(8,128)(2,1)S(1)}, bf16[32,4096]{1,0:T(8,128)(2,1)S(1)}, u32[]{:S(2)}, u32[]{:S(2)}) collective-permute-start(bf16[32,4096]{1,0:T(8,128)(2,1)S(1)} %fusion), channel_id=1, source_target_pairs={{0,4},{1,5},{2,6},{3,7},{4,0},{5,1},{6,2},{7,3},{8,12},{9,13},{10,... | collective-permute-start | bytes 786440 | tf_op jit(solution)/shard_map/ppermute | solution.py:65
  80.8 3.1 %collective-permute-done.22.refs_1_ = bf16[256,1024]{1,0:T(8,128)(2,1)S(1)} collective-permute-done((bf16[256,1024]{1,0:T(8,128)(2,1)S(1)}, bf16[256,1024]{1,0:T(8,128)(2,1)S(1)}, u32[]{:S(2)}, u32[]{:S(2)}) %collective-permute-start.22) | collective-permute-done | bytes 524320 | tf_op jit(solution)/shard_map/ppermute | solution.py:65
  83.9 1.6 %collective-permute-start.25 = (bf16[128,1024]{1,0:T(8,128)(2,1)S(1)}, bf16[128,1024]{1,0:T(8,128)(2,1)S(1)}, u32[]{:S(2)}, u32[]{:S(2)}) collective-permute-start(bf16[128,1024]{1,0:T(8,128)(2,1)S(1)} %slice.35), channel_id=1, source_target_pairs={{0,16},{8,24},{16,0},{24,8},{1,17},{9,25},{17,1},{25,9},{2,18},{10... | collective-permute-start | bytes 786440 | tf_op jit(solution)/shard_map/ppermute | solution.py:65
  85.5 1.3 %collective-permute-start.26 = (bf16[128,1024]{1,0:T(8,128)(2,1)S(1)}, bf16[128,1024]{1,0:T(8,128)(2,1)S(1)}, u32[]{:S(2)}, u32[]{:S(2)}) collective-permute-start(bf16[128,1024]{1,0:T(8,128)(2,1)S(1)} %slice.36), channel_id=1, source_target_pairs={{0,8},{8,0},{16,24},{24,16},{1,9},{9,1},{17,25},{25,17},{2,10},{10... | collective-permute-start | bytes 786440 | tf_op jit(solution)/shard_map/ppermute | solution.py:65
  86.8 0.0 collective-permute-done.24.refs_5_.refs_3_
  86.8 1.9 %shard_map.65.partial_ref = f32[1024,1024]{1,0:T(8,128)S(1)} custom-call(bf16[256,1024]{1,0:T(8,128)(2,1)S(1)} %get-tuple-element.43.refs_0_, bf16[256,1024]{1,0:T(8,128)(2,1)S(1)} %collective-permute-done.22.refs_1_, bf16[256,1024]{1,0:T(8,128)(2,1)S(1)} %collective-permute-done.23.refs_2_, bf16[256,1024]{1,0:T(8,128)(2,1)S(1)} %get-tuple-element.44.refs_3_, ...), custom_call_target="tpu_custom_call" | custom-call | flops 1610612736 | bytes 3670016 | tf_op jit(solution)/shard_map/pallas_call | solution.py:396
  88.7 3.4 %collective-permute-done.21 = bf16[32,4096]{1,0:T(8,128)(2,1)S(1)} collective-permute-done((bf16[32,4096]{1,0:T(8,128)(2,1)S(1)}, bf16[32,4096]{1,0:T(8,128)(2,1)S(1)}, u32[]{:S(2)}, u32[]{:S(2)}) %collective-permute-start.21) | collective-permute-done | bytes 262176 | tf_op jit(solution)/shard_map/ppermute | solution.py:65
  92.1 0.1 fusion.2.refs_4_
  92.2 0.0 copy-start.1
  92.2 0.3 collective-permute-done.26.refs_1_
  92.5 1.7 %shard_map.66 = bf16[1024,1024]{1,0:T(8,128)(2,1)} custom-call(f32[1024,1024]{1,0:T(8,128)S(1)} %shard_map.65.partial_ref, bf16[128,1024]{1,0:T(8,128)(2,1)S(1)} %collective-permute-done.25.refs_0_, bf16[128,1024]{1,0:T(8,128)(2,1)S(1)} %collective-permute-done.26.refs_1_, bf16[384,1024]{1,0:T(8,128)(2,1)S(1)} %get-tuple-element.45.refs_4_.refs_2_, ...), custom_call_target="tpu_custom_call" | custom-call | flops 536870912 | bytes 4194304 | tf_op jit(solution)/shard_map/pallas_call | solution.py:431
  (29 shorter events, 0.4 us)
Async XLA Ops:
  0.6 19.6 %copy-start = (s32[2,64]{1,0:T(2,128)S(1)}, s32[2,64]{1,0:T(2,128)}, u32[]{:S(2)}) copy-start(s32[2,64]{1,0:T(2,128)} %param.7) | copy-start | bytes 1540
  0.6 30.4 %copy-start.2 = (bf16[256,1024]{1,0:T(8,128)(2,1)S(1)}, bf16[256,1024]{1,0:T(8,128)(2,1)}, u32[]{:S(2)}) copy-start(bf16[256,1024]{1,0:T(8,128)(2,1)} %param.6) | copy-start | bytes 1572868
  0.7 27.5 %collective-permute-start = (bf16[32,4096]{1,0:T(8,128)(2,1)}, bf16[32,4096]{1,0:T(8,128)(2,1)S(1)}, u32[]{:S(2)}, u32[]{:S(2)}) collective-permute-start(bf16[32,4096]{1,0:T(8,128)(2,1)} %param.4), channel_id=1, source_target_pairs={{0,2},{1,3},{2,0},{3,1},{4,6},{5,7},{6,4},{7,5},{8,10},{9,11},{10,... | collective-permute-start | bytes 786440 | tf_op jit(solution)/shard_map/ppermute | solution.py:65
  3.7 16.1 %collective-permute-start.1 = (bf16[32,4096]{1,0:T(8,128)(2,1)}, bf16[32,4096]{1,0:T(8,128)(2,1)S(1)}, u32[]{:S(2)}, u32[]{:S(2)}) collective-permute-start(bf16[32,4096]{1,0:T(8,128)(2,1)} %param.4), channel_id=1, source_target_pairs={{0,4},{1,5},{2,6},{3,7},{4,0},{5,1},{6,2},{7,3},{8,12},{9,13},{10,... | collective-permute-start | bytes 786440 | tf_op jit(solution)/shard_map/ppermute | solution.py:65
  7.5 13.7 %collective-permute-start.3 = (bf16[64,1024]{1,0:T(8,128)(2,1)S(1)}, bf16[64,1024]{1,0:T(8,128)(2,1)S(1)}, u32[]{:S(2)}, u32[]{:S(2)}) collective-permute-start(bf16[64,1024]{1,0:T(8,128)(2,1)S(1)} %get-tuple-element.52), channel_id=1, source_target_pairs={{0,2},{1,3},{2,0},{3,1},{4,6},{5,7},{6,4},{7,5},{8,10},{9,11},{10,... | collective-permute-start | bytes 393224 | tf_op jit(solution)/shard_map/ppermute | solution.py:65
  8.0 20.1 %collective-permute-start.4 = (bf16[64,1024]{1,0:T(8,128)(2,1)S(1)}, bf16[64,1024]{1,0:T(8,128)(2,1)S(1)}, u32[]{:S(2)}, u32[]{:S(2)}) collective-permute-start(bf16[64,1024]{1,0:T(8,128)(2,1)S(1)} %get-tuple-element.51), channel_id=1, source_target_pairs={{0,4},{1,5},{2,6},{3,7},{4,0},{5,1},{6,2},{7,3},{8,12},{9,13},{10,... | collective-permute-start | bytes 393224 | tf_op jit(solution)/shard_map/ppermute | solution.py:65
  8.0 20.1 %collective-permute-start.5 = (bf16[64,1024]{1,0:T(8,128)(2,1)S(1)}, bf16[64,1024]{1,0:T(8,128)(2,1)S(1)}, u32[]{:S(2)}, u32[]{:S(2)}) collective-permute-start(bf16[64,1024]{1,0:T(8,128)(2,1)S(1)} %get-tuple-element.50), channel_id=1, source_target_pairs={{0,6},{1,7},{2,4},{3,5},{4,2},{5,3},{6,0},{7,1},{8,14},{9,15},{10,... | collective-permute-start | bytes 393224 | tf_op jit(solution)/shard_map/ppermute | solution.py:65
  19.8 10.1 %collective-permute-start.2 = (bf16[32,4096]{1,0:T(8,128)(2,1)S(1)}, bf16[32,4096]{1,0:T(8,128)(2,1)S(1)}, u32[]{:S(2)}, u32[]{:S(2)}) collective-permute-start(bf16[32,4096]{1,0:T(8,128)(2,1)S(1)} %collective-permute-done.1), channel_id=1, source_target_pairs={{0,2},{1,3},{2,0},{3,1},{4,6},{5,7},{6,4},{7,5},{8,10},{9,11},{10,... | collective-permute-start | bytes 786440 | tf_op jit(solution)/shard_map/ppermute | solution.py:65
  31.0 8.6 %collective-permute-start.6 = (bf16[128,4096]{1,0:T(8,128)(2,1)S(1)}, bf16[128,4096]{1,0:T(8,128)(2,1)S(1)}, u32[]{:S(2)}, u32[]{:S(2)}) collective-permute-start(bf16[128,4096]{1,0:T(8,128)(2,1)S(1)} %constant_dynamic-update-slice_fusion.refs_0_), channel_id=1, source_target_pairs={{0,1},{1,0},{2,3},{3,2},{4,5},{5,4},{6,7},{7,6},{8,9},{9,8},{10,11... | collective-permute-start | bytes 3145736 | tf_op jit(solution)/shard_map/ppermute | solution.py:65
  32.0 2.1 %collective-permute-start.10 = (bf16[4,32,1024]{2,1,0:T(8,128)(2,1)S(1)}, bf16[4,32,1024]{2,1,0:T(8,128)(2,1)S(1)}, u32[]{:S(2)}, u32[]{:S(2)}) collective-permute-start(bf16[4,32,1024]{2,1,0:T(8,128)(2,1)S(1)} %pad_maximum_fusion), channel_id=1, source_target_pairs={{0,1},{1,0},{2,3},{3,2},{4,5},{5,4},{6,7},{7,6},{8,9},{9,8},{10,11... | collective-permute-start | bytes 786440 | tf_op jit(solution)/shard_map/ppermute | solution.py:65
  35.1 16.5 %collective-permute-start.11 = (bf16[64,1024]{1,0:T(8,128)(2,1)S(1)}, bf16[64,1024]{1,0:T(8,128)(2,1)S(1)}, u32[]{:S(2)}, u32[]{:S(2)}) collective-permute-start(bf16[64,1024]{1,0:T(8,128)(2,1)S(1)} %get-tuple-element.36), channel_id=1, source_target_pairs={{0,2},{1,3},{2,0},{3,1},{4,6},{5,7},{6,4},{7,5},{8,10},{9,11},{10,... | collective-permute-start | bytes 393224 | tf_op jit(solution)/shard_map/ppermute | solution.py:65
  37.0 14.7 %collective-permute-start.12 = (bf16[64,1024]{1,0:T(8,128)(2,1)S(1)}, bf16[64,1024]{1,0:T(8,128)(2,1)S(1)}, u32[]{:S(2)}, u32[]{:S(2)}) collective-permute-start(bf16[64,1024]{1,0:T(8,128)(2,1)S(1)} %get-tuple-element.37), channel_id=1, source_target_pairs={{0,4},{1,5},{2,6},{3,7},{4,0},{5,1},{6,2},{7,3},{8,12},{9,13},{10,... | collective-permute-start | bytes 393224 | tf_op jit(solution)/shard_map/ppermute | solution.py:65
  39.5 12.2 %collective-permute-start.13 = (bf16[64,1024]{1,0:T(8,128)(2,1)S(1)}, bf16[64,1024]{1,0:T(8,128)(2,1)S(1)}, u32[]{:S(2)}, u32[]{:S(2)}) collective-permute-start(bf16[64,1024]{1,0:T(8,128)(2,1)S(1)} %get-tuple-element.38), channel_id=1, source_target_pairs={{0,6},{1,7},{2,4},{3,5},{4,2},{5,3},{6,0},{7,1},{8,14},{9,15},{10,... | collective-permute-start | bytes 393224 | tf_op jit(solution)/shard_map/ppermute | solution.py:65
  45.0 16.4 %collective-permute-start.15 = (bf16[256,1024]{1,0:T(8,128)(2,1)S(1)}, bf16[256,1024]{1,0:T(8,128)(2,1)S(1)}, u32[]{:S(2)}, u32[]{:S(2)}) collective-permute-start(bf16[256,1024]{1,0:T(8,128)(2,1)S(1)} %get-tuple-element.39), channel_id=1, source_target_pairs={{0,8},{1,17},{2,10},{3,19},{4,12},{5,21},{6,14},{7,23},{8,0},{9,25... | collective-permute-start | bytes 1572872 | tf_op jit(solution)/shard_map/ppermute | solution.py:223
  46.7 1.2 %collective-permute-start.7 = (f32[8,256]{1,0:T(8,128)S(1)}, f32[8,256]{1,0:T(8,128)S(1)}, u32[]{:S(2)}, u32[]{:S(2)}) collective-permute-start(f32[8,256]{1,0:T(8,128)S(1)} %get-tuple-element.29.a_ref), channel_id=1, source_target_pairs={{0,1},{1,0},{2,3},{3,2},{4,5},{5,4},{6,7},{7,6},{8,9},{9,8},{10,11... | collective-permute-start | bytes 24584 | tf_op jit(solution)/shard_map/ppermute | solution.py:65
  47.9 3.7 %collective-permute-start.8 = (f32[8,256]{1,0:T(8,128)S(1)}, f32[8,256]{1,0:T(8,128)S(1)}, u32[]{:S(2)}, u32[]{:S(2)}) collective-permute-start(f32[8,256]{1,0:T(8,128)S(1)} %shard_map.60.a_ref), channel_id=1, source_target_pairs={{0,2},{1,3},{2,0},{3,1},{4,6},{5,7},{6,4},{7,5},{8,10},{9,11},{10,... | collective-permute-start | bytes 24584 | tf_op jit(solution)/shard_map/ppermute | solution.py:65
  51.7 4.1 %collective-permute-start.14 = (bf16[4,32,1024]{2,1,0:T(8,128)(2,1)S(1)}, bf16[4,32,1024]{2,1,0:T(8,128)(2,1)S(1)}, u32[]{:S(2)}, u32[]{:S(2)}) collective-permute-start(bf16[4,32,1024]{2,1,0:T(8,128)(2,1)S(1)} %shard_map.63), channel_id=1, source_target_pairs={{0,1},{1,0},{2,3},{3,2},{4,5},{5,4},{6,7},{7,6},{8,9},{9,8},{10,11... | collective-permute-start | bytes 786440 | tf_op jit(solution)/shard_map/ppermute | solution.py:65
  51.8 9.6 %collective-permute-start.16 = (bf16[128,1024]{1,0:T(8,128)(2,1)S(1)}, bf16[128,1024]{1,0:T(8,128)(2,1)S(1)}, u32[]{:S(2)}, u32[]{:S(2)}) collective-permute-start(bf16[128,1024]{1,0:T(8,128)(2,1)S(1)} %get-tuple-element.40), channel_id=1, source_target_pairs={{0,24},{8,16},{16,8},{24,0},{1,25},{9,17},{17,9},{25,1},{2,26},{10... | collective-permute-start | bytes 786440 | tf_op jit(solution)/shard_map/ppermute | solution.py:65
  53.4 4.5 %collective-permute-start.9 = (f32[8,256]{1,0:T(8,128)S(1)}, f32[8,256]{1,0:T(8,128)S(1)}, u32[]{:S(2)}, u32[]{:S(2)}) collective-permute-start(f32[8,256]{1,0:T(8,128)S(1)} %shard_map.61.refs_4_.refs_0_), channel_id=1, source_target_pairs={{0,4},{1,5},{2,6},{3,7},{4,0},{5,1},{6,2},{7,3},{8,12},{9,13},{10,... | collective-permute-start | bytes 24584 | tf_op jit(solution)/shard_map/ppermute | solution.py:65
  55.8 5.6 %collective-permute-start.17 = (bf16[16,128]{1,0:T(8,128)(2,1)S(1)}, bf16[16,128]{1,0:T(8,128)(2,1)S(1)}, u32[]{:S(2)}, u32[]{:S(2)}) collective-permute-start(bf16[16,128]{1,0:T(8,128)(2,1)S(1)} %slice_bitcast_fusion), channel_id=1, source_target_pairs={{0,1},{1,0},{2,3},{3,2},{4,5},{5,4},{6,7},{7,6},{8,9},{9,8},{10,11... | collective-permute-start | bytes 12296 | tf_op jit(solution)/shard_map/ppermute | solution.py:65
  66.3 2.7 %collective-permute-start.18 = (bf16[128,4096]{1,0:T(8,128)(2,1)S(1)}, bf16[128,4096]{1,0:T(8,128)(2,1)S(1)}, u32[]{:S(2)}, u32[]{:S(2)}) collective-permute-start(bf16[128,4096]{1,0:T(8,128)(2,1)S(1)} %get-tuple-element.42), channel_id=1, source_target_pairs={{0,1},{1,0},{2,3},{3,2},{4,5},{5,4},{6,7},{7,6},{8,9},{9,8},{10,11... | collective-permute-start | bytes 3145736 | tf_op jit(solution)/shard_map/ppermute | solution.py:65
  69.4 9.2 %collective-permute-start.20 = (bf16[32,4096]{1,0:T(8,128)(2,1)S(1)}, bf16[32,4096]{1,0:T(8,128)(2,1)S(1)}, u32[]{:S(2)}, u32[]{:S(2)}) collective-permute-start(bf16[32,4096]{1,0:T(8,128)(2,1)S(1)} %get-tuple-element.49), channel_id=1, source_target_pairs={{0,2},{1,3},{2,0},{3,1},{4,6},{5,7},{6,4},{7,5},{8,10},{9,11},{10,... | collective-permute-start | bytes 786440 | tf_op jit(solution)/shard_map/ppermute | solution.py:65
  70.2 13.7 %collective-permute-start.22 = (bf16[256,1024]{1,0:T(8,128)(2,1)S(1)}, bf16[256,1024]{1,0:T(8,128)(2,1)S(1)}, u32[]{:S(2)}, u32[]{:S(2)}) collective-permute-start(bf16[256,1024]{1,0:T(8,128)(2,1)S(1)} %get-tuple-element.43.refs_0_), channel_id=1, source_target_pairs={{0,8},{8,0},{16,24},{24,16},{1,9},{9,1},{17,25},{25,17},{2,10},{10... | collective-permute-start | bytes 1572872 | tf_op jit(solution)/shard_map/ppermute | solution.py:65
  71.4 14.1 %collective-permute-start.23 = (bf16[256,1024]{1,0:T(8,128)(2,1)S(1)}, bf16[256,1024]{1,0:T(8,128)(2,1)S(1)}, u32[]{:S(2)}, u32[]{:S(2)}) collective-permute-start(bf16[256,1024]{1,0:T(8,128)(2,1)S(1)} %get-tuple-element.43.refs_0_), channel_id=1, source_target_pairs={{0,16},{8,24},{16,0},{24,8},{1,17},{9,25},{17,1},{25,9},{2,18},{10... | collective-permute-start | bytes 1572872 | tf_op jit(solution)/shard_map/ppermute | solution.py:65
  73.0 13.9 %collective-permute-start.24 = (bf16[384,1024]{1,0:T(8,128)(2,1)S(1)}, bf16[384,1024]{1,0:T(8,128)(2,1)S(1)}, u32[]{:S(2)}, u32[]{:S(2)}) collective-permute-start(bf16[384,1024]{1,0:T(8,128)(2,1)S(1)} %get-tuple-element.45.refs_4_.refs_2_), channel_id=1, source_target_pairs={{0,1},{1,0},{2,3},{3,2},{4,5},{5,4},{6,7},{7,6},{8,9},{9,8},{10,11... | collective-permute-start | bytes 2359304 | tf_op jit(solution)/shard_map/ppermute | solution.py:65
  73.0 15.7 %collective-permute-start.19 = (bf16[32,4096]{1,0:T(8,128)(2,1)S(1)}, bf16[32,4096]{1,0:T(8,128)(2,1)S(1)}, u32[]{:S(2)}, u32[]{:S(2)}) collective-permute-start(bf16[32,4096]{1,0:T(8,128)(2,1)S(1)} %get-tuple-element.48), channel_id=1, source_target_pairs={{0,2},{1,3},{2,0},{3,1},{4,6},{5,7},{6,4},{7,5},{8,10},{9,11},{10,... | collective-permute-start | bytes 786440 | tf_op jit(solution)/shard_map/ppermute | solution.py:65
  78.7 13.4 %collective-permute-start.21 = (bf16[32,4096]{1,0:T(8,128)(2,1)S(1)}, bf16[32,4096]{1,0:T(8,128)(2,1)S(1)}, u32[]{:S(2)}, u32[]{:S(2)}) collective-permute-start(bf16[32,4096]{1,0:T(8,128)(2,1)S(1)} %fusion), channel_id=1, source_target_pairs={{0,4},{1,5},{2,6},{3,7},{4,0},{5,1},{6,2},{7,3},{8,12},{9,13},{10,... | collective-permute-start | bytes 786440 | tf_op jit(solution)/shard_map/ppermute | solution.py:65
  83.9 8.3 %collective-permute-start.25 = (bf16[128,1024]{1,0:T(8,128)(2,1)S(1)}, bf16[128,1024]{1,0:T(8,128)(2,1)S(1)}, u32[]{:S(2)}, u32[]{:S(2)}) collective-permute-start(bf16[128,1024]{1,0:T(8,128)(2,1)S(1)} %slice.35), channel_id=1, source_target_pairs={{0,16},{8,24},{16,0},{24,8},{1,17},{9,25},{17,1},{25,9},{2,18},{10... | collective-permute-start | bytes 786440 | tf_op jit(solution)/shard_map/ppermute | solution.py:65
  85.5 7.0 %collective-permute-start.26 = (bf16[128,1024]{1,0:T(8,128)(2,1)S(1)}, bf16[128,1024]{1,0:T(8,128)(2,1)S(1)}, u32[]{:S(2)}, u32[]{:S(2)}) collective-permute-start(bf16[128,1024]{1,0:T(8,128)(2,1)S(1)} %slice.36), channel_id=1, source_target_pairs={{0,8},{8,0},{16,24},{24,16},{1,9},{9,1},{17,25},{25,17},{2,10},{10... | collective-permute-start | bytes 786440 | tf_op jit(solution)/shard_map/ppermute | solution.py:65
  92.2 2.0 %copy-start.1 = (bf16[32,4096]{1,0:T(8,128)(2,1)}, bf16[32,4096]{1,0:T(8,128)(2,1)S(1)}, u32[]{:S(2)}) copy-start(bf16[32,4096]{1,0:T(8,128)(2,1)S(1)} %fusion.2.refs_4_) | copy-start | bytes 786436

commit v5 on v4

--- a/solution.py
+++ b/solution.py
@@ -291,7 +291,7 @@
     )(slots, listed, *mine, sibling)
 
 
-def logit_grads(logits, stats, mine, sibling, weight, cols, after, parts=8):
+def logit_grads(logits, stats, mine, sibling, weight, cols, after, parts=4, ahead=3):
     chips, rows, vocab_rows = sibling.shape
     tokens = logits.shape[0]
     half = chips * rows
@@ -318,6 +318,7 @@
                     weight_ref.at[:, some], held_weight.at[:, some], sems.at[k]
                 )
             )
+        for k in range(ahead):
             copies[k].start()
         for move in moves:
             move.start()
@@ -338,6 +339,8 @@
                 out_ref[(h * chips + j) * rows : (h * chips + j + 1) * rows] = grads
         for k in range(parts):
             copies[k].wait()
+            if k + ahead < parts:
+                copies[k + ahead].start()
             some = slice(k * step, (k + 1) * step)
             share = jnp.dot(out_ref[...], held_weight[:, some], preferred_element_type=jnp.float32)
             own_ref[:, some] = share[:half]
@@ -467,7 +470,6 @@
     got = between_chips(
         [lax.dynamic_slice_in_dim(teacher, (chip ^ r) * 2 * rows, 2 * rows) for r in range(chips)]
     )
-    pieces, got = lax.optimization_barrier((pieces, got))
     own = jnp.concatenate(pieces)
     other = swap(own, "vocab", 1)
     my_ids = lax.dynamic_index_in_dim(block_ids, me * rows // BLK, keepdims=False)
@@ -492,14 +494,9 @@
     own_cols = [swap_by_core(near), swap(far, "dp", data_size - 1)]
 
     stats = merge_pair(stats, swap(stats, "vocab", 1))
-    bits = 2
-    while 2 * bits < vocab_size:
-        stats = merge_pair(stats, swap(stats, "vocab", bits))
-        bits *= 2
-    all_stats = [stats, swap(stats, "vocab", bits)]
+    all_stats = between_chips([stats] * chips)
     other_tiles = swap(siblings_part_after(tiles, rows, [stats]), "vocab", 1)
     spare = other_tiles[0, :TILE_ROWS, :BLK]
-    spare = swap(spare, "vocab", 1)
     grad_logits, share, rest, own_cols = logit_grads(
         logits, all_stats, tiles, other_tiles, weight, own_cols, [spare]
     )

time: 94.4 us -> 92.8 us (0.983)
  waiting for transfers between devices: 43 us -> 38.9 us
  starting transfers between devices: 31.3 us -> 33.4 us
    ppermute x26, waiting for transfers between devices: 43 us -> 38.9 us  [swap(): lax.ppermute(x, axis, [(i, i ^ bits) for i in range(lax.axis_size(axis))])]
    ppermute x26, starting transfers between devices: 29.6 us -> 31.7 us  [swap(): lax.ppermute(x, axis, [(i, i ^ bits) for i in range(lax.axis_size(axis))])]
  transfers between devices with their start and end apart: 27 -> 27, of which waited for: 14 -> 12; matrix products, arithmetic and copies ran while one was open for 3% -> 5% of each run, Pallas kernels for 9% -> 9%
where the time goes in v5:
time: 92.8 us; the launch traced here: 92.6 us
  waiting for transfers between devices  38.9 us (42%)
  starting transfers between devices  33.4 us (36%)
  Pallas kernels  14.5 us (16%)
  local copies, waits for them, and re-layouts  2.49 us (3%)
  other arithmetic  2.27 us (2%)
  between operations  0.95 us (1%)
    ppermute x26, waiting for transfers between devices, swap(): lax.ppermute(x, axis, [(i, i ^ bits) for i in range(lax.axis_size(axis))])  38.9 us
    ppermute x26, starting transfers between devices, swap(): lax.ppermute(x, axis, [(i, i ^ bits) for i in range(lax.axis_size(axis))])  31.7 us
    pallas_call x1, Pallas kernels, logits_and_stats(): pl.pallas_call(body, out_shape=[jax.ShapeDtypeStruct((tokens, vocab_rows)...  5.43 us
    pallas_call x1, Pallas kernels, logit_grads(): pl.pallas_call(body, out_shape=[jax.ShapeDtypeStruct((tokens, vocab_rows)...  4.5 us
    pallas_call x1, Pallas kernels, weight_grad_part(): pl.pallas_call(body, out_shape=jax.ShapeDtypeStruct((vocab_rows, columns)...  1.86 us
  transfers between devices with their start and end apart: 27, of which 12 were waited for; matrix products, arithmetic and copies ran while one was open for 5% of the time, Pallas kernels for 9%

profile of v5, /device:TPU:0, one launch (start us, length us, event | category | flops | bytes accessed | tf_op | source)
XLA Modules:
  0.0 92.6 jit_solution(10787752947325597650)
XLA Ops:
  0.6 0.0 copy-start
  0.7 3.1 %collective-permute-start = (bf16[32,4096]{1,0:T(8,128)(2,1)}, bf16[32,4096]{1,0:T(8,128)(2,1)S(1)}, u32[]{:S(2)}, u32[]{:S(2)}) collective-permute-start(bf16[32,4096]{1,0:T(8,128)(2,1)} %param.4), channel_id=1, source_target_pairs={{0,2},{1,3},{2,0},{3,1},{4,6},{5,7},{6,4},{7,5},{8,10},{9,11},{10,... | collective-permute-start | bytes 786440 | tf_op jit(solution)/shard_map/ppermute | solution.py:65
  3.7 2.6 %collective-permute-start.1 = (bf16[32,4096]{1,0:T(8,128)(2,1)}, bf16[32,4096]{1,0:T(8,128)(2,1)S(1)}, u32[]{:S(2)}, u32[]{:S(2)}) collective-permute-start(bf16[32,4096]{1,0:T(8,128)(2,1)} %param.4), channel_id=1, source_target_pairs={{0,4},{1,5},{2,6},{3,7},{4,0},{5,1},{6,2},{7,3},{8,12},{9,13},{10,... | collective-permute-start | bytes 786440 | tf_op jit(solution)/shard_map/ppermute | solution.py:65
  6.3 1.1 %constant_dynamic-slice_fusion = (bf16[64,1024]{1,0:T(8,128)(2,1)S(1)}, bf16[64,1024]{1,0:T(8,128)(2,1)S(1)}, bf16[64,1024]{1,0:T(8,128)(2,1)S(1)}, bf16[64,1024]{1,0:T(8,128)(2,1)S(1)}) fusion(bf16[256,1024]{1,0:T(8,128)(2,1)} %param.6, s32[]{:T(128)S(6)} %select_n.66, s32[]{:T(128)S(6)} %select_n.65, s32[]{:T(128)S(6)} %select_n.64, s32[]{:T(128)S(6)} %select_n.63), kind=kLoop, calls=%fused_computation.20 | loop fusion | bytes 1048592 | tf_op jit(solution)/shard_map/dynamic_slice | solution.py:471
  7.5 0.5 collective-permute-start.8
  8.0 0.0 collective-permute-start.9
  8.0 3.9 %collective-permute-start.10 = (bf16[64,1024]{1,0:T(8,128)(2,1)S(1)}, bf16[64,1024]{1,0:T(8,128)(2,1)S(1)}, u32[]{:S(2)}, u32[]{:S(2)}) collective-permute-start(bf16[64,1024]{1,0:T(8,128)(2,1)S(1)} %get-tuple-element.34), channel_id=1, source_target_pairs={{0,6},{1,7},{2,4},{3,5},{4,2},{5,3},{6,0},{7,1},{8,14},{9,15},{10,... | collective-permute-start | bytes 393224 | tf_op jit(solution)/shard_map/ppermute | solution.py:65
  11.9 1.0 %constant_dynamic-update-slice_fusion.3 = bf16[128,4096]{1,0:T(8,128)(2,1)S(1)} fusion(bf16[32,4096]{1,0:T(8,128)(2,1)} %param.4), kind=kLoop, calls=%fused_computation.17 | loop fusion | bytes 524288
  12.9 0.1 stack.50
  13.0 0.1 iota_add_fusion
  13.1 0.1 add.96
  13.2 0.7 compare_reduce_fusion.1
  13.9 5.9 %collective-permute-done.1 = bf16[32,4096]{1,0:T(8,128)(2,1)S(1)} collective-permute-done((bf16[32,4096]{1,0:T(8,128)(2,1)}, bf16[32,4096]{1,0:T(8,128)(2,1)S(1)}, u32[]{:S(2)}, u32[]{:S(2)}) %collective-permute-start.1) | collective-permute-done | bytes 262176 | tf_op jit(solution)/shard_map/ppermute | solution.py:65
  19.8 0.2 collective-permute-start.2
  20.0 0.0 collective-permute-done
  20.1 9.8 %collective-permute-done.2 = bf16[32,4096]{1,0:T(8,128)(2,1)S(1)} collective-permute-done((bf16[32,4096]{1,0:T(8,128)(2,1)S(1)}, bf16[32,4096]{1,0:T(8,128)(2,1)S(1)}, u32[]{:S(2)}, u32[]{:S(2)}) %collective-permute-start.2) | collective-permute-done | bytes 262176 | tf_op jit(solution)/shard_map/ppermute | solution.py:65
  29.9 0.1 collective-permute-start.3
  30.0 0.1 convert_reduce_fusion
  30.2 0.0 collective-permute-done.10.refs_3_
  30.3 0.0 collective-permute-done.8.refs_1_
  30.4 0.6 collective-permute-start.11
  30.9 0.8 compare_reduce_fusion
  31.8 1.2 %collective-permute-done.11.refs_4_ = bf16[4,32,1024]{2,1,0:T(8,128)(2,1)S(1)} collective-permute-done((bf16[4,32,1024]{2,1,0:T(8,128)(2,1)S(1)}, bf16[4,32,1024]{2,1,0:T(8,128)(2,1)S(1)}, u32[]{:S(2)}, u32[]{:S(2)}) %collective-permute-start.11) | collective-permute-done | bytes 262176 | tf_op jit(solution)/shard_map/ppermute | solution.py:65
  33.0 1.0 %shard_map.61 = (bf16[64,1024]{1,0:T(8,128)(2,1)S(1)}, bf16[64,1024]{1,0:T(8,128)(2,1)S(1)}, bf16[64,1024]{1,0:T(8,128)(2,1)S(1)}, bf16[64,1024]{1,0:T(8,128)(2,1)S(1)}) custom-call(s32[64]{0:T(128)S(1)} %fusion.3.slots_ref, s32[64]{0:T(128)S(1)} %convert_element_type.27.listed_ref, bf16[64,1024]{1,0:T(8,128)(2,1)S(1)} %get-tuple-element.37.refs_0_, ...), custom_call_target="tpu_custom_call" | custom-call | bytes 524288 | tf_op jit(solution)/shard_map/pallas_call | solution.py:283
  34.1 1.9 %collective-permute-start.12 = (bf16[64,1024]{1,0:T(8,128)(2,1)S(1)}, bf16[64,1024]{1,0:T(8,128)(2,1)S(1)}, u32[]{:S(2)}, u32[]{:S(2)}) collective-permute-start(bf16[64,1024]{1,0:T(8,128)(2,1)S(1)} %get-tuple-element.20), channel_id=1, source_target_pairs={{0,2},{1,3},{2,0},{3,1},{4,6},{5,7},{6,4},{7,5},{8,10},{9,11},{10,... | collective-permute-start | bytes 393224 | tf_op jit(solution)/shard_map/ppermute | solution.py:65
  36.0 2.5 %collective-permute-start.13 = (bf16[64,1024]{1,0:T(8,128)(2,1)S(1)}, bf16[64,1024]{1,0:T(8,128)(2,1)S(1)}, u32[]{:S(2)}, u32[]{:S(2)}) collective-permute-start(bf16[64,1024]{1,0:T(8,128)(2,1)S(1)} %get-tuple-element.21), channel_id=1, source_target_pairs={{0,4},{1,5},{2,6},{3,7},{4,0},{5,1},{6,2},{7,3},{8,12},{9,13},{10,... | collective-permute-start | bytes 393224 | tf_op jit(solution)/shard_map/ppermute | solution.py:65
  38.5 0.1 collective-permute-start.14
  38.5 0.0 collective-permute-done.3.refs_1_
  38.5 5.4 %shard_map.59 = (f32[256,1024]{1,0:T(8,128)S(1)}, f32[8,256]{1,0:T(8,128)S(1)}, bf16[256,1024]{1,0:T(8,128)(2,1)S(1)}, bf16[256,1024]{1,0:T(8,128)(2,1)S(1)}, bf16[128,1024]{1,0:T(8,128)(2,1)S(1)}) custom-call(bf16[128,4096]{1,0:T(8,128)(2,1)S(1)} %constant_dynamic-update-slice_fusion.refs_0_, bf16[128,4096]{1,0:T(8,128)(2,1)S(1)} %collective-permute-done.3.refs_1_, ...), custom_call_target="tpu_custom_call" | custom-call | flops 2147483648 | bytes 10486272 | tf_op jit(solution)/shard_map/pallas_call | solution.py:193
  44.0 1.7 %collective-permute-start.16 = (bf16[256,1024]{1,0:T(8,128)(2,1)S(1)}, bf16[256,1024]{1,0:T(8,128)(2,1)S(1)}, u32[]{:S(2)}, u32[]{:S(2)}) collective-permute-start(bf16[256,1024]{1,0:T(8,128)(2,1)S(1)} %get-tuple-element.23), channel_id=1, source_target_pairs={{0,8},{1,17},{2,10},{3,19},{4,12},{5,21},{6,14},{7,23},{8,0},{9,25... | collective-permute-start | bytes 1572872 | tf_op jit(solution)/shard_map/ppermute | solution.py:223
  45.7 0.0 collective-permute-start.4
  45.7 1.2 %collective-permute-done.4.b_ref = f32[8,256]{1,0:T(8,128)S(1)} collective-permute-done((f32[8,256]{1,0:T(8,128)S(1)}, f32[8,256]{1,0:T(8,128)S(1)}, u32[]{:S(2)}, u32[]{:S(2)}) %collective-permute-start.4) | collective-permute-done | bytes 8224 | tf_op jit(solution)/shard_map/ppermute | solution.py:65
  46.9 2.0 %collective-permute-done.13.refs_2_.refs_6_ = bf16[64,1024]{1,0:T(8,128)(2,1)S(1)} collective-permute-done((bf16[64,1024]{1,0:T(8,128)(2,1)S(1)}, bf16[64,1024]{1,0:T(8,128)(2,1)S(1)}, u32[]{:S(2)}, u32[]{:S(2)}) %collective-permute-start.13) | collective-permute-done | bytes 131104 | tf_op jit(solution)/shard_map/ppermute | solution.py:65
  48.9 0.1 collective-permute-start.15
  49.0 2.5 %collective-permute-start.17 = (bf16[128,1024]{1,0:T(8,128)(2,1)S(1)}, bf16[128,1024]{1,0:T(8,128)(2,1)S(1)}, u32[]{:S(2)}, u32[]{:S(2)}) collective-permute-start(bf16[128,1024]{1,0:T(8,128)(2,1)S(1)} %get-tuple-element.24), channel_id=1, source_target_pairs={{0,24},{8,16},{16,8},{24,0},{1,25},{9,17},{17,9},{25,1},{2,26},{10... | collective-permute-start | bytes 786440 | tf_op jit(solution)/shard_map/ppermute | solution.py:65
  51.5 2.3 %collective-permute-start.5 = (f32[8,256]{1,0:T(8,128)S(1)}, f32[8,256]{1,0:T(8,128)S(1)}, u32[]{:S(2)}, u32[]{:S(2)}) collective-permute-start(f32[8,256]{1,0:T(8,128)S(1)} %shard_map.60.refs_4_.refs_0_), channel_id=1, source_target_pairs={{0,2},{1,3},{2,0},{3,1},{4,6},{5,7},{6,4},{7,5},{8,10},{9,11},{10,... | collective-permute-start | bytes 24584 | tf_op jit(solution)/shard_map/ppermute | solution.py:65
  53.8 1.0 %collective-permute-start.6 = (f32[8,256]{1,0:T(8,128)S(1)}, f32[8,256]{1,0:T(8,128)S(1)}, u32[]{:S(2)}, u32[]{:S(2)}) collective-permute-start(f32[8,256]{1,0:T(8,128)S(1)} %shard_map.60.refs_4_.refs_0_), channel_id=1, source_target_pairs={{0,4},{1,5},{2,6},{3,7},{4,0},{5,1},{6,2},{7,3},{8,12},{9,13},{10,... | collective-permute-start | bytes 24584 | tf_op jit(solution)/shard_map/ppermute | solution.py:65
  54.8 0.0 collective-permute-done.15.refs_8_
  54.8 1.5 %collective-permute-start.7 = (f32[8,256]{1,0:T(8,128)S(1)}, f32[8,256]{1,0:T(8,128)S(1)}, u32[]{:S(2)}, u32[]{:S(2)}) collective-permute-start(f32[8,256]{1,0:T(8,128)S(1)} %shard_map.60.refs_4_.refs_0_), channel_id=1, source_target_pairs={{0,6},{1,7},{2,4},{3,5},{4,2},{5,3},{6,0},{7,1},{8,14},{9,15},{10,... | collective-permute-start | bytes 24584 | tf_op jit(solution)/shard_map/ppermute | solution.py:65
  56.3 2.1 %collective-permute-done.6.refs_2_ = f32[8,256]{1,0:T(8,128)S(1)} collective-permute-done((f32[8,256]{1,0:T(8,128)S(1)}, f32[8,256]{1,0:T(8,128)S(1)}, u32[]{:S(2)}, u32[]{:S(2)}) %collective-permute-start.6) | collective-permute-done | bytes 8224 | tf_op jit(solution)/shard_map/ppermute | solution.py:65
  58.3 1.9 %collective-permute-done.7.refs_3_ = f32[8,256]{1,0:T(8,128)S(1)} collective-permute-done((f32[8,256]{1,0:T(8,128)S(1)}, f32[8,256]{1,0:T(8,128)S(1)}, u32[]{:S(2)}, u32[]{:S(2)}) %collective-permute-start.7) | collective-permute-done | bytes 8224 | tf_op jit(solution)/shard_map/ppermute | solution.py:65
  60.2 0.0 collective-permute-done.17.refs_11_
  60.2 4.5 %shard_map.63 = (bf16[256,1024]{1,0:T(8,128)(2,1)S(1)}, f32[128,4096]{1,0:T(8,128)S(1)}, bf16[128,4096]{1,0:T(8,128)(2,1)S(1)}, bf16[384,1024]{1,0:T(8,128)(2,1)S(1)}) custom-call(f32[256,1024]{1,0:T(8,128)S(1)} %get-tuple-element.16.logits_ref, f32[8,256]{1,0:T(8,128)S(1)} %shard_map.60.refs_4_.refs_0_, f32[8,256]{1,0:T(8,128)S(1)} %collective-permute-done.5.refs_1_, ...), custom_call_target="tpu_custom_call" | custom-call | flops 2147483648 | bytes 9715712 | tf_op jit(solution)/shard_map/pallas_call | solution.py:352
  64.7 0.1 collective-permute-start.18
  64.8 2.6 %collective-permute-done.18 = bf16[128,4096]{1,0:T(8,128)(2,1)S(1)} collective-permute-done((bf16[128,4096]{1,0:T(8,128)(2,1)S(1)}, bf16[128,4096]{1,0:T(8,128)(2,1)S(1)}, u32[]{:S(2)}, u32[]{:S(2)}) %collective-permute-start.18) | collective-permute-done | bytes 1048608 | tf_op jit(solution)/shard_map/ppermute | solution.py:65
  67.5 0.3 fusion.8
  67.8 0.7 collective-permute-start.20
  68.6 1.5 %collective-permute-start.22 = (bf16[256,1024]{1,0:T(8,128)(2,1)S(1)}, bf16[256,1024]{1,0:T(8,128)(2,1)S(1)}, u32[]{:S(2)}, u32[]{:S(2)}) collective-permute-start(bf16[256,1024]{1,0:T(8,128)(2,1)S(1)} %get-tuple-element.27.refs_0_), channel_id=1, source_target_pairs={{0,8},{8,0},{16,24},{24,16},{1,9},{9,1},{17,25},{25,17},{2,10},{10... | collective-permute-start | bytes 1572872 | tf_op jit(solution)/shard_map/ppermute | solution.py:65
  70.1 1.5 %collective-permute-start.23 = (bf16[256,1024]{1,0:T(8,128)(2,1)S(1)}, bf16[256,1024]{1,0:T(8,128)(2,1)S(1)}, u32[]{:S(2)}, u32[]{:S(2)}) collective-permute-start(bf16[256,1024]{1,0:T(8,128)(2,1)S(1)} %get-tuple-element.27.refs_0_), channel_id=1, source_target_pairs={{0,16},{8,24},{16,0},{24,8},{1,17},{9,25},{17,1},{25,9},{2,18},{10... | collective-permute-start | bytes 1572872 | tf_op jit(solution)/shard_map/ppermute | solution.py:65
  71.6 0.0 collective-permute-start.24
  71.6 0.1 collective-permute-start.19
  71.7 5.4 %collective-permute-done.20 = bf16[32,4096]{1,0:T(8,128)(2,1)S(1)} collective-permute-done((bf16[32,4096]{1,0:T(8,128)(2,1)S(1)}, bf16[32,4096]{1,0:T(8,128)(2,1)S(1)}, u32[]{:S(2)}, u32[]{:S(2)}) %collective-permute-start.20) | collective-permute-done | bytes 262176 | tf_op jit(solution)/shard_map/ppermute | solution.py:65
  77.1 1.9 %collective-permute-start.21 = (bf16[32,4096]{1,0:T(8,128)(2,1)S(1)}, bf16[32,4096]{1,0:T(8,128)(2,1)S(1)}, u32[]{:S(2)}, u32[]{:S(2)}) collective-permute-start(bf16[32,4096]{1,0:T(8,128)(2,1)S(1)} %fusion), channel_id=1, source_target_pairs={{0,4},{1,5},{2,6},{3,7},{4,0},{5,1},{6,2},{7,3},{8,12},{9,13},{10,... | collective-permute-start | bytes 786440 | tf_op jit(solution)/shard_map/ppermute | solution.py:65
  79.0 3.2 %collective-permute-done.22.refs_1_ = bf16[256,1024]{1,0:T(8,128)(2,1)S(1)} collective-permute-done((bf16[256,1024]{1,0:T(8,128)(2,1)S(1)}, bf16[256,1024]{1,0:T(8,128)(2,1)S(1)}, u32[]{:S(2)}, u32[]{:S(2)}) %collective-permute-start.22) | collective-permute-done | bytes 524320 | tf_op jit(solution)/shard_map/ppermute | solution.py:65
  82.3 1.6 %collective-permute-start.25 = (bf16[128,1024]{1,0:T(8,128)(2,1)S(1)}, bf16[128,1024]{1,0:T(8,128)(2,1)S(1)}, u32[]{:S(2)}, u32[]{:S(2)}) collective-permute-start(bf16[128,1024]{1,0:T(8,128)(2,1)S(1)} %slice.35), channel_id=1, source_target_pairs={{0,16},{8,24},{16,0},{24,8},{1,17},{9,25},{17,1},{25,9},{2,18},{10... | collective-permute-start | bytes 786440 | tf_op jit(solution)/shard_map/ppermute | solution.py:65
  83.9 0.0 collective-permute-done.23.refs_2_
  83.9 1.6 %collective-permute-start.26 = (bf16[128,1024]{1,0:T(8,128)(2,1)S(1)}, bf16[128,1024]{1,0:T(8,128)(2,1)S(1)}, u32[]{:S(2)}, u32[]{:S(2)}) collective-permute-start(bf16[128,1024]{1,0:T(8,128)(2,1)S(1)} %slice.36), channel_id=1, source_target_pairs={{0,8},{8,0},{16,24},{24,16},{1,9},{9,1},{17,25},{25,17},{2,10},{10... | collective-permute-start | bytes 786440 | tf_op jit(solution)/shard_map/ppermute | solution.py:65
  85.4 1.9 %shard_map.64.partial_ref = f32[1024,1024]{1,0:T(8,128)S(1)} custom-call(bf16[256,1024]{1,0:T(8,128)(2,1)S(1)} %get-tuple-element.27.refs_0_, bf16[256,1024]{1,0:T(8,128)(2,1)S(1)} %collective-permute-done.22.refs_1_, bf16[256,1024]{1,0:T(8,128)(2,1)S(1)} %collective-permute-done.23.refs_2_, bf16[256,1024]{1,0:T(8,128)(2,1)S(1)} %get-tuple-element.28.refs_3_, ...), custom_call_target="tpu_custom_call" | custom-call | flops 1610612736 | bytes 3670016 | tf_op jit(solution)/shard_map/pallas_call | solution.py:399
  87.3 0.0 collective-permute-done.19
  87.3 3.1 %collective-permute-done.21 = bf16[32,4096]{1,0:T(8,128)(2,1)S(1)} collective-permute-done((bf16[32,4096]{1,0:T(8,128)(2,1)S(1)}, bf16[32,4096]{1,0:T(8,128)(2,1)S(1)}, u32[]{:S(2)}, u32[]{:S(2)}) %collective-permute-start.21) | collective-permute-done | bytes 262176 | tf_op jit(solution)/shard_map/ppermute | solution.py:65
  90.5 0.1 fusion.2.refs_4_
  90.5 0.0 copy-start.1
  90.6 0.3 collective-permute-done.26.refs_1_
  90.9 1.7 %shard_map.65 = bf16[1024,1024]{1,0:T(8,128)(2,1)} custom-call(f32[1024,1024]{1,0:T(8,128)S(1)} %shard_map.64.partial_ref, bf16[128,1024]{1,0:T(8,128)(2,1)S(1)} %collective-permute-done.25.refs_0_, bf16[128,1024]{1,0:T(8,128)(2,1)S(1)} %collective-permute-done.26.refs_1_, bf16[384,1024]{1,0:T(8,128)(2,1)S(1)} %get-tuple-element.29.refs_4_.refs_2_, ...), custom_call_target="tpu_custom_call" | custom-call | flops 536870912 | bytes 4194304 | tf_op jit(solution)/shard_map/pallas_call | solution.py:434
  (32 shorter events, 0.4 us)
Async XLA Ops:
  0.6 12.5 %copy-start = (s32[2,64]{1,0:T(2,128)S(1)}, s32[2,64]{1,0:T(2,128)}, u32[]{:S(2)}) copy-start(s32[2,64]{1,0:T(2,128)} %param.7) | copy-start | bytes 1540
  0.6 29.4 %copy-start.2 = (bf16[256,1024]{1,0:T(8,128)(2,1)S(1)}, bf16[256,1024]{1,0:T(8,128)(2,1)}, u32[]{:S(2)}) copy-start(bf16[256,1024]{1,0:T(8,128)(2,1)} %param.6) | copy-start | bytes 1572868
  0.7 19.4 %collective-permute-start = (bf16[32,4096]{1,0:T(8,128)(2,1)}, bf16[32,4096]{1,0:T(8,128)(2,1)S(1)}, u32[]{:S(2)}, u32[]{:S(2)}) collective-permute-start(bf16[32,4096]{1,0:T(8,128)(2,1)} %param.4), channel_id=1, source_target_pairs={{0,2},{1,3},{2,0},{3,1},{4,6},{5,7},{6,4},{7,5},{8,10},{9,11},{10,... | collective-permute-start | bytes 786440 | tf_op jit(solution)/shard_map/ppermute | solution.py:65
  3.7 16.1 %collective-permute-start.1 = (bf16[32,4096]{1,0:T(8,128)(2,1)}, bf16[32,4096]{1,0:T(8,128)(2,1)S(1)}, u32[]{:S(2)}, u32[]{:S(2)}) collective-permute-start(bf16[32,4096]{1,0:T(8,128)(2,1)} %param.4), channel_id=1, source_target_pairs={{0,4},{1,5},{2,6},{3,7},{4,0},{5,1},{6,2},{7,3},{8,12},{9,13},{10,... | collective-permute-start | bytes 786440 | tf_op jit(solution)/shard_map/ppermute | solution.py:65
  7.5 22.8 %collective-permute-start.8 = (bf16[64,1024]{1,0:T(8,128)(2,1)S(1)}, bf16[64,1024]{1,0:T(8,128)(2,1)S(1)}, u32[]{:S(2)}, u32[]{:S(2)}) collective-permute-start(bf16[64,1024]{1,0:T(8,128)(2,1)S(1)} %get-tuple-element.36), channel_id=1, source_target_pairs={{0,2},{1,3},{2,0},{3,1},{4,6},{5,7},{6,4},{7,5},{8,10},{9,11},{10,... | collective-permute-start | bytes 393224 | tf_op jit(solution)/shard_map/ppermute | solution.py:65
  8.0 22.3 %collective-permute-start.9 = (bf16[64,1024]{1,0:T(8,128)(2,1)S(1)}, bf16[64,1024]{1,0:T(8,128)(2,1)S(1)}, u32[]{:S(2)}, u32[]{:S(2)}) collective-permute-start(bf16[64,1024]{1,0:T(8,128)(2,1)S(1)} %get-tuple-element.35), channel_id=1, source_target_pairs={{0,4},{1,5},{2,6},{3,7},{4,0},{5,1},{6,2},{7,3},{8,12},{9,13},{10,... | collective-permute-start | bytes 393224 | tf_op jit(solution)/shard_map/ppermute | solution.py:65
  8.0 22.2 %collective-permute-start.10 = (bf16[64,1024]{1,0:T(8,128)(2,1)S(1)}, bf16[64,1024]{1,0:T(8,128)(2,1)S(1)}, u32[]{:S(2)}, u32[]{:S(2)}) collective-permute-start(bf16[64,1024]{1,0:T(8,128)(2,1)S(1)} %get-tuple-element.34), channel_id=1, source_target_pairs={{0,6},{1,7},{2,4},{3,5},{4,2},{5,3},{6,0},{7,1},{8,14},{9,15},{10,... | collective-permute-start | bytes 393224 | tf_op jit(solution)/shard_map/ppermute | solution.py:65
  13.1 0.8 copy-start.3
  19.8 10.1 %collective-permute-start.2 = (bf16[32,4096]{1,0:T(8,128)(2,1)S(1)}, bf16[32,4096]{1,0:T(8,128)(2,1)S(1)}, u32[]{:S(2)}, u32[]{:S(2)}) collective-permute-start(bf16[32,4096]{1,0:T(8,128)(2,1)S(1)} %collective-permute-done.1), channel_id=1, source_target_pairs={{0,2},{1,3},{2,0},{3,1},{4,6},{5,7},{6,4},{7,5},{8,10},{9,11},{10,... | collective-permute-start | bytes 786440 | tf_op jit(solution)/shard_map/ppermute | solution.py:65
  29.9 8.6 %collective-permute-start.3 = (bf16[128,4096]{1,0:T(8,128)(2,1)S(1)}, bf16[128,4096]{1,0:T(8,128)(2,1)S(1)}, u32[]{:S(2)}, u32[]{:S(2)}) collective-permute-start(bf16[128,4096]{1,0:T(8,128)(2,1)S(1)} %constant_dynamic-update-slice_fusion.refs_0_), channel_id=1, source_target_pairs={{0,1},{1,0},{2,3},{3,2},{4,5},{5,4},{6,7},{7,6},{8,9},{9,8},{10,11... | collective-permute-start | bytes 3145736 | tf_op jit(solution)/shard_map/ppermute | solution.py:65
  30.4 2.7 %collective-permute-start.11 = (bf16[4,32,1024]{2,1,0:T(8,128)(2,1)S(1)}, bf16[4,32,1024]{2,1,0:T(8,128)(2,1)S(1)}, u32[]{:S(2)}, u32[]{:S(2)}) collective-permute-start(bf16[4,32,1024]{2,1,0:T(8,128)(2,1)S(1)} %pad_maximum_fusion), channel_id=1, source_target_pairs={{0,1},{1,0},{2,3},{3,2},{4,5},{5,4},{6,7},{7,6},{8,9},{9,8},{10,11... | collective-permute-start | bytes 786440 | tf_op jit(solution)/shard_map/ppermute | solution.py:65
  34.1 12.8 %collective-permute-start.12 = (bf16[64,1024]{1,0:T(8,128)(2,1)S(1)}, bf16[64,1024]{1,0:T(8,128)(2,1)S(1)}, u32[]{:S(2)}, u32[]{:S(2)}) collective-permute-start(bf16[64,1024]{1,0:T(8,128)(2,1)S(1)} %get-tuple-element.20), channel_id=1, source_target_pairs={{0,2},{1,3},{2,0},{3,1},{4,6},{5,7},{6,4},{7,5},{8,10},{9,11},{10,... | collective-permute-start | bytes 393224 | tf_op jit(solution)/shard_map/ppermute | solution.py:65
  36.0 12.9 %collective-permute-start.13 = (bf16[64,1024]{1,0:T(8,128)(2,1)S(1)}, bf16[64,1024]{1,0:T(8,128)(2,1)S(1)}, u32[]{:S(2)}, u32[]{:S(2)}) collective-permute-start(bf16[64,1024]{1,0:T(8,128)(2,1)S(1)} %get-tuple-element.21), channel_id=1, source_target_pairs={{0,4},{1,5},{2,6},{3,7},{4,0},{5,1},{6,2},{7,3},{8,12},{9,13},{10,... | collective-permute-start | bytes 393224 | tf_op jit(solution)/shard_map/ppermute | solution.py:65
  38.5 10.4 %collective-permute-start.14 = (bf16[64,1024]{1,0:T(8,128)(2,1)S(1)}, bf16[64,1024]{1,0:T(8,128)(2,1)S(1)}, u32[]{:S(2)}, u32[]{:S(2)}) collective-permute-start(bf16[64,1024]{1,0:T(8,128)(2,1)S(1)} %get-tuple-element.22), channel_id=1, source_target_pairs={{0,6},{1,7},{2,4},{3,5},{4,2},{5,3},{6,0},{7,1},{8,14},{9,15},{10,... | collective-permute-start | bytes 393224 | tf_op jit(solution)/shard_map/ppermute | solution.py:65
  44.0 16.3 %collective-permute-start.16 = (bf16[256,1024]{1,0:T(8,128)(2,1)S(1)}, bf16[256,1024]{1,0:T(8,128)(2,1)S(1)}, u32[]{:S(2)}, u32[]{:S(2)}) collective-permute-start(bf16[256,1024]{1,0:T(8,128)(2,1)S(1)} %get-tuple-element.23), channel_id=1, source_target_pairs={{0,8},{1,17},{2,10},{3,19},{4,12},{5,21},{6,14},{7,23},{8,0},{9,25... | collective-permute-start | bytes 1572872 | tf_op jit(solution)/shard_map/ppermute | solution.py:223
  45.7 1.2 %collective-permute-start.4 = (f32[8,256]{1,0:T(8,128)S(1)}, f32[8,256]{1,0:T(8,128)S(1)}, u32[]{:S(2)}, u32[]{:S(2)}) collective-permute-start(f32[8,256]{1,0:T(8,128)S(1)} %get-tuple-element.17.a_ref), channel_id=1, source_target_pairs={{0,1},{1,0},{2,3},{3,2},{4,5},{5,4},{6,7},{7,6},{8,9},{9,8},{10,11... | collective-permute-start | bytes 24584 | tf_op jit(solution)/shard_map/ppermute | solution.py:65
  48.9 5.9 %collective-permute-start.15 = (bf16[4,32,1024]{2,1,0:T(8,128)(2,1)S(1)}, bf16[4,32,1024]{2,1,0:T(8,128)(2,1)S(1)}, u32[]{:S(2)}, u32[]{:S(2)}) collective-permute-start(bf16[4,32,1024]{2,1,0:T(8,128)(2,1)S(1)} %shard_map.62), channel_id=1, source_target_pairs={{0,1},{1,0},{2,3},{3,2},{4,5},{5,4},{6,7},{7,6},{8,9},{9,8},{10,11... | collective-permute-start | bytes 786440 | tf_op jit(solution)/shard_map/ppermute | solution.py:65
  49.0 11.3 %collective-permute-start.17 = (bf16[128,1024]{1,0:T(8,128)(2,1)S(1)}, bf16[128,1024]{1,0:T(8,128)(2,1)S(1)}, u32[]{:S(2)}, u32[]{:S(2)}) collective-permute-start(bf16[128,1024]{1,0:T(8,128)(2,1)S(1)} %get-tuple-element.24), channel_id=1, source_target_pairs={{0,24},{8,16},{16,8},{24,0},{1,25},{9,17},{17,9},{25,1},{2,26},{10... | collective-permute-start | bytes 786440 | tf_op jit(solution)/shard_map/ppermute | solution.py:65
  51.5 4.8 %collective-permute-start.5 = (f32[8,256]{1,0:T(8,128)S(1)}, f32[8,256]{1,0:T(8,128)S(1)}, u32[]{:S(2)}, u32[]{:S(2)}) collective-permute-start(f32[8,256]{1,0:T(8,128)S(1)} %shard_map.60.refs_4_.refs_0_), channel_id=1, source_target_pairs={{0,2},{1,3},{2,0},{3,1},{4,6},{5,7},{6,4},{7,5},{8,10},{9,11},{10,... | collective-permute-start | bytes 24584 | tf_op jit(solution)/shard_map/ppermute | solution.py:65
  53.8 4.5 %collective-permute-start.6 = (f32[8,256]{1,0:T(8,128)S(1)}, f32[8,256]{1,0:T(8,128)S(1)}, u32[]{:S(2)}, u32[]{:S(2)}) collective-permute-start(f32[8,256]{1,0:T(8,128)S(1)} %shard_map.60.refs_4_.refs_0_), channel_id=1, source_target_pairs={{0,4},{1,5},{2,6},{3,7},{4,0},{5,1},{6,2},{7,3},{8,12},{9,13},{10,... | collective-permute-start | bytes 24584 | tf_op jit(solution)/shard_map/ppermute | solution.py:65
  54.8 5.4 %collective-permute-start.7 = (f32[8,256]{1,0:T(8,128)S(1)}, f32[8,256]{1,0:T(8,128)S(1)}, u32[]{:S(2)}, u32[]{:S(2)}) collective-permute-start(f32[8,256]{1,0:T(8,128)S(1)} %shard_map.60.refs_4_.refs_0_), channel_id=1, source_target_pairs={{0,6},{1,7},{2,4},{3,5},{4,2},{5,3},{6,0},{7,1},{8,14},{9,15},{10,... | collective-permute-start | bytes 24584 | tf_op jit(solution)/shard_map/ppermute | solution.py:65
  64.7 2.7 %collective-permute-start.18 = (bf16[128,4096]{1,0:T(8,128)(2,1)S(1)}, bf16[128,4096]{1,0:T(8,128)(2,1)S(1)}, u32[]{:S(2)}, u32[]{:S(2)}) collective-permute-start(bf16[128,4096]{1,0:T(8,128)(2,1)S(1)} %get-tuple-element.26), channel_id=1, source_target_pairs={{0,1},{1,0},{2,3},{3,2},{4,5},{5,4},{6,7},{7,6},{8,9},{9,8},{10,11... | collective-permute-start | bytes 3145736 | tf_op jit(solution)/shard_map/ppermute | solution.py:65
  67.8 9.2 %collective-permute-start.20 = (bf16[32,4096]{1,0:T(8,128)(2,1)S(1)}, bf16[32,4096]{1,0:T(8,128)(2,1)S(1)}, u32[]{:S(2)}, u32[]{:S(2)}) collective-permute-start(bf16[32,4096]{1,0:T(8,128)(2,1)S(1)} %get-tuple-element.33), channel_id=1, source_target_pairs={{0,2},{1,3},{2,0},{3,1},{4,6},{5,7},{6,4},{7,5},{8,10},{9,11},{10,... | collective-permute-start | bytes 786440 | tf_op jit(solution)/shard_map/ppermute | solution.py:65
  68.6 13.7 %collective-permute-start.22 = (bf16[256,1024]{1,0:T(8,128)(2,1)S(1)}, bf16[256,1024]{1,0:T(8,128)(2,1)S(1)}, u32[]{:S(2)}, u32[]{:S(2)}) collective-permute-start(bf16[256,1024]{1,0:T(8,128)(2,1)S(1)} %get-tuple-element.27.refs_0_), channel_id=1, source_target_pairs={{0,8},{8,0},{16,24},{24,16},{1,9},{9,1},{17,25},{25,17},{2,10},{10... | collective-permute-start | bytes 1572872 | tf_op jit(solution)/shard_map/ppermute | solution.py:65
  70.1 13.8 %collective-permute-start.23 = (bf16[256,1024]{1,0:T(8,128)(2,1)S(1)}, bf16[256,1024]{1,0:T(8,128)(2,1)S(1)}, u32[]{:S(2)}, u32[]{:S(2)}) collective-permute-start(bf16[256,1024]{1,0:T(8,128)(2,1)S(1)} %get-tuple-element.27.refs_0_), channel_id=1, source_target_pairs={{0,16},{8,24},{16,0},{24,8},{1,17},{9,25},{17,1},{25,9},{2,18},{10... | collective-permute-start | bytes 1572872 | tf_op jit(solution)/shard_map/ppermute | solution.py:65
  71.6 13.9 %collective-permute-start.24 = (bf16[384,1024]{1,0:T(8,128)(2,1)S(1)}, bf16[384,1024]{1,0:T(8,128)(2,1)S(1)}, u32[]{:S(2)}, u32[]{:S(2)}) collective-permute-start(bf16[384,1024]{1,0:T(8,128)(2,1)S(1)} %get-tuple-element.29.refs_4_.refs_2_), channel_id=1, source_target_pairs={{0,1},{1,0},{2,3},{3,2},{4,5},{5,4},{6,7},{7,6},{8,9},{9,8},{10,11... | collective-permute-start | bytes 2359304 | tf_op jit(solution)/shard_map/ppermute | solution.py:65
  71.6 15.7 %collective-permute-start.19 = (bf16[32,4096]{1,0:T(8,128)(2,1)S(1)}, bf16[32,4096]{1,0:T(8,128)(2,1)S(1)}, u32[]{:S(2)}, u32[]{:S(2)}) collective-permute-start(bf16[32,4096]{1,0:T(8,128)(2,1)S(1)} %get-tuple-element.32), channel_id=1, source_target_pairs={{0,2},{1,3},{2,0},{3,1},{4,6},{5,7},{6,4},{7,5},{8,10},{9,11},{10,... | collective-permute-start | bytes 786440 | tf_op jit(solution)/shard_map/ppermute | solution.py:65
  77.1 13.3 %collective-permute-start.21 = (bf16[32,4096]{1,0:T(8,128)(2,1)S(1)}, bf16[32,4096]{1,0:T(8,128)(2,1)S(1)}, u32[]{:S(2)}, u32[]{:S(2)}) collective-permute-start(bf16[32,4096]{1,0:T(8,128)(2,1)S(1)} %fusion), channel_id=1, source_target_pairs={{0,4},{1,5},{2,6},{3,7},{4,0},{5,1},{6,2},{7,3},{8,12},{9,13},{10,... | collective-permute-start | bytes 786440 | tf_op jit(solution)/shard_map/ppermute | solution.py:65
  82.3 8.3 %collective-permute-start.25 = (bf16[128,1024]{1,0:T(8,128)(2,1)S(1)}, bf16[128,1024]{1,0:T(8,128)(2,1)S(1)}, u32[]{:S(2)}, u32[]{:S(2)}) collective-permute-start(bf16[128,1024]{1,0:T(8,128)(2,1)S(1)} %slice.35), channel_id=1, source_target_pairs={{0,16},{8,24},{16,0},{24,8},{1,17},{9,25},{17,1},{25,9},{2,18},{10... | collective-permute-start | bytes 786440 | tf_op jit(solution)/shard_map/ppermute | solution.py:65
  83.9 7.0 %collective-permute-start.26 = (bf16[128,1024]{1,0:T(8,128)(2,1)S(1)}, bf16[128,1024]{1,0:T(8,128)(2,1)S(1)}, u32[]{:S(2)}, u32[]{:S(2)}) collective-permute-start(bf16[128,1024]{1,0:T(8,128)(2,1)S(1)} %slice.36), channel_id=1, source_target_pairs={{0,8},{8,0},{16,24},{24,16},{1,9},{9,1},{17,25},{25,17},{2,10},{10... | collective-permute-start | bytes 786440 | tf_op jit(solution)/shard_map/ppermute | solution.py:65
  90.5 2.0 %copy-start.1 = (bf16[32,4096]{1,0:T(8,128)(2,1)}, bf16[32,4096]{1,0:T(8,128)(2,1)S(1)}, u32[]{:S(2)}) copy-start(bf16[32,4096]{1,0:T(8,128)(2,1)S(1)} %fusion.2.refs_4_) | copy-start | bytes 786436

commit v6 on v5

--- a/solution.py
+++ b/solution.py
@@ -256,14 +256,14 @@
     )(*parts, *after)
 
 
-def place_tiles(slots, listed, mine, sibling):
+def place_tiles(slots, listed, mine, sibling, after):
     chips, rows, columns = sibling.shape
     per = columns // BLK
     owned = slots.shape[0] // (2 * chips)
 
     def body(slots_ref, listed_ref, *refs):
         mine_refs, sibling_ref = refs[:chips], refs[chips]
-        outs, held = refs[chips + 1 : 2 * chips + 1], refs[2 * chips + 1]
+        outs, held = refs[-chips - 1 : -1], refs[-1]
         start = pl.multiple_of(place_on_mesh()[1] * rows, rows)
         for j in range(chips):
             held[j] = mine_refs[j][pl.ds(start, rows), :]
@@ -283,12 +283,12 @@
     return pl.pallas_call(
         body,
         out_shape=[shape] * chips,
-        in_specs=[SCALARS] * 2 + [WHOLE] * (chips + 1),
+        in_specs=[SCALARS] * 2 + [WHOLE] * (chips + 1) + [ANY] * len(after),
         out_specs=[WHOLE] * chips,
         scratch_shapes=[pltpu.VMEM((2 * chips, rows, columns), sibling.dtype)],
         compiler_params=pltpu.CompilerParams(vmem_limit_bytes=16 * MIB),
         cost_estimate=cost(0, (sibling, sibling)),
-    )(slots, listed, *mine, sibling)
+    )(slots, listed, *mine, sibling, *after)
 
 
 def logit_grads(logits, stats, mine, sibling, weight, cols, after, parts=4, ahead=3):
@@ -466,10 +466,16 @@
         given = [lax.dynamic_slice_in_dim(part, (1 - core) * rows, rows) for part in parts]
         return jnp.stack(given)
 
-    pieces = pieces + [far] + [swap(far, "vocab", 2 * j) for j in range(1, len(pieces))]
+    halves = [
+        [swap(far[k : k + rows // 2], "vocab", 2 * j) for k in (0, rows // 2)]
+        for j in range(1, len(pieces))
+    ]
     got = between_chips(
         [lax.dynamic_slice_in_dim(teacher, (chip ^ r) * 2 * rows, 2 * rows) for r in range(chips)]
     )
+    firsts, got = lax.optimization_barrier(([pair[0] for pair in halves], got))
+    seconds = [pair[1] for pair in halves]
+    pieces = pieces + [far] + [part for pair in zip(firsts, seconds) for part in pair]
     own = jnp.concatenate(pieces)
     other = swap(own, "vocab", 1)
     my_ids = lax.dynamic_index_in_dim(block_ids, me * rows // BLK, keepdims=False)
@@ -481,9 +487,10 @@
     slots = jnp.argmax(match, axis=1).astype(jnp.int32)
     source = slots // per
     place = ((source % 2) ^ core) * chips + ((source // 2) ^ chip)
-    placed = place_tiles(
-        place * per + slots % per, listed, got, swap(siblings_part(got), "vocab", 1)
-    )
+    from_sibling = swap(siblings_part(got), "vocab", 1)
+    seen = from_sibling[0, :TILE_ROWS, :BLK]
+    seen = lax.optimization_barrier(seen) * jnp.bfloat16(0.5)
+    placed = place_tiles(place * per + slots % per, listed, got, from_sibling, [seen])
     tiles = between_chips(placed)
 
     mass = jnp.sum(teacher, axis=1, dtype=jnp.float32)[None, :]

time: 92.8 us -> 92.8 us (level)
  waiting for transfers between devices: 38.9 us -> 36.7 us
  starting transfers between devices: 33.4 us -> 35.3 us
    ppermute x26 -> x27, waiting for transfers between devices: 38.9 us -> 36.7 us  [swap(): lax.ppermute(x, axis, [(i, i ^ bits) for i in range(lax.axis_size(axis))])]
    ppermute x26 -> x27, starting transfers between devices: 31.7 us -> 33.6 us  [swap(): lax.ppermute(x, axis, [(i, i ^ bits) for i in range(lax.axis_size(axis))])]
    reduce_sum x1, other arithmetic: 0.15 us -> 1.19 us  [shards(): mass = jnp.sum(teacher, axis=1, dtype=jnp.float32)[None, :]]
  transfers between devices with their start and end apart: 27 -> 28, of which waited for: 12 -> 14; matrix products, arithmetic and copies ran while one was open for 5% -> 5% of each run, Pallas kernels for 9% -> 9%
where the time goes in v6:
time: 92.8 us; the launch traced here: 92.6 us
  waiting for transfers between devices  36.7 us (40%)
  starting transfers between devices  35.3 us (38%)
  Pallas kernels  14.5 us (16%)
  other arithmetic  2.67 us (3%)
  local copies, waits for them, and re-layouts  2.47 us (3%)
    ppermute x27, waiting for transfers between devices, swap(): lax.ppermute(x, axis, [(i, i ^ bits) for i in range(lax.axis_size(axis))])  36.7 us
    ppermute x27, starting transfers between devices, swap(): lax.ppermute(x, axis, [(i, i ^ bits) for i in range(lax.axis_size(axis))])  33.6 us
    pallas_call x1, Pallas kernels, logits_and_stats(): pl.pallas_call(body, out_shape=[jax.ShapeDtypeStruct((tokens, vocab_rows)...  5.43 us
    pallas_call x1, Pallas kernels, logit_grads(): pl.pallas_call(body, out_shape=[jax.ShapeDtypeStruct((tokens, vocab_rows)...  4.5 us
  transfers between devices with their start and end apart: 28, of which 14 were waited for; matrix products, arithmetic and copies ran while one was open for 5% of the time, Pallas kernels for 9%

profile of v6, /device:TPU:0, one launch (start us, length us, event | category | flops | bytes accessed | tf_op | source)
XLA Modules:
  0.0 92.6 jit_solution(16265758311890294091)
XLA Ops:
  0.6 0.0 copy-start
  0.6 3.1 %collective-permute-start = (bf16[32,4096]{1,0:T(8,128)(2,1)}, bf16[32,4096]{1,0:T(8,128)(2,1)S(1)}, u32[]{:S(2)}, u32[]{:S(2)}) collective-permute-start(bf16[32,4096]{1,0:T(8,128)(2,1)} %param.4), channel_id=1, source_target_pairs={{0,2},{1,3},{2,0},{3,1},{4,6},{5,7},{6,4},{7,5},{8,10},{9,11},{10,... | collective-permute-start | bytes 786440 | tf_op jit(solution)/shard_map/ppermute | solution.py:65
  3.7 2.6 %collective-permute-start.1 = (bf16[32,4096]{1,0:T(8,128)(2,1)}, bf16[32,4096]{1,0:T(8,128)(2,1)S(1)}, u32[]{:S(2)}, u32[]{:S(2)}) collective-permute-start(bf16[32,4096]{1,0:T(8,128)(2,1)} %param.4), channel_id=1, source_target_pairs={{0,4},{1,5},{2,6},{3,7},{4,0},{5,1},{6,2},{7,3},{8,12},{9,13},{10,... | collective-permute-start | bytes 786440 | tf_op jit(solution)/shard_map/ppermute | solution.py:65
  6.3 1.1 %constant_dynamic-slice_fusion.1 = (bf16[64,1024]{1,0:T(8,128)(2,1)S(1)}, bf16[64,1024]{1,0:T(8,128)(2,1)S(1)}, bf16[64,1024]{1,0:T(8,128)(2,1)S(1)}, bf16[64,1024]{1,0:T(8,128)(2,1)S(1)}) fusion(bf16[256,1024]{1,0:T(8,128)(2,1)} %param.6, s32[]{:T(128)S(6)} %select_n.56, s32[]{:T(128)S(6)} %select_n.55, s32[]{:T(128)S(6)} %select_n.54, s32[]{:T(128)S(6)} %select_n.53), kind=kLoop, calls=%fused_computation.23 | loop fusion | bytes 1048592 | tf_op jit(solution)/shard_map/dynamic_slice | solution.py:474
  7.5 0.5 collective-permute-start.3
  8.0 0.0 collective-permute-start.4
  8.0 3.9 %collective-permute-start.5 = (bf16[64,1024]{1,0:T(8,128)(2,1)S(1)}, bf16[64,1024]{1,0:T(8,128)(2,1)S(1)}, u32[]{:S(2)}, u32[]{:S(2)}) collective-permute-start(bf16[64,1024]{1,0:T(8,128)(2,1)S(1)} %get-tuple-element.44), channel_id=1, source_target_pairs={{0,6},{1,7},{2,4},{3,5},{4,2},{5,3},{6,0},{7,1},{8,14},{9,15},{10,... | collective-permute-start | bytes 393224 | tf_op jit(solution)/shard_map/ppermute | solution.py:65
  11.9 1.0 %constant_dynamic-update-slice_fusion.4 = bf16[128,4096]{1,0:T(8,128)(2,1)S(1)} fusion(bf16[32,4096]{1,0:T(8,128)(2,1)} %param.4), kind=kLoop, calls=%fused_computation.18 | loop fusion | bytes 524288
  12.9 1.2 %convert_reduce_fusion = f32[256]{0:T(256)S(1)} fusion(bf16[256,1024]{1,0:T(8,128)(2,1)} %param.6), kind=kLoop, calls=%fused_computation.1 | loop fusion | flops 524032 | bytes 525312 | tf_op jit(solution)/shard_map/reduce_sum | solution.py:496
  14.1 0.1 stack.50
  14.2 0.1 iota_add_fusion
  14.3 0.1 add.98
  14.3 0.7 compare_reduce_fusion.1
  15.1 4.7 %collective-permute-done.1 = bf16[32,4096]{1,0:T(8,128)(2,1)S(1)} collective-permute-done((bf16[32,4096]{1,0:T(8,128)(2,1)}, bf16[32,4096]{1,0:T(8,128)(2,1)S(1)}, u32[]{:S(2)}, u32[]{:S(2)}) %collective-permute-start.1) | collective-permute-done | bytes 262176 | tf_op jit(solution)/shard_map/ppermute | solution.py:65
  19.8 0.3 collective-permute-start.2
  20.1 1.8 %collective-permute-start.6 = (bf16[16,4096]{1,0:T(8,128)(2,1)S(1)}, bf16[16,4096]{1,0:T(8,128)(2,1)S(1)}, u32[]{:S(2)}, u32[]{:S(2)}) collective-permute-start(bf16[16,4096]{1,0:T(8,128)(2,1)S(1)} %get-tuple-element.48), channel_id=1, source_target_pairs={{0,2},{1,3},{2,0},{3,1},{4,6},{5,7},{6,4},{7,5},{8,10},{9,11},{10,... | collective-permute-start | bytes 393224 | tf_op jit(solution)/shard_map/ppermute | solution.py:65
  22.0 6.2 %collective-permute-done.4.refs_2_ = bf16[64,1024]{1,0:T(8,128)(2,1)S(1)} collective-permute-done((bf16[64,1024]{1,0:T(8,128)(2,1)S(1)}, bf16[64,1024]{1,0:T(8,128)(2,1)S(1)}, u32[]{:S(2)}, u32[]{:S(2)}) %collective-permute-start.4) | collective-permute-done | bytes 131104 | tf_op jit(solution)/shard_map/ppermute | solution.py:65
  28.1 0.0 collective-permute-done.5.refs_3_
  28.1 0.4 collective-permute-done.2
  28.5 1.4 %collective-permute-done.6 = bf16[16,4096]{1,0:T(8,128)(2,1)S(1)} collective-permute-done((bf16[16,4096]{1,0:T(8,128)(2,1)S(1)}, bf16[16,4096]{1,0:T(8,128)(2,1)S(1)}, u32[]{:S(2)}, u32[]{:S(2)}) %collective-permute-start.6) | collective-permute-done | bytes 131104 | tf_op jit(solution)/shard_map/ppermute | solution.py:65
  29.9 0.1 collective-permute-start.7
  30.1 0.5 collective-permute-start.12
  30.7 0.2 compare_reduce_fusion
  30.9 2.2 %collective-permute-done.12.refs_4_ = bf16[4,32,1024]{2,1,0:T(8,128)(2,1)S(1)} collective-permute-done((bf16[4,32,1024]{2,1,0:T(8,128)(2,1)S(1)}, bf16[4,32,1024]{2,1,0:T(8,128)(2,1)S(1)}, u32[]{:S(2)}, u32[]{:S(2)}) %collective-permute-start.12) | collective-permute-done | bytes 262176 | tf_op jit(solution)/shard_map/ppermute | solution.py:65
  33.0 1.0 %shard_map.61 = (bf16[64,1024]{1,0:T(8,128)(2,1)S(1)}, bf16[64,1024]{1,0:T(8,128)(2,1)S(1)}, bf16[64,1024]{1,0:T(8,128)(2,1)S(1)}, bf16[64,1024]{1,0:T(8,128)(2,1)S(1)}) custom-call(s32[64]{0:T(128)S(1)} %fusion.3.slots_ref, s32[64]{0:T(128)S(1)} %convert_element_type.27.listed_ref, bf16[64,1024]{1,0:T(8,128)(2,1)S(1)} %get-tuple-element.25.refs_0_, ...), custom_call_target="tpu_custom_call" | custom-call | bytes 524288 | tf_op jit(solution)/shard_map/pallas_call | solution.py:283
  34.1 1.9 %collective-permute-start.13 = (bf16[64,1024]{1,0:T(8,128)(2,1)S(1)}, bf16[64,1024]{1,0:T(8,128)(2,1)S(1)}, u32[]{:S(2)}, u32[]{:S(2)}) collective-permute-start(bf16[64,1024]{1,0:T(8,128)(2,1)S(1)} %get-tuple-element.30), channel_id=1, source_target_pairs={{0,2},{1,3},{2,0},{3,1},{4,6},{5,7},{6,4},{7,5},{8,10},{9,11},{10,... | collective-permute-start | bytes 393224 | tf_op jit(solution)/shard_map/ppermute | solution.py:65
  36.0 2.5 %collective-permute-start.14 = (bf16[64,1024]{1,0:T(8,128)(2,1)S(1)}, bf16[64,1024]{1,0:T(8,128)(2,1)S(1)}, u32[]{:S(2)}, u32[]{:S(2)}) collective-permute-start(bf16[64,1024]{1,0:T(8,128)(2,1)S(1)} %get-tuple-element.31), channel_id=1, source_target_pairs={{0,4},{1,5},{2,6},{3,7},{4,0},{5,1},{6,2},{7,3},{8,12},{9,13},{10,... | collective-permute-start | bytes 393224 | tf_op jit(solution)/shard_map/ppermute | solution.py:65
  38.5 0.1 collective-permute-start.15
  38.5 0.0 collective-permute-done.7.refs_1_
  38.5 5.4 %shard_map.59 = (f32[256,1024]{1,0:T(8,128)S(1)}, f32[8,256]{1,0:T(8,128)S(1)}, bf16[256,1024]{1,0:T(8,128)(2,1)S(1)}, bf16[256,1024]{1,0:T(8,128)(2,1)S(1)}, bf16[128,1024]{1,0:T(8,128)(2,1)S(1)}) custom-call(bf16[128,4096]{1,0:T(8,128)(2,1)S(1)} %constant_dynamic-update-slice_fusion.refs_0_, bf16[128,4096]{1,0:T(8,128)(2,1)S(1)} %collective-permute-done.7.refs_1_, ...), custom_call_target="tpu_custom_call" | custom-call | flops 2147483648 | bytes 10486272 | tf_op jit(solution)/shard_map/pallas_call | solution.py:193
  44.0 1.7 %collective-permute-start.17 = (bf16[256,1024]{1,0:T(8,128)(2,1)S(1)}, bf16[256,1024]{1,0:T(8,128)(2,1)S(1)}, u32[]{:S(2)}, u32[]{:S(2)}) collective-permute-start(bf16[256,1024]{1,0:T(8,128)(2,1)S(1)} %get-tuple-element.33), channel_id=1, source_target_pairs={{0,8},{1,17},{2,10},{3,19},{4,12},{5,21},{6,14},{7,23},{8,0},{9,25... | collective-permute-start | bytes 1572872 | tf_op jit(solution)/shard_map/ppermute | solution.py:223
  45.7 0.0 collective-permute-start.8
  45.7 1.2 %collective-permute-done.8.b_ref = f32[8,256]{1,0:T(8,128)S(1)} collective-permute-done((f32[8,256]{1,0:T(8,128)S(1)}, f32[8,256]{1,0:T(8,128)S(1)}, u32[]{:S(2)}, u32[]{:S(2)}) %collective-permute-start.8) | collective-permute-done | bytes 8224 | tf_op jit(solution)/shard_map/ppermute | solution.py:65
  46.9 2.0 %collective-permute-done.14.refs_2_.refs_6_ = bf16[64,1024]{1,0:T(8,128)(2,1)S(1)} collective-permute-done((bf16[64,1024]{1,0:T(8,128)(2,1)S(1)}, bf16[64,1024]{1,0:T(8,128)(2,1)S(1)}, u32[]{:S(2)}, u32[]{:S(2)}) %collective-permute-start.14) | collective-permute-done | bytes 131104 | tf_op jit(solution)/shard_map/ppermute | solution.py:65
  48.9 0.0 collective-permute-done.15.refs_3_.refs_7_
  48.9 0.1 collective-permute-start.16
  49.0 2.5 %collective-permute-start.18 = (bf16[128,1024]{1,0:T(8,128)(2,1)S(1)}, bf16[128,1024]{1,0:T(8,128)(2,1)S(1)}, u32[]{:S(2)}, u32[]{:S(2)}) collective-permute-start(bf16[128,1024]{1,0:T(8,128)(2,1)S(1)} %get-tuple-element.34), channel_id=1, source_target_pairs={{0,24},{8,16},{16,8},{24,0},{1,25},{9,17},{17,9},{25,1},{2,26},{10... | collective-permute-start | bytes 786440 | tf_op jit(solution)/shard_map/ppermute | solution.py:65
  51.5 2.3 %collective-permute-start.9 = (f32[8,256]{1,0:T(8,128)S(1)}, f32[8,256]{1,0:T(8,128)S(1)}, u32[]{:S(2)}, u32[]{:S(2)}) collective-permute-start(f32[8,256]{1,0:T(8,128)S(1)} %shard_map.60.refs_4_.refs_0_), channel_id=1, source_target_pairs={{0,2},{1,3},{2,0},{3,1},{4,6},{5,7},{6,4},{7,5},{8,10},{9,11},{10,... | collective-permute-start | bytes 24584 | tf_op jit(solution)/shard_map/ppermute | solution.py:65
  53.8 1.0 %collective-permute-start.10 = (f32[8,256]{1,0:T(8,128)S(1)}, f32[8,256]{1,0:T(8,128)S(1)}, u32[]{:S(2)}, u32[]{:S(2)}) collective-permute-start(f32[8,256]{1,0:T(8,128)S(1)} %shard_map.60.refs_4_.refs_0_), channel_id=1, source_target_pairs={{0,4},{1,5},{2,6},{3,7},{4,0},{5,1},{6,2},{7,3},{8,12},{9,13},{10,... | collective-permute-start | bytes 24584 | tf_op jit(solution)/shard_map/ppermute | solution.py:65
  54.8 1.5 %collective-permute-start.11 = (f32[8,256]{1,0:T(8,128)S(1)}, f32[8,256]{1,0:T(8,128)S(1)}, u32[]{:S(2)}, u32[]{:S(2)}) collective-permute-start(f32[8,256]{1,0:T(8,128)S(1)} %shard_map.60.refs_4_.refs_0_), channel_id=1, source_target_pairs={{0,6},{1,7},{2,4},{3,5},{4,2},{5,3},{6,0},{7,1},{8,14},{9,15},{10,... | collective-permute-start | bytes 24584 | tf_op jit(solution)/shard_map/ppermute | solution.py:65
  56.2 0.0 collective-permute-done.9.refs_1_
  56.2 2.1 %collective-permute-done.10.refs_2_ = f32[8,256]{1,0:T(8,128)S(1)} collective-permute-done((f32[8,256]{1,0:T(8,128)S(1)}, f32[8,256]{1,0:T(8,128)S(1)}, u32[]{:S(2)}, u32[]{:S(2)}) %collective-permute-start.10) | collective-permute-done | bytes 8224 | tf_op jit(solution)/shard_map/ppermute | solution.py:65
  58.3 1.9 %collective-permute-done.11.refs_3_ = f32[8,256]{1,0:T(8,128)S(1)} collective-permute-done((f32[8,256]{1,0:T(8,128)S(1)}, f32[8,256]{1,0:T(8,128)S(1)}, u32[]{:S(2)}, u32[]{:S(2)}) %collective-permute-start.11) | collective-permute-done | bytes 8224 | tf_op jit(solution)/shard_map/ppermute | solution.py:65
  60.2 0.0 collective-permute-done.17.refs_10_
  60.2 4.5 %shard_map.63 = (bf16[256,1024]{1,0:T(8,128)(2,1)S(1)}, f32[128,4096]{1,0:T(8,128)S(1)}, bf16[128,4096]{1,0:T(8,128)(2,1)S(1)}, bf16[384,1024]{1,0:T(8,128)(2,1)S(1)}) custom-call(f32[256,1024]{1,0:T(8,128)S(1)} %get-tuple-element.22.logits_ref, f32[8,256]{1,0:T(8,128)S(1)} %shard_map.60.refs_4_.refs_0_, f32[8,256]{1,0:T(8,128)S(1)} %collective-permute-done.9.refs_1_, ...), custom_call_target="tpu_custom_call" | custom-call | flops 2147483648 | bytes 9715712 | tf_op jit(solution)/shard_map/pallas_call | solution.py:352
  64.7 0.1 collective-permute-start.19
  64.8 2.6 %collective-permute-done.19 = bf16[128,4096]{1,0:T(8,128)(2,1)S(1)} collective-permute-done((bf16[128,4096]{1,0:T(8,128)(2,1)S(1)}, bf16[128,4096]{1,0:T(8,128)(2,1)S(1)}, u32[]{:S(2)}, u32[]{:S(2)}) %collective-permute-start.19) | collective-permute-done | bytes 1048608 | tf_op jit(solution)/shard_map/ppermute | solution.py:65
  67.5 0.3 fusion.8
  67.8 0.7 collective-permute-start.21
  68.6 1.5 %collective-permute-start.23 = (bf16[256,1024]{1,0:T(8,128)(2,1)S(1)}, bf16[256,1024]{1,0:T(8,128)(2,1)S(1)}, u32[]{:S(2)}, u32[]{:S(2)}) collective-permute-start(bf16[256,1024]{1,0:T(8,128)(2,1)S(1)} %get-tuple-element.37.refs_0_), channel_id=1, source_target_pairs={{0,8},{8,0},{16,24},{24,16},{1,9},{9,1},{17,25},{25,17},{2,10},{10... | collective-permute-start | bytes 1572872 | tf_op jit(solution)/shard_map/ppermute | solution.py:65
  70.0 1.5 %collective-permute-start.24 = (bf16[256,1024]{1,0:T(8,128)(2,1)S(1)}, bf16[256,1024]{1,0:T(8,128)(2,1)S(1)}, u32[]{:S(2)}, u32[]{:S(2)}) collective-permute-start(bf16[256,1024]{1,0:T(8,128)(2,1)S(1)} %get-tuple-element.37.refs_0_), channel_id=1, source_target_pairs={{0,16},{8,24},{16,0},{24,8},{1,17},{9,25},{17,1},{25,9},{2,18},{10... | collective-permute-start | bytes 1572872 | tf_op jit(solution)/shard_map/ppermute | solution.py:65
  71.6 0.1 collective-permute-start.20
  71.7 5.4 %collective-permute-done.21 = bf16[32,4096]{1,0:T(8,128)(2,1)S(1)} collective-permute-done((bf16[32,4096]{1,0:T(8,128)(2,1)S(1)}, bf16[32,4096]{1,0:T(8,128)(2,1)S(1)}, u32[]{:S(2)}, u32[]{:S(2)}) %collective-permute-start.21) | collective-permute-done | bytes 262176 | tf_op jit(solution)/shard_map/ppermute | solution.py:65
  77.1 1.9 %collective-permute-start.22 = (bf16[32,4096]{1,0:T(8,128)(2,1)S(1)}, bf16[32,4096]{1,0:T(8,128)(2,1)S(1)}, u32[]{:S(2)}, u32[]{:S(2)}) collective-permute-start(bf16[32,4096]{1,0:T(8,128)(2,1)S(1)} %fusion), channel_id=1, source_target_pairs={{0,4},{1,5},{2,6},{3,7},{4,0},{5,1},{6,2},{7,3},{8,12},{9,13},{10,... | collective-permute-start | bytes 786440 | tf_op jit(solution)/shard_map/ppermute | solution.py:65
  79.0 3.2 %collective-permute-done.23.refs_1_ = bf16[256,1024]{1,0:T(8,128)(2,1)S(1)} collective-permute-done((bf16[256,1024]{1,0:T(8,128)(2,1)S(1)}, bf16[256,1024]{1,0:T(8,128)(2,1)S(1)}, u32[]{:S(2)}, u32[]{:S(2)}) %collective-permute-start.23) | collective-permute-done | bytes 524320 | tf_op jit(solution)/shard_map/ppermute | solution.py:65
  82.3 1.6 %collective-permute-start.26 = (bf16[128,1024]{1,0:T(8,128)(2,1)S(1)}, bf16[128,1024]{1,0:T(8,128)(2,1)S(1)}, u32[]{:S(2)}, u32[]{:S(2)}) collective-permute-start(bf16[128,1024]{1,0:T(8,128)(2,1)S(1)} %slice.50), channel_id=1, source_target_pairs={{0,16},{8,24},{16,0},{24,8},{1,17},{9,25},{17,1},{25,9},{2,18},{10... | collective-permute-start | bytes 786440 | tf_op jit(solution)/shard_map/ppermute | solution.py:65
  83.8 0.0 collective-permute-done.24.refs_2_
  83.9 1.6 %collective-permute-start.27 = (bf16[128,1024]{1,0:T(8,128)(2,1)S(1)}, bf16[128,1024]{1,0:T(8,128)(2,1)S(1)}, u32[]{:S(2)}, u32[]{:S(2)}) collective-permute-start(bf16[128,1024]{1,0:T(8,128)(2,1)S(1)} %slice.51), channel_id=1, source_target_pairs={{0,8},{8,0},{16,24},{24,16},{1,9},{9,1},{17,25},{25,17},{2,10},{10... | collective-permute-start | bytes 786440 | tf_op jit(solution)/shard_map/ppermute | solution.py:65
  85.4 1.9 %shard_map.64.partial_ref = f32[1024,1024]{1,0:T(8,128)S(1)} custom-call(bf16[256,1024]{1,0:T(8,128)(2,1)S(1)} %get-tuple-element.37.refs_0_, bf16[256,1024]{1,0:T(8,128)(2,1)S(1)} %collective-permute-done.23.refs_1_, bf16[256,1024]{1,0:T(8,128)(2,1)S(1)} %collective-permute-done.24.refs_2_, bf16[256,1024]{1,0:T(8,128)(2,1)S(1)} %get-tuple-element.38.refs_3_, ...), custom_call_target="tpu_custom_call" | custom-call | flops 1610612736 | bytes 3670016 | tf_op jit(solution)/shard_map/pallas_call | solution.py:399
  87.3 3.1 %collective-permute-done.22 = bf16[32,4096]{1,0:T(8,128)(2,1)S(1)} collective-permute-done((bf16[32,4096]{1,0:T(8,128)(2,1)S(1)}, bf16[32,4096]{1,0:T(8,128)(2,1)S(1)}, u32[]{:S(2)}, u32[]{:S(2)}) %collective-permute-start.22) | collective-permute-done | bytes 262176 | tf_op jit(solution)/shard_map/ppermute | solution.py:65
  90.4 0.1 fusion.2.refs_4_
  90.5 0.0 copy-start.1
  90.6 0.3 collective-permute-done.27.refs_1_
  90.9 1.7 %shard_map.65 = bf16[1024,1024]{1,0:T(8,128)(2,1)} custom-call(f32[1024,1024]{1,0:T(8,128)S(1)} %shard_map.64.partial_ref, bf16[128,1024]{1,0:T(8,128)(2,1)S(1)} %collective-permute-done.26.refs_0_, bf16[128,1024]{1,0:T(8,128)(2,1)S(1)} %collective-permute-done.27.refs_1_, bf16[384,1024]{1,0:T(8,128)(2,1)S(1)} %get-tuple-element.39.refs_4_.refs_2_, ...), custom_call_target="tpu_custom_call" | custom-call | flops 536870912 | bytes 4194304 | tf_op jit(solution)/shard_map/pallas_call | solution.py:434
  (32 shorter events, 0.4 us)
Async XLA Ops:
  0.6 13.6 %copy-start = (s32[2,64]{1,0:T(2,128)S(1)}, s32[2,64]{1,0:T(2,128)}, u32[]{:S(2)}) copy-start(s32[2,64]{1,0:T(2,128)} %param.7) | copy-start | bytes 1540
  0.6 19.5 %collective-permute-start = (bf16[32,4096]{1,0:T(8,128)(2,1)}, bf16[32,4096]{1,0:T(8,128)(2,1)S(1)}, u32[]{:S(2)}, u32[]{:S(2)}) collective-permute-start(bf16[32,4096]{1,0:T(8,128)(2,1)} %param.4), channel_id=1, source_target_pairs={{0,2},{1,3},{2,0},{3,1},{4,6},{5,7},{6,4},{7,5},{8,10},{9,11},{10,... | collective-permute-start | bytes 786440 | tf_op jit(solution)/shard_map/ppermute | solution.py:65
  3.7 16.1 %collective-permute-start.1 = (bf16[32,4096]{1,0:T(8,128)(2,1)}, bf16[32,4096]{1,0:T(8,128)(2,1)S(1)}, u32[]{:S(2)}, u32[]{:S(2)}) collective-permute-start(bf16[32,4096]{1,0:T(8,128)(2,1)} %param.4), channel_id=1, source_target_pairs={{0,4},{1,5},{2,6},{3,7},{4,0},{5,1},{6,2},{7,3},{8,12},{9,13},{10,... | collective-permute-start | bytes 786440 | tf_op jit(solution)/shard_map/ppermute | solution.py:65
  7.5 14.5 %collective-permute-start.3 = (bf16[64,1024]{1,0:T(8,128)(2,1)S(1)}, bf16[64,1024]{1,0:T(8,128)(2,1)S(1)}, u32[]{:S(2)}, u32[]{:S(2)}) collective-permute-start(bf16[64,1024]{1,0:T(8,128)(2,1)S(1)} %get-tuple-element.46), channel_id=1, source_target_pairs={{0,2},{1,3},{2,0},{3,1},{4,6},{5,7},{6,4},{7,5},{8,10},{9,11},{10,... | collective-permute-start | bytes 393224 | tf_op jit(solution)/shard_map/ppermute | solution.py:65
  8.0 20.1 %collective-permute-start.4 = (bf16[64,1024]{1,0:T(8,128)(2,1)S(1)}, bf16[64,1024]{1,0:T(8,128)(2,1)S(1)}, u32[]{:S(2)}, u32[]{:S(2)}) collective-permute-start(bf16[64,1024]{1,0:T(8,128)(2,1)S(1)} %get-tuple-element.45), channel_id=1, source_target_pairs={{0,4},{1,5},{2,6},{3,7},{4,0},{5,1},{6,2},{7,3},{8,12},{9,13},{10,... | collective-permute-start | bytes 393224 | tf_op jit(solution)/shard_map/ppermute | solution.py:65
  8.0 20.1 %collective-permute-start.5 = (bf16[64,1024]{1,0:T(8,128)(2,1)S(1)}, bf16[64,1024]{1,0:T(8,128)(2,1)S(1)}, u32[]{:S(2)}, u32[]{:S(2)}) collective-permute-start(bf16[64,1024]{1,0:T(8,128)(2,1)S(1)} %get-tuple-element.44), channel_id=1, source_target_pairs={{0,6},{1,7},{2,4},{3,5},{4,2},{5,3},{6,0},{7,1},{8,14},{9,15},{10,... | collective-permute-start | bytes 393224 | tf_op jit(solution)/shard_map/ppermute | solution.py:65
  19.8 8.7 %collective-permute-start.2 = (bf16[16,4096]{1,0:T(8,128)(2,1)S(1)}, bf16[16,4096]{1,0:T(8,128)(2,1)S(1)}, u32[]{:S(2)}, u32[]{:S(2)}) collective-permute-start(bf16[16,4096]{1,0:T(8,128)(2,1)S(1)} %get-tuple-element.49), channel_id=1, source_target_pairs={{0,2},{1,3},{2,0},{3,1},{4,6},{5,7},{6,4},{7,5},{8,10},{9,11},{10,... | collective-permute-start | bytes 393224 | tf_op jit(solution)/shard_map/ppermute | solution.py:65
  20.1 9.8 %collective-permute-start.6 = (bf16[16,4096]{1,0:T(8,128)(2,1)S(1)}, bf16[16,4096]{1,0:T(8,128)(2,1)S(1)}, u32[]{:S(2)}, u32[]{:S(2)}) collective-permute-start(bf16[16,4096]{1,0:T(8,128)(2,1)S(1)} %get-tuple-element.48), channel_id=1, source_target_pairs={{0,2},{1,3},{2,0},{3,1},{4,6},{5,7},{6,4},{7,5},{8,10},{9,11},{10,... | collective-permute-start | bytes 393224 | tf_op jit(solution)/shard_map/ppermute | solution.py:65
  29.9 8.6 %collective-permute-start.7 = (bf16[128,4096]{1,0:T(8,128)(2,1)S(1)}, bf16[128,4096]{1,0:T(8,128)(2,1)S(1)}, u32[]{:S(2)}, u32[]{:S(2)}) collective-permute-start(bf16[128,4096]{1,0:T(8,128)(2,1)S(1)} %constant_dynamic-update-slice_fusion.refs_0_), channel_id=1, source_target_pairs={{0,1},{1,0},{2,3},{3,2},{4,5},{5,4},{6,7},{7,6},{8,9},{9,8},{10,11... | collective-permute-start | bytes 3145736 | tf_op jit(solution)/shard_map/ppermute | solution.py:65
  30.1 2.9 %collective-permute-start.12 = (bf16[4,32,1024]{2,1,0:T(8,128)(2,1)S(1)}, bf16[4,32,1024]{2,1,0:T(8,128)(2,1)S(1)}, u32[]{:S(2)}, u32[]{:S(2)}) collective-permute-start(bf16[4,32,1024]{2,1,0:T(8,128)(2,1)S(1)} %pad_maximum_fusion), channel_id=1, source_target_pairs={{0,1},{1,0},{2,3},{3,2},{4,5},{5,4},{6,7},{7,6},{8,9},{9,8},{10,11... | collective-permute-start | bytes 786440 | tf_op jit(solution)/shard_map/ppermute | solution.py:65
  34.1 12.8 %collective-permute-start.13 = (bf16[64,1024]{1,0:T(8,128)(2,1)S(1)}, bf16[64,1024]{1,0:T(8,128)(2,1)S(1)}, u32[]{:S(2)}, u32[]{:S(2)}) collective-permute-start(bf16[64,1024]{1,0:T(8,128)(2,1)S(1)} %get-tuple-element.30), channel_id=1, source_target_pairs={{0,2},{1,3},{2,0},{3,1},{4,6},{5,7},{6,4},{7,5},{8,10},{9,11},{10,... | collective-permute-start | bytes 393224 | tf_op jit(solution)/shard_map/ppermute | solution.py:65
  36.0 12.9 %collective-permute-start.14 = (bf16[64,1024]{1,0:T(8,128)(2,1)S(1)}, bf16[64,1024]{1,0:T(8,128)(2,1)S(1)}, u32[]{:S(2)}, u32[]{:S(2)}) collective-permute-start(bf16[64,1024]{1,0:T(8,128)(2,1)S(1)} %get-tuple-element.31), channel_id=1, source_target_pairs={{0,4},{1,5},{2,6},{3,7},{4,0},{5,1},{6,2},{7,3},{8,12},{9,13},{10,... | collective-permute-start | bytes 393224 | tf_op jit(solution)/shard_map/ppermute | solution.py:65
  38.5 10.4 %collective-permute-start.15 = (bf16[64,1024]{1,0:T(8,128)(2,1)S(1)}, bf16[64,1024]{1,0:T(8,128)(2,1)S(1)}, u32[]{:S(2)}, u32[]{:S(2)}) collective-permute-start(bf16[64,1024]{1,0:T(8,128)(2,1)S(1)} %get-tuple-element.32), channel_id=1, source_target_pairs={{0,6},{1,7},{2,4},{3,5},{4,2},{5,3},{6,0},{7,1},{8,14},{9,15},{10,... | collective-permute-start | bytes 393224 | tf_op jit(solution)/shard_map/ppermute | solution.py:65
  44.0 16.3 %collective-permute-start.17 = (bf16[256,1024]{1,0:T(8,128)(2,1)S(1)}, bf16[256,1024]{1,0:T(8,128)(2,1)S(1)}, u32[]{:S(2)}, u32[]{:S(2)}) collective-permute-start(bf16[256,1024]{1,0:T(8,128)(2,1)S(1)} %get-tuple-element.33), channel_id=1, source_target_pairs={{0,8},{1,17},{2,10},{3,19},{4,12},{5,21},{6,14},{7,23},{8,0},{9,25... | collective-permute-start | bytes 1572872 | tf_op jit(solution)/shard_map/ppermute | solution.py:223
  45.7 1.2 %collective-permute-start.8 = (f32[8,256]{1,0:T(8,128)S(1)}, f32[8,256]{1,0:T(8,128)S(1)}, u32[]{:S(2)}, u32[]{:S(2)}) collective-permute-start(f32[8,256]{1,0:T(8,128)S(1)} %get-tuple-element.23.a_ref), channel_id=1, source_target_pairs={{0,1},{1,0},{2,3},{3,2},{4,5},{5,4},{6,7},{7,6},{8,9},{9,8},{10,11... | collective-permute-start | bytes 24584 | tf_op jit(solution)/shard_map/ppermute | solution.py:65
  48.9 5.9 %collective-permute-start.16 = (bf16[4,32,1024]{2,1,0:T(8,128)(2,1)S(1)}, bf16[4,32,1024]{2,1,0:T(8,128)(2,1)S(1)}, u32[]{:S(2)}, u32[]{:S(2)}) collective-permute-start(bf16[4,32,1024]{2,1,0:T(8,128)(2,1)S(1)} %shard_map.62), channel_id=1, source_target_pairs={{0,1},{1,0},{2,3},{3,2},{4,5},{5,4},{6,7},{7,6},{8,9},{9,8},{10,11... | collective-permute-start | bytes 786440 | tf_op jit(solution)/shard_map/ppermute | solution.py:65
  49.0 11.3 %collective-permute-start.18 = (bf16[128,1024]{1,0:T(8,128)(2,1)S(1)}, bf16[128,1024]{1,0:T(8,128)(2,1)S(1)}, u32[]{:S(2)}, u32[]{:S(2)}) collective-permute-start(bf16[128,1024]{1,0:T(8,128)(2,1)S(1)} %get-tuple-element.34), channel_id=1, source_target_pairs={{0,24},{8,16},{16,8},{24,0},{1,25},{9,17},{17,9},{25,1},{2,26},{10... | collective-permute-start | bytes 786440 | tf_op jit(solution)/shard_map/ppermute | solution.py:65
  51.5 4.8 %collective-permute-start.9 = (f32[8,256]{1,0:T(8,128)S(1)}, f32[8,256]{1,0:T(8,128)S(1)}, u32[]{:S(2)}, u32[]{:S(2)}) collective-permute-start(f32[8,256]{1,0:T(8,128)S(1)} %shard_map.60.refs_4_.refs_0_), channel_id=1, source_target_pairs={{0,2},{1,3},{2,0},{3,1},{4,6},{5,7},{6,4},{7,5},{8,10},{9,11},{10,... | collective-permute-start | bytes 24584 | tf_op jit(solution)/shard_map/ppermute | solution.py:65
  53.8 4.5 %collective-permute-start.10 = (f32[8,256]{1,0:T(8,128)S(1)}, f32[8,256]{1,0:T(8,128)S(1)}, u32[]{:S(2)}, u32[]{:S(2)}) collective-permute-start(f32[8,256]{1,0:T(8,128)S(1)} %shard_map.60.refs_4_.refs_0_), channel_id=1, source_target_pairs={{0,4},{1,5},{2,6},{3,7},{4,0},{5,1},{6,2},{7,3},{8,12},{9,13},{10,... | collective-permute-start | bytes 24584 | tf_op jit(solution)/shard_map/ppermute | solution.py:65
  54.8 5.4 %collective-permute-start.11 = (f32[8,256]{1,0:T(8,128)S(1)}, f32[8,256]{1,0:T(8,128)S(1)}, u32[]{:S(2)}, u32[]{:S(2)}) collective-permute-start(f32[8,256]{1,0:T(8,128)S(1)} %shard_map.60.refs_4_.refs_0_), channel_id=1, source_target_pairs={{0,6},{1,7},{2,4},{3,5},{4,2},{5,3},{6,0},{7,1},{8,14},{9,15},{10,... | collective-permute-start | bytes 24584 | tf_op jit(solution)/shard_map/ppermute | solution.py:65
  64.7 2.7 %collective-permute-start.19 = (bf16[128,4096]{1,0:T(8,128)(2,1)S(1)}, bf16[128,4096]{1,0:T(8,128)(2,1)S(1)}, u32[]{:S(2)}, u32[]{:S(2)}) collective-permute-start(bf16[128,4096]{1,0:T(8,128)(2,1)S(1)} %get-tuple-element.36), channel_id=1, source_target_pairs={{0,1},{1,0},{2,3},{3,2},{4,5},{5,4},{6,7},{7,6},{8,9},{9,8},{10,11... | collective-permute-start | bytes 3145736 | tf_op jit(solution)/shard_map/ppermute | solution.py:65
  67.8 9.2 %collective-permute-start.21 = (bf16[32,4096]{1,0:T(8,128)(2,1)S(1)}, bf16[32,4096]{1,0:T(8,128)(2,1)S(1)}, u32[]{:S(2)}, u32[]{:S(2)}) collective-permute-start(bf16[32,4096]{1,0:T(8,128)(2,1)S(1)} %get-tuple-element.43), channel_id=1, source_target_pairs={{0,2},{1,3},{2,0},{3,1},{4,6},{5,7},{6,4},{7,5},{8,10},{9,11},{10,... | collective-permute-start | bytes 786440 | tf_op jit(solution)/shard_map/ppermute | solution.py:65
  68.6 13.7 %collective-permute-start.23 = (bf16[256,1024]{1,0:T(8,128)(2,1)S(1)}, bf16[256,1024]{1,0:T(8,128)(2,1)S(1)}, u32[]{:S(2)}, u32[]{:S(2)}) collective-permute-start(bf16[256,1024]{1,0:T(8,128)(2,1)S(1)} %get-tuple-element.37.refs_0_), channel_id=1, source_target_pairs={{0,8},{8,0},{16,24},{24,16},{1,9},{9,1},{17,25},{25,17},{2,10},{10... | collective-permute-start | bytes 1572872 | tf_op jit(solution)/shard_map/ppermute | solution.py:65
  70.0 13.8 %collective-permute-start.24 = (bf16[256,1024]{1,0:T(8,128)(2,1)S(1)}, bf16[256,1024]{1,0:T(8,128)(2,1)S(1)}, u32[]{:S(2)}, u32[]{:S(2)}) collective-permute-start(bf16[256,1024]{1,0:T(8,128)(2,1)S(1)} %get-tuple-element.37.refs_0_), channel_id=1, source_target_pairs={{0,16},{8,24},{16,0},{24,8},{1,17},{9,25},{17,1},{25,9},{2,18},{10... | collective-permute-start | bytes 1572872 | tf_op jit(solution)/shard_map/ppermute | solution.py:65
  71.6 13.9 %collective-permute-start.25 = (bf16[384,1024]{1,0:T(8,128)(2,1)S(1)}, bf16[384,1024]{1,0:T(8,128)(2,1)S(1)}, u32[]{:S(2)}, u32[]{:S(2)}) collective-permute-start(bf16[384,1024]{1,0:T(8,128)(2,1)S(1)} %get-tuple-element.39.refs_4_.refs_2_), channel_id=1, source_target_pairs={{0,1},{1,0},{2,3},{3,2},{4,5},{5,4},{6,7},{7,6},{8,9},{9,8},{10,11... | collective-permute-start | bytes 2359304 | tf_op jit(solution)/shard_map/ppermute | solution.py:65
  71.6 15.7 %collective-permute-start.20 = (bf16[32,4096]{1,0:T(8,128)(2,1)S(1)}, bf16[32,4096]{1,0:T(8,128)(2,1)S(1)}, u32[]{:S(2)}, u32[]{:S(2)}) collective-permute-start(bf16[32,4096]{1,0:T(8,128)(2,1)S(1)} %get-tuple-element.42), channel_id=1, source_target_pairs={{0,2},{1,3},{2,0},{3,1},{4,6},{5,7},{6,4},{7,5},{8,10},{9,11},{10,... | collective-permute-start | bytes 786440 | tf_op jit(solution)/shard_map/ppermute | solution.py:65
  77.1 13.3 %collective-permute-start.22 = (bf16[32,4096]{1,0:T(8,128)(2,1)S(1)}, bf16[32,4096]{1,0:T(8,128)(2,1)S(1)}, u32[]{:S(2)}, u32[]{:S(2)}) collective-permute-start(bf16[32,4096]{1,0:T(8,128)(2,1)S(1)} %fusion), channel_id=1, source_target_pairs={{0,4},{1,5},{2,6},{3,7},{4,0},{5,1},{6,2},{7,3},{8,12},{9,13},{10,... | collective-permute-start | bytes 786440 | tf_op jit(solution)/shard_map/ppermute | solution.py:65
  82.3 8.3 %collective-permute-start.26 = (bf16[128,1024]{1,0:T(8,128)(2,1)S(1)}, bf16[128,1024]{1,0:T(8,128)(2,1)S(1)}, u32[]{:S(2)}, u32[]{:S(2)}) collective-permute-start(bf16[128,1024]{1,0:T(8,128)(2,1)S(1)} %slice.50), channel_id=1, source_target_pairs={{0,16},{8,24},{16,0},{24,8},{1,17},{9,25},{17,1},{25,9},{2,18},{10... | collective-permute-start | bytes 786440 | tf_op jit(solution)/shard_map/ppermute | solution.py:65
  83.9 7.0 %collective-permute-start.27 = (bf16[128,1024]{1,0:T(8,128)(2,1)S(1)}, bf16[128,1024]{1,0:T(8,128)(2,1)S(1)}, u32[]{:S(2)}, u32[]{:S(2)}) collective-permute-start(bf16[128,1024]{1,0:T(8,128)(2,1)S(1)} %slice.51), channel_id=1, source_target_pairs={{0,8},{8,0},{16,24},{24,16},{1,9},{9,1},{17,25},{25,17},{2,10},{10... | collective-permute-start | bytes 786440 | tf_op jit(solution)/shard_map/ppermute | solution.py:65
  90.5 2.0 %copy-start.1 = (bf16[32,4096]{1,0:T(8,128)(2,1)}, bf16[32,4096]{1,0:T(8,128)(2,1)S(1)}, u32[]{:S(2)}) copy-start(bf16[32,4096]{1,0:T(8,128)(2,1)S(1)} %fusion.2.refs_4_) | copy-start | bytes 786436

commit v7 on v6

--- a/solution.py
+++ b/solution.py
@@ -460,7 +460,8 @@
     far = swap(hidden, "vocab", 2 * len(pieces))
 
     def between_chips(parts):
-        return [parts[0]] + [swap(parts[r], "vocab", 2 * r) for r in range(1, chips)]
+        moved = [swap(parts[r], "vocab", 2 * r) for r in reversed(range(1, chips))]
+        return [parts[0]] + moved[::-1]
 
     def siblings_part(parts):
         given = [lax.dynamic_slice_in_dim(part, (1 - core) * rows, rows) for part in parts]

time: 92.8 us -> 92.8 us (level)
  no operation moved by 1% of the time
where the time goes in v7:
time: 92.8 us; the launch traced here: 92.6 us
  waiting for transfers between devices  36.7 us (40%)
  starting transfers between devices  35.3 us (38%)
  Pallas kernels  14.5 us (16%)
  other arithmetic  2.67 us (3%)
  local copies, waits for them, and re-layouts  2.47 us (3%)
    ppermute x27, waiting for transfers between devices, swap(): lax.ppermute(x, axis, [(i, i ^ bits) for i in range(lax.axis_size(axis))])  36.7 us
    ppermute x27, starting transfers between devices, swap(): lax.ppermute(x, axis, [(i, i ^ bits) for i in range(lax.axis_size(axis))])  33.6 us
    pallas_call x1, Pallas kernels, logits_and_stats(): pl.pallas_call(body, out_shape=[jax.ShapeDtypeStruct((tokens, vocab_rows)...  5.43 us
    pallas_call x1, Pallas kernels, logit_grads(): pl.pallas_call(body, out_shape=[jax.ShapeDtypeStruct((tokens, vocab_rows)...  4.5 us
  transfers between devices with their start and end apart: 28, of which 14 were waited for; matrix products, arithmetic and copies ran while one was open for 5% of the time, Pallas kernels for 9%

profile of v7, /device:TPU:0, one launch (start us, length us, event | category | flops | bytes accessed | tf_op | source)
XLA Modules:
  0.0 92.6 jit_solution(16265758311890294091)
XLA Ops:
  0.6 0.0 copy-start
  0.6 3.1 %collective-permute-start = (bf16[32,4096]{1,0:T(8,128)(2,1)}, bf16[32,4096]{1,0:T(8,128)(2,1)S(1)}, u32[]{:S(2)}, u32[]{:S(2)}) collective-permute-start(bf16[32,4096]{1,0:T(8,128)(2,1)} %param.4), channel_id=1, source_target_pairs={{0,2},{1,3},{2,0},{3,1},{4,6},{5,7},{6,4},{7,5},{8,10},{9,11},{10,... | collective-permute-start | bytes 786440 | tf_op jit(solution)/shard_map/ppermute | solution.py:65
  3.7 2.6 %collective-permute-start.1 = (bf16[32,4096]{1,0:T(8,128)(2,1)}, bf16[32,4096]{1,0:T(8,128)(2,1)S(1)}, u32[]{:S(2)}, u32[]{:S(2)}) collective-permute-start(bf16[32,4096]{1,0:T(8,128)(2,1)} %param.4), channel_id=1, source_target_pairs={{0,4},{1,5},{2,6},{3,7},{4,0},{5,1},{6,2},{7,3},{8,12},{9,13},{10,... | collective-permute-start | bytes 786440 | tf_op jit(solution)/shard_map/ppermute | solution.py:65
  6.3 1.1 %constant_dynamic-slice_fusion.1 = (bf16[64,1024]{1,0:T(8,128)(2,1)S(1)}, bf16[64,1024]{1,0:T(8,128)(2,1)S(1)}, bf16[64,1024]{1,0:T(8,128)(2,1)S(1)}, bf16[64,1024]{1,0:T(8,128)(2,1)S(1)}) fusion(bf16[256,1024]{1,0:T(8,128)(2,1)} %param.6, s32[]{:T(128)S(6)} %select_n.56, s32[]{:T(128)S(6)} %select_n.55, s32[]{:T(128)S(6)} %select_n.54, s32[]{:T(128)S(6)} %select_n.53), kind=kLoop, calls=%fused_computation.23 | loop fusion | bytes 1048592 | tf_op jit(solution)/shard_map/dynamic_slice | solution.py:475
  7.5 0.5 collective-permute-start.3
  8.0 0.0 collective-permute-start.4
  8.0 3.9 %collective-permute-start.5 = (bf16[64,1024]{1,0:T(8,128)(2,1)S(1)}, bf16[64,1024]{1,0:T(8,128)(2,1)S(1)}, u32[]{:S(2)}, u32[]{:S(2)}) collective-permute-start(bf16[64,1024]{1,0:T(8,128)(2,1)S(1)} %get-tuple-element.44), channel_id=1, source_target_pairs={{0,6},{1,7},{2,4},{3,5},{4,2},{5,3},{6,0},{7,1},{8,14},{9,15},{10,... | collective-permute-start | bytes 393224 | tf_op jit(solution)/shard_map/ppermute | solution.py:65
  11.9 1.0 %constant_dynamic-update-slice_fusion.4 = bf16[128,4096]{1,0:T(8,128)(2,1)S(1)} fusion(bf16[32,4096]{1,0:T(8,128)(2,1)} %param.4), kind=kLoop, calls=%fused_computation.18 | loop fusion | bytes 524288
  12.9 1.2 %convert_reduce_fusion = f32[256]{0:T(256)S(1)} fusion(bf16[256,1024]{1,0:T(8,128)(2,1)} %param.6), kind=kLoop, calls=%fused_computation.1 | loop fusion | flops 524032 | bytes 525312 | tf_op jit(solution)/shard_map/reduce_sum | solution.py:497
  14.1 0.1 stack.50
  14.2 0.1 iota_add_fusion
  14.3 0.1 add.98
  14.3 0.7 compare_reduce_fusion.1
  15.1 4.7 %collective-permute-done.1 = bf16[32,4096]{1,0:T(8,128)(2,1)S(1)} collective-permute-done((bf16[32,4096]{1,0:T(8,128)(2,1)}, bf16[32,4096]{1,0:T(8,128)(2,1)S(1)}, u32[]{:S(2)}, u32[]{:S(2)}) %collective-permute-start.1) | collective-permute-done | bytes 262176 | tf_op jit(solution)/shard_map/ppermute | solution.py:65
  19.8 0.3 collective-permute-start.2
  20.1 1.8 %collective-permute-start.6 = (bf16[16,4096]{1,0:T(8,128)(2,1)S(1)}, bf16[16,4096]{1,0:T(8,128)(2,1)S(1)}, u32[]{:S(2)}, u32[]{:S(2)}) collective-permute-start(bf16[16,4096]{1,0:T(8,128)(2,1)S(1)} %get-tuple-element.48), channel_id=1, source_target_pairs={{0,2},{1,3},{2,0},{3,1},{4,6},{5,7},{6,4},{7,5},{8,10},{9,11},{10,... | collective-permute-start | bytes 393224 | tf_op jit(solution)/shard_map/ppermute | solution.py:65
  22.0 6.2 %collective-permute-done.4.refs_2_ = bf16[64,1024]{1,0:T(8,128)(2,1)S(1)} collective-permute-done((bf16[64,1024]{1,0:T(8,128)(2,1)S(1)}, bf16[64,1024]{1,0:T(8,128)(2,1)S(1)}, u32[]{:S(2)}, u32[]{:S(2)}) %collective-permute-start.4) | collective-permute-done | bytes 131104 | tf_op jit(solution)/shard_map/ppermute | solution.py:65
  28.1 0.0 collective-permute-done.5.refs_3_
  28.1 0.4 collective-permute-done.2
  28.5 1.4 %collective-permute-done.6 = bf16[16,4096]{1,0:T(8,128)(2,1)S(1)} collective-permute-done((bf16[16,4096]{1,0:T(8,128)(2,1)S(1)}, bf16[16,4096]{1,0:T(8,128)(2,1)S(1)}, u32[]{:S(2)}, u32[]{:S(2)}) %collective-permute-start.6) | collective-permute-done | bytes 131104 | tf_op jit(solution)/shard_map/ppermute | solution.py:65
  29.9 0.1 collective-permute-start.7
  30.1 0.5 collective-permute-start.12
  30.7 0.2 compare_reduce_fusion
  30.9 2.2 %collective-permute-done.12.refs_4_ = bf16[4,32,1024]{2,1,0:T(8,128)(2,1)S(1)} collective-permute-done((bf16[4,32,1024]{2,1,0:T(8,128)(2,1)S(1)}, bf16[4,32,1024]{2,1,0:T(8,128)(2,1)S(1)}, u32[]{:S(2)}, u32[]{:S(2)}) %collective-permute-start.12) | collective-permute-done | bytes 262176 | tf_op jit(solution)/shard_map/ppermute | solution.py:65
  33.0 1.0 %shard_map.61 = (bf16[64,1024]{1,0:T(8,128)(2,1)S(1)}, bf16[64,1024]{1,0:T(8,128)(2,1)S(1)}, bf16[64,1024]{1,0:T(8,128)(2,1)S(1)}, bf16[64,1024]{1,0:T(8,128)(2,1)S(1)}) custom-call(s32[64]{0:T(128)S(1)} %fusion.3.slots_ref, s32[64]{0:T(128)S(1)} %convert_element_type.27.listed_ref, bf16[64,1024]{1,0:T(8,128)(2,1)S(1)} %get-tuple-element.25.refs_0_, ...), custom_call_target="tpu_custom_call" | custom-call | bytes 524288 | tf_op jit(solution)/shard_map/pallas_call | solution.py:283
  34.1 1.9 %collective-permute-start.13 = (bf16[64,1024]{1,0:T(8,128)(2,1)S(1)}, bf16[64,1024]{1,0:T(8,128)(2,1)S(1)}, u32[]{:S(2)}, u32[]{:S(2)}) collective-permute-start(bf16[64,1024]{1,0:T(8,128)(2,1)S(1)} %get-tuple-element.30), channel_id=1, source_target_pairs={{0,2},{1,3},{2,0},{3,1},{4,6},{5,7},{6,4},{7,5},{8,10},{9,11},{10,... | collective-permute-start | bytes 393224 | tf_op jit(solution)/shard_map/ppermute | solution.py:65
  36.0 2.5 %collective-permute-start.14 = (bf16[64,1024]{1,0:T(8,128)(2,1)S(1)}, bf16[64,1024]{1,0:T(8,128)(2,1)S(1)}, u32[]{:S(2)}, u32[]{:S(2)}) collective-permute-start(bf16[64,1024]{1,0:T(8,128)(2,1)S(1)} %get-tuple-element.31), channel_id=1, source_target_pairs={{0,4},{1,5},{2,6},{3,7},{4,0},{5,1},{6,2},{7,3},{8,12},{9,13},{10,... | collective-permute-start | bytes 393224 | tf_op jit(solution)/shard_map/ppermute | solution.py:65
  38.5 0.1 collective-permute-start.15
  38.5 0.0 collective-permute-done.7.refs_1_
  38.5 5.4 %shard_map.59 = (f32[256,1024]{1,0:T(8,128)S(1)}, f32[8,256]{1,0:T(8,128)S(1)}, bf16[256,1024]{1,0:T(8,128)(2,1)S(1)}, bf16[256,1024]{1,0:T(8,128)(2,1)S(1)}, bf16[128,1024]{1,0:T(8,128)(2,1)S(1)}) custom-call(bf16[128,4096]{1,0:T(8,128)(2,1)S(1)} %constant_dynamic-update-slice_fusion.refs_0_, bf16[128,4096]{1,0:T(8,128)(2,1)S(1)} %collective-permute-done.7.refs_1_, ...), custom_call_target="tpu_custom_call" | custom-call | flops 2147483648 | bytes 10486272 | tf_op jit(solution)/shard_map/pallas_call | solution.py:193
  44.0 1.7 %collective-permute-start.17 = (bf16[256,1024]{1,0:T(8,128)(2,1)S(1)}, bf16[256,1024]{1,0:T(8,128)(2,1)S(1)}, u32[]{:S(2)}, u32[]{:S(2)}) collective-permute-start(bf16[256,1024]{1,0:T(8,128)(2,1)S(1)} %get-tuple-element.33), channel_id=1, source_target_pairs={{0,8},{1,17},{2,10},{3,19},{4,12},{5,21},{6,14},{7,23},{8,0},{9,25... | collective-permute-start | bytes 1572872 | tf_op jit(solution)/shard_map/ppermute | solution.py:223
  45.7 0.0 collective-permute-start.8
  45.7 1.2 %collective-permute-done.8.b_ref = f32[8,256]{1,0:T(8,128)S(1)} collective-permute-done((f32[8,256]{1,0:T(8,128)S(1)}, f32[8,256]{1,0:T(8,128)S(1)}, u32[]{:S(2)}, u32[]{:S(2)}) %collective-permute-start.8) | collective-permute-done | bytes 8224 | tf_op jit(solution)/shard_map/ppermute | solution.py:65
  46.9 2.0 %collective-permute-done.14.refs_2_.refs_6_ = bf16[64,1024]{1,0:T(8,128)(2,1)S(1)} collective-permute-done((bf16[64,1024]{1,0:T(8,128)(2,1)S(1)}, bf16[64,1024]{1,0:T(8,128)(2,1)S(1)}, u32[]{:S(2)}, u32[]{:S(2)}) %collective-permute-start.14) | collective-permute-done | bytes 131104 | tf_op jit(solution)/shard_map/ppermute | solution.py:65
  48.9 0.0 collective-permute-done.15.refs_3_.refs_7_
  48.9 0.1 collective-permute-start.16
  49.0 2.5 %collective-permute-start.18 = (bf16[128,1024]{1,0:T(8,128)(2,1)S(1)}, bf16[128,1024]{1,0:T(8,128)(2,1)S(1)}, u32[]{:S(2)}, u32[]{:S(2)}) collective-permute-start(bf16[128,1024]{1,0:T(8,128)(2,1)S(1)} %get-tuple-element.34), channel_id=1, source_target_pairs={{0,24},{8,16},{16,8},{24,0},{1,25},{9,17},{17,9},{25,1},{2,26},{10... | collective-permute-start | bytes 786440 | tf_op jit(solution)/shard_map/ppermute | solution.py:65
  51.5 2.3 %collective-permute-start.9 = (f32[8,256]{1,0:T(8,128)S(1)}, f32[8,256]{1,0:T(8,128)S(1)}, u32[]{:S(2)}, u32[]{:S(2)}) collective-permute-start(f32[8,256]{1,0:T(8,128)S(1)} %shard_map.60.refs_4_.refs_0_), channel_id=1, source_target_pairs={{0,2},{1,3},{2,0},{3,1},{4,6},{5,7},{6,4},{7,5},{8,10},{9,11},{10,... | collective-permute-start | bytes 24584 | tf_op jit(solution)/shard_map/ppermute | solution.py:65
  53.8 1.0 %collective-permute-start.10 = (f32[8,256]{1,0:T(8,128)S(1)}, f32[8,256]{1,0:T(8,128)S(1)}, u32[]{:S(2)}, u32[]{:S(2)}) collective-permute-start(f32[8,256]{1,0:T(8,128)S(1)} %shard_map.60.refs_4_.refs_0_), channel_id=1, source_target_pairs={{0,4},{1,5},{2,6},{3,7},{4,0},{5,1},{6,2},{7,3},{8,12},{9,13},{10,... | collective-permute-start | bytes 24584 | tf_op jit(solution)/shard_map/ppermute | solution.py:65
  54.8 1.5 %collective-permute-start.11 = (f32[8,256]{1,0:T(8,128)S(1)}, f32[8,256]{1,0:T(8,128)S(1)}, u32[]{:S(2)}, u32[]{:S(2)}) collective-permute-start(f32[8,256]{1,0:T(8,128)S(1)} %shard_map.60.refs_4_.refs_0_), channel_id=1, source_target_pairs={{0,6},{1,7},{2,4},{3,5},{4,2},{5,3},{6,0},{7,1},{8,14},{9,15},{10,... | collective-permute-start | bytes 24584 | tf_op jit(solution)/shard_map/ppermute | solution.py:65
  56.2 0.0 collective-permute-done.9.refs_1_
  56.2 2.1 %collective-permute-done.10.refs_2_ = f32[8,256]{1,0:T(8,128)S(1)} collective-permute-done((f32[8,256]{1,0:T(8,128)S(1)}, f32[8,256]{1,0:T(8,128)S(1)}, u32[]{:S(2)}, u32[]{:S(2)}) %collective-permute-start.10) | collective-permute-done | bytes 8224 | tf_op jit(solution)/shard_map/ppermute | solution.py:65
  58.3 1.9 %collective-permute-done.11.refs_3_ = f32[8,256]{1,0:T(8,128)S(1)} collective-permute-done((f32[8,256]{1,0:T(8,128)S(1)}, f32[8,256]{1,0:T(8,128)S(1)}, u32[]{:S(2)}, u32[]{:S(2)}) %collective-permute-start.11) | collective-permute-done | bytes 8224 | tf_op jit(solution)/shard_map/ppermute | solution.py:65
  60.2 0.0 collective-permute-done.17.refs_10_
  60.2 4.5 %shard_map.63 = (bf16[256,1024]{1,0:T(8,128)(2,1)S(1)}, f32[128,4096]{1,0:T(8,128)S(1)}, bf16[128,4096]{1,0:T(8,128)(2,1)S(1)}, bf16[384,1024]{1,0:T(8,128)(2,1)S(1)}) custom-call(f32[256,1024]{1,0:T(8,128)S(1)} %get-tuple-element.22.logits_ref, f32[8,256]{1,0:T(8,128)S(1)} %shard_map.60.refs_4_.refs_0_, f32[8,256]{1,0:T(8,128)S(1)} %collective-permute-done.9.refs_1_, ...), custom_call_target="tpu_custom_call" | custom-call | flops 2147483648 | bytes 9715712 | tf_op jit(solution)/shard_map/pallas_call | solution.py:352
  64.7 0.1 collective-permute-start.19
  64.8 2.6 %collective-permute-done.19 = bf16[128,4096]{1,0:T(8,128)(2,1)S(1)} collective-permute-done((bf16[128,4096]{1,0:T(8,128)(2,1)S(1)}, bf16[128,4096]{1,0:T(8,128)(2,1)S(1)}, u32[]{:S(2)}, u32[]{:S(2)}) %collective-permute-start.19) | collective-permute-done | bytes 1048608 | tf_op jit(solution)/shard_map/ppermute | solution.py:65
  67.5 0.3 fusion.8
  67.8 0.7 collective-permute-start.21
  68.6 1.5 %collective-permute-start.23 = (bf16[256,1024]{1,0:T(8,128)(2,1)S(1)}, bf16[256,1024]{1,0:T(8,128)(2,1)S(1)}, u32[]{:S(2)}, u32[]{:S(2)}) collective-permute-start(bf16[256,1024]{1,0:T(8,128)(2,1)S(1)} %get-tuple-element.37.refs_0_), channel_id=1, source_target_pairs={{0,8},{8,0},{16,24},{24,16},{1,9},{9,1},{17,25},{25,17},{2,10},{10... | collective-permute-start | bytes 1572872 | tf_op jit(solution)/shard_map/ppermute | solution.py:65
  70.0 1.5 %collective-permute-start.24 = (bf16[256,1024]{1,0:T(8,128)(2,1)S(1)}, bf16[256,1024]{1,0:T(8,128)(2,1)S(1)}, u32[]{:S(2)}, u32[]{:S(2)}) collective-permute-start(bf16[256,1024]{1,0:T(8,128)(2,1)S(1)} %get-tuple-element.37.refs_0_), channel_id=1, source_target_pairs={{0,16},{8,24},{16,0},{24,8},{1,17},{9,25},{17,1},{25,9},{2,18},{10... | collective-permute-start | bytes 1572872 | tf_op jit(solution)/shard_map/ppermute | solution.py:65
  71.6 0.1 collective-permute-start.20
  71.7 5.4 %collective-permute-done.21 = bf16[32,4096]{1,0:T(8,128)(2,1)S(1)} collective-permute-done((bf16[32,4096]{1,0:T(8,128)(2,1)S(1)}, bf16[32,4096]{1,0:T(8,128)(2,1)S(1)}, u32[]{:S(2)}, u32[]{:S(2)}) %collective-permute-start.21) | collective-permute-done | bytes 262176 | tf_op jit(solution)/shard_map/ppermute | solution.py:65
  77.1 1.9 %collective-permute-start.22 = (bf16[32,4096]{1,0:T(8,128)(2,1)S(1)}, bf16[32,4096]{1,0:T(8,128)(2,1)S(1)}, u32[]{:S(2)}, u32[]{:S(2)}) collective-permute-start(bf16[32,4096]{1,0:T(8,128)(2,1)S(1)} %fusion), channel_id=1, source_target_pairs={{0,4},{1,5},{2,6},{3,7},{4,0},{5,1},{6,2},{7,3},{8,12},{9,13},{10,... | collective-permute-start | bytes 786440 | tf_op jit(solution)/shard_map/ppermute | solution.py:65
  79.0 3.2 %collective-permute-done.23.refs_1_ = bf16[256,1024]{1,0:T(8,128)(2,1)S(1)} collective-permute-done((bf16[256,1024]{1,0:T(8,128)(2,1)S(1)}, bf16[256,1024]{1,0:T(8,128)(2,1)S(1)}, u32[]{:S(2)}, u32[]{:S(2)}) %collective-permute-start.23) | collective-permute-done | bytes 524320 | tf_op jit(solution)/shard_map/ppermute | solution.py:65
  82.3 1.6 %collective-permute-start.26 = (bf16[128,1024]{1,0:T(8,128)(2,1)S(1)}, bf16[128,1024]{1,0:T(8,128)(2,1)S(1)}, u32[]{:S(2)}, u32[]{:S(2)}) collective-permute-start(bf16[128,1024]{1,0:T(8,128)(2,1)S(1)} %slice.50), channel_id=1, source_target_pairs={{0,16},{8,24},{16,0},{24,8},{1,17},{9,25},{17,1},{25,9},{2,18},{10... | collective-permute-start | bytes 786440 | tf_op jit(solution)/shard_map/ppermute | solution.py:65
  83.8 0.0 collective-permute-done.24.refs_2_
  83.9 1.6 %collective-permute-start.27 = (bf16[128,1024]{1,0:T(8,128)(2,1)S(1)}, bf16[128,1024]{1,0:T(8,128)(2,1)S(1)}, u32[]{:S(2)}, u32[]{:S(2)}) collective-permute-start(bf16[128,1024]{1,0:T(8,128)(2,1)S(1)} %slice.51), channel_id=1, source_target_pairs={{0,8},{8,0},{16,24},{24,16},{1,9},{9,1},{17,25},{25,17},{2,10},{10... | collective-permute-start | bytes 786440 | tf_op jit(solution)/shard_map/ppermute | solution.py:65
  85.4 1.9 %shard_map.64.partial_ref = f32[1024,1024]{1,0:T(8,128)S(1)} custom-call(bf16[256,1024]{1,0:T(8,128)(2,1)S(1)} %get-tuple-element.37.refs_0_, bf16[256,1024]{1,0:T(8,128)(2,1)S(1)} %collective-permute-done.23.refs_1_, bf16[256,1024]{1,0:T(8,128)(2,1)S(1)} %collective-permute-done.24.refs_2_, bf16[256,1024]{1,0:T(8,128)(2,1)S(1)} %get-tuple-element.38.refs_3_, ...), custom_call_target="tpu_custom_call" | custom-call | flops 1610612736 | bytes 3670016 | tf_op jit(solution)/shard_map/pallas_call | solution.py:399
  87.3 3.1 %collective-permute-done.22 = bf16[32,4096]{1,0:T(8,128)(2,1)S(1)} collective-permute-done((bf16[32,4096]{1,0:T(8,128)(2,1)S(1)}, bf16[32,4096]{1,0:T(8,128)(2,1)S(1)}, u32[]{:S(2)}, u32[]{:S(2)}) %collective-permute-start.22) | collective-permute-done | bytes 262176 | tf_op jit(solution)/shard_map/ppermute | solution.py:65
  90.4 0.1 fusion.2.refs_4_
  90.5 0.0 copy-start.1
  90.6 0.3 collective-permute-done.27.refs_1_
  90.9 1.7 %shard_map.65 = bf16[1024,1024]{1,0:T(8,128)(2,1)} custom-call(f32[1024,1024]{1,0:T(8,128)S(1)} %shard_map.64.partial_ref, bf16[128,1024]{1,0:T(8,128)(2,1)S(1)} %collective-permute-done.26.refs_0_, bf16[128,1024]{1,0:T(8,128)(2,1)S(1)} %collective-permute-done.27.refs_1_, bf16[384,1024]{1,0:T(8,128)(2,1)S(1)} %get-tuple-element.39.refs_4_.refs_2_, ...), custom_call_target="tpu_custom_call" | custom-call | flops 536870912 | bytes 4194304 | tf_op jit(solution)/shard_map/pallas_call | solution.py:434
  (32 shorter events, 0.4 us)
Async XLA Ops:
  0.6 13.6 %copy-start = (s32[2,64]{1,0:T(2,128)S(1)}, s32[2,64]{1,0:T(2,128)}, u32[]{:S(2)}) copy-start(s32[2,64]{1,0:T(2,128)} %param.7) | copy-start | bytes 1540
  0.6 19.5 %collective-permute-start = (bf16[32,4096]{1,0:T(8,128)(2,1)}, bf16[32,4096]{1,0:T(8,128)(2,1)S(1)}, u32[]{:S(2)}, u32[]{:S(2)}) collective-permute-start(bf16[32,4096]{1,0:T(8,128)(2,1)} %param.4), channel_id=1, source_target_pairs={{0,2},{1,3},{2,0},{3,1},{4,6},{5,7},{6,4},{7,5},{8,10},{9,11},{10,... | collective-permute-start | bytes 786440 | tf_op jit(solution)/shard_map/ppermute | solution.py:65
  3.7 16.1 %collective-permute-start.1 = (bf16[32,4096]{1,0:T(8,128)(2,1)}, bf16[32,4096]{1,0:T(8,128)(2,1)S(1)}, u32[]{:S(2)}, u32[]{:S(2)}) collective-permute-start(bf16[32,4096]{1,0:T(8,128)(2,1)} %param.4), channel_id=1, source_target_pairs={{0,4},{1,5},{2,6},{3,7},{4,0},{5,1},{6,2},{7,3},{8,12},{9,13},{10,... | collective-permute-start | bytes 786440 | tf_op jit(solution)/shard_map/ppermute | solution.py:65
  7.5 14.5 %collective-permute-start.3 = (bf16[64,1024]{1,0:T(8,128)(2,1)S(1)}, bf16[64,1024]{1,0:T(8,128)(2,1)S(1)}, u32[]{:S(2)}, u32[]{:S(2)}) collective-permute-start(bf16[64,1024]{1,0:T(8,128)(2,1)S(1)} %get-tuple-element.46), channel_id=1, source_target_pairs={{0,2},{1,3},{2,0},{3,1},{4,6},{5,7},{6,4},{7,5},{8,10},{9,11},{10,... | collective-permute-start | bytes 393224 | tf_op jit(solution)/shard_map/ppermute | solution.py:65
  8.0 20.1 %collective-permute-start.4 = (bf16[64,1024]{1,0:T(8,128)(2,1)S(1)}, bf16[64,1024]{1,0:T(8,128)(2,1)S(1)}, u32[]{:S(2)}, u32[]{:S(2)}) collective-permute-start(bf16[64,1024]{1,0:T(8,128)(2,1)S(1)} %get-tuple-element.45), channel_id=1, source_target_pairs={{0,4},{1,5},{2,6},{3,7},{4,0},{5,1},{6,2},{7,3},{8,12},{9,13},{10,... | collective-permute-start | bytes 393224 | tf_op jit(solution)/shard_map/ppermute | solution.py:65
  8.0 20.1 %collective-permute-start.5 = (bf16[64,1024]{1,0:T(8,128)(2,1)S(1)}, bf16[64,1024]{1,0:T(8,128)(2,1)S(1)}, u32[]{:S(2)}, u32[]{:S(2)}) collective-permute-start(bf16[64,1024]{1,0:T(8,128)(2,1)S(1)} %get-tuple-element.44), channel_id=1, source_target_pairs={{0,6},{1,7},{2,4},{3,5},{4,2},{5,3},{6,0},{7,1},{8,14},{9,15},{10,... | collective-permute-start | bytes 393224 | tf_op jit(solution)/shard_map/ppermute | solution.py:65
  19.8 8.7 %collective-permute-start.2 = (bf16[16,4096]{1,0:T(8,128)(2,1)S(1)}, bf16[16,4096]{1,0:T(8,128)(2,1)S(1)}, u32[]{:S(2)}, u32[]{:S(2)}) collective-permute-start(bf16[16,4096]{1,0:T(8,128)(2,1)S(1)} %get-tuple-element.49), channel_id=1, source_target_pairs={{0,2},{1,3},{2,0},{3,1},{4,6},{5,7},{6,4},{7,5},{8,10},{9,11},{10,... | collective-permute-start | bytes 393224 | tf_op jit(solution)/shard_map/ppermute | solution.py:65
  20.1 9.8 %collective-permute-start.6 = (bf16[16,4096]{1,0:T(8,128)(2,1)S(1)}, bf16[16,4096]{1,0:T(8,128)(2,1)S(1)}, u32[]{:S(2)}, u32[]{:S(2)}) collective-permute-start(bf16[16,4096]{1,0:T(8,128)(2,1)S(1)} %get-tuple-element.48), channel_id=1, source_target_pairs={{0,2},{1,3},{2,0},{3,1},{4,6},{5,7},{6,4},{7,5},{8,10},{9,11},{10,... | collective-permute-start | bytes 393224 | tf_op jit(solution)/shard_map/ppermute | solution.py:65
  29.9 8.6 %collective-permute-start.7 = (bf16[128,4096]{1,0:T(8,128)(2,1)S(1)}, bf16[128,4096]{1,0:T(8,128)(2,1)S(1)}, u32[]{:S(2)}, u32[]{:S(2)}) collective-permute-start(bf16[128,4096]{1,0:T(8,128)(2,1)S(1)} %constant_dynamic-update-slice_fusion.refs_0_), channel_id=1, source_target_pairs={{0,1},{1,0},{2,3},{3,2},{4,5},{5,4},{6,7},{7,6},{8,9},{9,8},{10,11... | collective-permute-start | bytes 3145736 | tf_op jit(solution)/shard_map/ppermute | solution.py:65
  30.1 2.9 %collective-permute-start.12 = (bf16[4,32,1024]{2,1,0:T(8,128)(2,1)S(1)}, bf16[4,32,1024]{2,1,0:T(8,128)(2,1)S(1)}, u32[]{:S(2)}, u32[]{:S(2)}) collective-permute-start(bf16[4,32,1024]{2,1,0:T(8,128)(2,1)S(1)} %pad_maximum_fusion), channel_id=1, source_target_pairs={{0,1},{1,0},{2,3},{3,2},{4,5},{5,4},{6,7},{7,6},{8,9},{9,8},{10,11... | collective-permute-start | bytes 786440 | tf_op jit(solution)/shard_map/ppermute | solution.py:65
  34.1 12.8 %collective-permute-start.13 = (bf16[64,1024]{1,0:T(8,128)(2,1)S(1)}, bf16[64,1024]{1,0:T(8,128)(2,1)S(1)}, u32[]{:S(2)}, u32[]{:S(2)}) collective-permute-start(bf16[64,1024]{1,0:T(8,128)(2,1)S(1)} %get-tuple-element.30), channel_id=1, source_target_pairs={{0,2},{1,3},{2,0},{3,1},{4,6},{5,7},{6,4},{7,5},{8,10},{9,11},{10,... | collective-permute-start | bytes 393224 | tf_op jit(solution)/shard_map/ppermute | solution.py:65
  36.0 12.9 %collective-permute-start.14 = (bf16[64,1024]{1,0:T(8,128)(2,1)S(1)}, bf16[64,1024]{1,0:T(8,128)(2,1)S(1)}, u32[]{:S(2)}, u32[]{:S(2)}) collective-permute-start(bf16[64,1024]{1,0:T(8,128)(2,1)S(1)} %get-tuple-element.31), channel_id=1, source_target_pairs={{0,4},{1,5},{2,6},{3,7},{4,0},{5,1},{6,2},{7,3},{8,12},{9,13},{10,... | collective-permute-start | bytes 393224 | tf_op jit(solution)/shard_map/ppermute | solution.py:65
  38.5 10.4 %collective-permute-start.15 = (bf16[64,1024]{1,0:T(8,128)(2,1)S(1)}, bf16[64,1024]{1,0:T(8,128)(2,1)S(1)}, u32[]{:S(2)}, u32[]{:S(2)}) collective-permute-start(bf16[64,1024]{1,0:T(8,128)(2,1)S(1)} %get-tuple-element.32), channel_id=1, source_target_pairs={{0,6},{1,7},{2,4},{3,5},{4,2},{5,3},{6,0},{7,1},{8,14},{9,15},{10,... | collective-permute-start | bytes 393224 | tf_op jit(solution)/shard_map/ppermute | solution.py:65
  44.0 16.3 %collective-permute-start.17 = (bf16[256,1024]{1,0:T(8,128)(2,1)S(1)}, bf16[256,1024]{1,0:T(8,128)(2,1)S(1)}, u32[]{:S(2)}, u32[]{:S(2)}) collective-permute-start(bf16[256,1024]{1,0:T(8,128)(2,1)S(1)} %get-tuple-element.33), channel_id=1, source_target_pairs={{0,8},{1,17},{2,10},{3,19},{4,12},{5,21},{6,14},{7,23},{8,0},{9,25... | collective-permute-start | bytes 1572872 | tf_op jit(solution)/shard_map/ppermute | solution.py:223
  45.7 1.2 %collective-permute-start.8 = (f32[8,256]{1,0:T(8,128)S(1)}, f32[8,256]{1,0:T(8,128)S(1)}, u32[]{:S(2)}, u32[]{:S(2)}) collective-permute-start(f32[8,256]{1,0:T(8,128)S(1)} %get-tuple-element.23.a_ref), channel_id=1, source_target_pairs={{0,1},{1,0},{2,3},{3,2},{4,5},{5,4},{6,7},{7,6},{8,9},{9,8},{10,11... | collective-permute-start | bytes 24584 | tf_op jit(solution)/shard_map/ppermute | solution.py:65
  48.9 5.9 %collective-permute-start.16 = (bf16[4,32,1024]{2,1,0:T(8,128)(2,1)S(1)}, bf16[4,32,1024]{2,1,0:T(8,128)(2,1)S(1)}, u32[]{:S(2)}, u32[]{:S(2)}) collective-permute-start(bf16[4,32,1024]{2,1,0:T(8,128)(2,1)S(1)} %shard_map.62), channel_id=1, source_target_pairs={{0,1},{1,0},{2,3},{3,2},{4,5},{5,4},{6,7},{7,6},{8,9},{9,8},{10,11... | collective-permute-start | bytes 786440 | tf_op jit(solution)/shard_map/ppermute | solution.py:65
  49.0 11.3 %collective-permute-start.18 = (bf16[128,1024]{1,0:T(8,128)(2,1)S(1)}, bf16[128,1024]{1,0:T(8,128)(2,1)S(1)}, u32[]{:S(2)}, u32[]{:S(2)}) collective-permute-start(bf16[128,1024]{1,0:T(8,128)(2,1)S(1)} %get-tuple-element.34), channel_id=1, source_target_pairs={{0,24},{8,16},{16,8},{24,0},{1,25},{9,17},{17,9},{25,1},{2,26},{10... | collective-permute-start | bytes 786440 | tf_op jit(solution)/shard_map/ppermute | solution.py:65
  51.5 4.8 %collective-permute-start.9 = (f32[8,256]{1,0:T(8,128)S(1)}, f32[8,256]{1,0:T(8,128)S(1)}, u32[]{:S(2)}, u32[]{:S(2)}) collective-permute-start(f32[8,256]{1,0:T(8,128)S(1)} %shard_map.60.refs_4_.refs_0_), channel_id=1, source_target_pairs={{0,2},{1,3},{2,0},{3,1},{4,6},{5,7},{6,4},{7,5},{8,10},{9,11},{10,... | collective-permute-start | bytes 24584 | tf_op jit(solution)/shard_map/ppermute | solution.py:65
  53.8 4.5 %collective-permute-start.10 = (f32[8,256]{1,0:T(8,128)S(1)}, f32[8,256]{1,0:T(8,128)S(1)}, u32[]{:S(2)}, u32[]{:S(2)}) collective-permute-start(f32[8,256]{1,0:T(8,128)S(1)} %shard_map.60.refs_4_.refs_0_), channel_id=1, source_target_pairs={{0,4},{1,5},{2,6},{3,7},{4,0},{5,1},{6,2},{7,3},{8,12},{9,13},{10,... | collective-permute-start | bytes 24584 | tf_op jit(solution)/shard_map/ppermute | solution.py:65
  54.8 5.4 %collective-permute-start.11 = (f32[8,256]{1,0:T(8,128)S(1)}, f32[8,256]{1,0:T(8,128)S(1)}, u32[]{:S(2)}, u32[]{:S(2)}) collective-permute-start(f32[8,256]{1,0:T(8,128)S(1)} %shard_map.60.refs_4_.refs_0_), channel_id=1, source_target_pairs={{0,6},{1,7},{2,4},{3,5},{4,2},{5,3},{6,0},{7,1},{8,14},{9,15},{10,... | collective-permute-start | bytes 24584 | tf_op jit(solution)/shard_map/ppermute | solution.py:65
  64.7 2.7 %collective-permute-start.19 = (bf16[128,4096]{1,0:T(8,128)(2,1)S(1)}, bf16[128,4096]{1,0:T(8,128)(2,1)S(1)}, u32[]{:S(2)}, u32[]{:S(2)}) collective-permute-start(bf16[128,4096]{1,0:T(8,128)(2,1)S(1)} %get-tuple-element.36), channel_id=1, source_target_pairs={{0,1},{1,0},{2,3},{3,2},{4,5},{5,4},{6,7},{7,6},{8,9},{9,8},{10,11... | collective-permute-start | bytes 3145736 | tf_op jit(solution)/shard_map/ppermute | solution.py:65
  67.8 9.2 %collective-permute-start.21 = (bf16[32,4096]{1,0:T(8,128)(2,1)S(1)}, bf16[32,4096]{1,0:T(8,128)(2,1)S(1)}, u32[]{:S(2)}, u32[]{:S(2)}) collective-permute-start(bf16[32,4096]{1,0:T(8,128)(2,1)S(1)} %get-tuple-element.43), channel_id=1, source_target_pairs={{0,2},{1,3},{2,0},{3,1},{4,6},{5,7},{6,4},{7,5},{8,10},{9,11},{10,... | collective-permute-start | bytes 786440 | tf_op jit(solution)/shard_map/ppermute | solution.py:65
  68.6 13.7 %collective-permute-start.23 = (bf16[256,1024]{1,0:T(8,128)(2,1)S(1)}, bf16[256,1024]{1,0:T(8,128)(2,1)S(1)}, u32[]{:S(2)}, u32[]{:S(2)}) collective-permute-start(bf16[256,1024]{1,0:T(8,128)(2,1)S(1)} %get-tuple-element.37.refs_0_), channel_id=1, source_target_pairs={{0,8},{8,0},{16,24},{24,16},{1,9},{9,1},{17,25},{25,17},{2,10},{10... | collective-permute-start | bytes 1572872 | tf_op jit(solution)/shard_map/ppermute | solution.py:65
  70.0 13.8 %collective-permute-start.24 = (bf16[256,1024]{1,0:T(8,128)(2,1)S(1)}, bf16[256,1024]{1,0:T(8,128)(2,1)S(1)}, u32[]{:S(2)}, u32[]{:S(2)}) collective-permute-start(bf16[256,1024]{1,0:T(8,128)(2,1)S(1)} %get-tuple-element.37.refs_0_), channel_id=1, source_target_pairs={{0,16},{8,24},{16,0},{24,8},{1,17},{9,25},{17,1},{25,9},{2,18},{10... | collective-permute-start | bytes 1572872 | tf_op jit(solution)/shard_map/ppermute | solution.py:65
  71.6 13.9 %collective-permute-start.25 = (bf16[384,1024]{1,0:T(8,128)(2,1)S(1)}, bf16[384,1024]{1,0:T(8,128)(2,1)S(1)}, u32[]{:S(2)}, u32[]{:S(2)}) collective-permute-start(bf16[384,1024]{1,0:T(8,128)(2,1)S(1)} %get-tuple-element.39.refs_4_.refs_2_), channel_id=1, source_target_pairs={{0,1},{1,0},{2,3},{3,2},{4,5},{5,4},{6,7},{7,6},{8,9},{9,8},{10,11... | collective-permute-start | bytes 2359304 | tf_op jit(solution)/shard_map/ppermute | solution.py:65
  71.6 15.7 %collective-permute-start.20 = (bf16[32,4096]{1,0:T(8,128)(2,1)S(1)}, bf16[32,4096]{1,0:T(8,128)(2,1)S(1)}, u32[]{:S(2)}, u32[]{:S(2)}) collective-permute-start(bf16[32,4096]{1,0:T(8,128)(2,1)S(1)} %get-tuple-element.42), channel_id=1, source_target_pairs={{0,2},{1,3},{2,0},{3,1},{4,6},{5,7},{6,4},{7,5},{8,10},{9,11},{10,... | collective-permute-start | bytes 786440 | tf_op jit(solution)/shard_map/ppermute | solution.py:65
  77.1 13.3 %collective-permute-start.22 = (bf16[32,4096]{1,0:T(8,128)(2,1)S(1)}, bf16[32,4096]{1,0:T(8,128)(2,1)S(1)}, u32[]{:S(2)}, u32[]{:S(2)}) collective-permute-start(bf16[32,4096]{1,0:T(8,128)(2,1)S(1)} %fusion), channel_id=1, source_target_pairs={{0,4},{1,5},{2,6},{3,7},{4,0},{5,1},{6,2},{7,3},{8,12},{9,13},{10,... | collective-permute-start | bytes 786440 | tf_op jit(solution)/shard_map/ppermute | solution.py:65
  82.3 8.3 %collective-permute-start.26 = (bf16[128,1024]{1,0:T(8,128)(2,1)S(1)}, bf16[128,1024]{1,0:T(8,128)(2,1)S(1)}, u32[]{:S(2)}, u32[]{:S(2)}) collective-permute-start(bf16[128,1024]{1,0:T(8,128)(2,1)S(1)} %slice.50), channel_id=1, source_target_pairs={{0,16},{8,24},{16,0},{24,8},{1,17},{9,25},{17,1},{25,9},{2,18},{10... | collective-permute-start | bytes 786440 | tf_op jit(solution)/shard_map/ppermute | solution.py:65
  83.9 7.0 %collective-permute-start.27 = (bf16[128,1024]{1,0:T(8,128)(2,1)S(1)}, bf16[128,1024]{1,0:T(8,128)(2,1)S(1)}, u32[]{:S(2)}, u32[]{:S(2)}) collective-permute-start(bf16[128,1024]{1,0:T(8,128)(2,1)S(1)} %slice.51), channel_id=1, source_target_pairs={{0,8},{8,0},{16,24},{24,16},{1,9},{9,1},{17,25},{25,17},{2,10},{10... | collective-permute-start | bytes 786440 | tf_op jit(solution)/shard_map/ppermute | solution.py:65
  90.5 2.0 %copy-start.1 = (bf16[32,4096]{1,0:T(8,128)(2,1)}, bf16[32,4096]{1,0:T(8,128)(2,1)S(1)}, u32[]{:S(2)}) copy-start(bf16[32,4096]{1,0:T(8,128)(2,1)S(1)} %fusion.2.refs_4_) | copy-start | bytes 786436
